TPU v7x, 32 devices: a whole 2x2x4 slice. The times are simulated.
32 devices in a mesh: dp: 16 (over z, x, core), ctx: 2 (over y).
Axes of the slice: x: 2, y: 2, z: 4, core: 2. Of those that a mesh axis runs over, the one named last changes fastest.
Arguments:
- clip_in: bfloat16 [16, 8, 4, 96, 128], P('dp', 'ctx'), may hold values from -100 to 100
- norm_gain: float32 [128], replicated, may hold values from 0.1 to 1.9
- norm_bias: float32 [128], replicated, may hold values from -3 to 3
- conv_weight: bfloat16 [3456, 256], replicated, may hold values from -0.109375 to 0.109375
- short_weight: bfloat16 [128, 256], replicated, may hold values from -0.5 to 0.5
- out_cotangent: bfloat16 [16, 8, 4, 96, 256], P('dp', 'ctx'), may hold values from -6 to 6
Outputs:
- clip_out: bfloat16 [16, 8, 4, 96, 256], P('dp', 'ctx')
- clip_grad: bfloat16 [16, 8, 4, 96, 128], P('dp', 'ctx')
- conv_grad: float32 [3456, 256], P('dp', 'ctx')
- short_grad: float32 [128, 256], P('dp', 'ctx')
All inputs are finite; a program needn't handle non-finite values.
Results may differ from a plain program's by a relative error of at most 0.0027.
Values may be sent and summed in bfloat16 or wider, within the bound.
No kernel may reach another device: no remote copies, remote signals or barrier semaphores. Data moves between devices by JAX's collectives and lax.ppermute only.
A program may use at most 128 MiB of HBM per device.

v0:
```python
import jax
import jax.numpy as jnp
from jax import lax
from jax.sharding import PartitionSpec as P

GROUPS = 32
KT = 3
KS = 3


epsilon = 1e-06


def from_behind(value, axis, steps):
    count = lax.axis_size(axis)
    initial, last = (max(0, -steps), min(count, count - steps))
    return lax.ppermute(value, axis, [(source, source + steps) for source in range(initial, last)])


def group_stats(clip_in, members):
    batch_clips = clip_in.shape[0]
    in_width = clip_in.shape[4]
    per_group = in_width // GROUPS
    widened = clip_in.astype(jnp.float32).reshape(clip_in.shape[:4] + (GROUPS, per_group))
    totals = lax.psum(
        (jnp.sum(widened, axis=(1, 2, 3, 5)), jnp.sum(widened * widened, axis=(1, 2, 3, 5))), "ctx"
    )
    group_mean = totals[0] / members
    variance = totals[1] / members - group_mean * group_mean
    inv_std = lax.rsqrt(variance + epsilon)
    mean_chan = jnp.repeat(group_mean, per_group, axis=1).reshape(batch_clips, 1, 1, 1, in_width)
    inv_chan = jnp.repeat(inv_std, per_group, axis=1).reshape(batch_clips, 1, 1, 1, in_width)
    return (mean_chan, inv_chan)


def body(clip_in, norm_gain, norm_bias, conv_weight, short_weight, out_cotangent):
    batch_clips, frames, height, breadth, in_width = clip_in.shape
    out_width = conv_weight.shape[1]
    per_group = in_width // GROUPS
    ctx_size = lax.axis_size("ctx")
    total_frames = frames * ctx_size
    members = total_frames * height * breadth * per_group
    at_start = lax.axis_index("ctx") == 0
    mean_chan, inv_chan = group_stats(clip_in, members)
    standard = (clip_in.astype(jnp.float32) - mean_chan) * inv_chan
    standard, affine = (standard, standard * norm_gain + norm_bias)
    hidden = jax.nn.silu(affine).astype(jnp.bfloat16)
    prev_hidden = from_behind(hidden[:, frames - 2 :], "ctx", 1)
    repeated = jnp.concatenate([hidden[:, :1], hidden[:, :1]], axis=1)
    front = jnp.where(at_start, repeated, prev_hidden)
    padded = jnp.concatenate([front, hidden], axis=1)
    padded = jnp.pad(padded, ((0, 0), (0, 0), (1, 1), (1, 1), (0, 0)))
    pieces = []
    for tap_t in range(KT):
        for tap_r in range(KS):
            for tap_c in range(KS):
                pieces.append(
                    padded[
                        :, tap_t : tap_t + frames, tap_r : tap_r + height, tap_c : tap_c + breadth
                    ]
                )
    columns = jnp.concatenate(pieces, axis=-1).reshape(-1, KT * KS * KS * in_width)
    in_flat = clip_in.reshape(-1, in_width)
    result = jnp.dot(columns, conv_weight, preferred_element_type=jnp.float32)
    result = result + jnp.dot(in_flat, short_weight, preferred_element_type=jnp.float32)
    clip_out = result.astype(jnp.bfloat16).reshape(batch_clips, frames, height, breadth, out_width)
    following = from_behind(out_cotangent[:, :2], "ctx", -1)
    extended = jnp.concatenate([out_cotangent, following], axis=1)
    padded_cot = jnp.pad(extended, ((0, 0), (0, 0), (1, 1), (1, 1), (0, 0)))
    spatial = []
    for tap_r in range(KS):
        for tap_c in range(KS):
            spatial.append(
                padded_cot[:, :, 2 - tap_r : 2 - tap_r + height, 2 - tap_c : 2 - tap_c + breadth]
            )
    spatial = jnp.concatenate(spatial, axis=-1)
    w_back = (
        conv_weight.reshape(KT, KS * KS, in_width, out_width)
        .transpose(0, 1, 3, 2)
        .reshape(KT, KS * KS * out_width, in_width)
    )
    grad_hidden = jnp.zeros((batch_clips * frames * height * breadth, in_width), jnp.float32)
    for tap_t in range(KT):
        block = spatial[:, 2 - tap_t : 2 - tap_t + frames].reshape(-1, KS * KS * out_width)
        grad_hidden = grad_hidden + jnp.dot(
            block, w_back[tap_t], preferred_element_type=jnp.float32
        )
    grad_hidden = grad_hidden.reshape(batch_clips, frames, height, breadth, in_width)

    def pad_terms():
        lead = spatial[:, 0].reshape(-1, KS * KS * out_width)
        second = spatial[:, 1].reshape(-1, KS * KS * out_width)
        terms = jnp.dot(lead, w_back[0], preferred_element_type=jnp.float32)
        terms = terms + jnp.dot(second, w_back[0], preferred_element_type=jnp.float32)
        terms = terms + jnp.dot(lead, w_back[1], preferred_element_type=jnp.float32)
        return terms.reshape(batch_clips, height, breadth, in_width)

    def no_terms():
        return jnp.zeros((batch_clips, height, breadth, in_width), jnp.float32)

    extra_terms = lax.cond(at_start, pad_terms, no_terms)
    grad_hidden = grad_hidden.at[:, 0].add(extra_terms)
    logistic = jax.nn.sigmoid(affine)
    grad_standard = grad_hidden * logistic * (1.0 + affine * (1.0 - logistic)) * norm_gain
    grouped_grad = grad_standard.reshape(grad_standard.shape[:4] + (GROUPS, per_group))
    grouped_std = standard.reshape(standard.shape[:4] + (GROUPS, per_group))
    grad_sums = lax.psum(
        (
            jnp.sum(grouped_grad, axis=(1, 2, 3, 5)),
            jnp.sum(grouped_grad * grouped_std, axis=(1, 2, 3, 5)),
        ),
        "ctx",
    )
    mean_grad = jnp.repeat(grad_sums[0] / members, per_group, axis=1).reshape(
        batch_clips, 1, 1, 1, in_width
    )
    mean_cross = jnp.repeat(grad_sums[1] / members, per_group, axis=1).reshape(
        batch_clips, 1, 1, 1, in_width
    )
    cot_flat = out_cotangent.reshape(-1, out_width)
    shortcut = lax.dot_general(
        cot_flat, short_weight, (((1,), (1,)), ((), ())), preferred_element_type=jnp.float32
    )
    in_grad = (grad_standard - mean_grad - standard * mean_cross) * inv_chan + shortcut.reshape(
        batch_clips, frames, height, breadth, in_width
    )
    clip_grad = in_grad.astype(jnp.bfloat16)
    conv_part = lax.dot_general(
        columns, cot_flat, (((0,), (0,)), ((), ())), preferred_element_type=jnp.float32
    )
    short_part = lax.dot_general(
        in_flat, cot_flat, (((0,), (0,)), ((), ())), preferred_element_type=jnp.float32
    )
    conv_part, short_part = (
        lax.psum_scatter(conv_part, "dp", scatter_dimension=0, tiled=True),
        lax.psum_scatter(short_part, "dp", scatter_dimension=0, tiled=True),
    )
    conv_part, short_part = (
        lax.psum_scatter(conv_part, "ctx", scatter_dimension=1, tiled=True),
        lax.psum_scatter(short_part, "ctx", scatter_dimension=1, tiled=True),
    )
    scale_factor = 1.0 / (batch_clips * lax.axis_size("dp") * total_frames)
    return (clip_out, clip_grad, conv_part * scale_factor, short_part * scale_factor)


def solution(mesh):
    return jax.shard_map(
        body,
        mesh=mesh,
        in_specs=(
            P("dp", "ctx", None, None, None),
            P(),
            P(),
            P(),
            P(),
            P("dp", "ctx", None, None, None),
        ),
        out_specs=(
            P("dp", "ctx", None, None, None),
            P("dp", "ctx", None, None, None),
            P("dp", "ctx"),
            P("dp", "ctx"),
        ),
        check_vma=False,
    )
```

profile of v0, /device:TPU:0, one launch (start us, length us, event | category | flops | bytes accessed | tf_op | source)
XLA Modules:
  0.0 192.6 jit_solution(4293383858363217466)
XLA Ops:
  7.2 2.2 %convolution_bitcast_fusion.1 = f32[128,256]{1,0:T(8,128)} fusion(bf16[1,4,4,96,256]{4,3,2,1,0:T(8,128)(2,1)} %param.15, bf16[1,4,4,96,128]{4,3,2,1,0:T(8,128)(2,1)} %param.10), kind=kOutput, calls=%fused_computation.59 | convolution fusion | flops 100663296 | bytes 1310720 | tf_op jit(solution)/shard_map/dot_general | solution.py:131
  9.5 1.1 slice.213
  10.6 1.3 collective-permute-start.1
  11.9 1.2 convert_reduce_fusion
  13.3 0.1 reduce_sum.55
  13.4 0.1 reduce_sum.62
  13.6 10.5 %all-reduce.3 = (f32[1,32]{1,0:T(1,128)S(1)}, f32[1,32]{1,0:T(1,128)S(1)}) all-reduce(f32[1,32]{1,0:T(1,128)S(1)} %bitcast.102, f32[1,32]{1,0:T(1,128)S(1)} %bitcast.100), channel_id=1, replica_groups=mesh['dp'=16,'ctx'=2] {'ctx'}, use_global_device_ids=true, to_apply=%region_5.6 | all-reduce | flops 64 | bytes 512 | tf_op jit(solution)/shard_map/psum | solution.py:25
  24.4 1.6 fusion.74
  26.0 1.1 copy.13
  27.0 1.1 copy.12
  28.1 1.1 copy.11
  29.2 1.8 fusion.12
  30.9 1.5 slice_dynamic-update-slice_fusion.7
  32.5 1.6 slice_dynamic-update-slice_fusion.6
  34.1 1.2 slice_dynamic-update-slice_fusion.5
  35.3 1.6 slice_dynamic-update-slice_fusion.4
  36.9 1.0 constant_dynamic-update-slice_fusion.2
  37.9 0.8 constant_dynamic-update-slice_fusion.1
  38.8 1.2 slice_dynamic-update-slice_fusion.3
  40.0 1.7 slice_dynamic-update-slice_fusion.2
  41.6 1.6 slice_dynamic-update-slice_fusion.1
  43.2 1.3 slice_dynamic-update-slice_fusion
  44.5 14.0 %fusion.73 = (bf16[1,4,4,96,2304]{4,3,2,1,0:T(8,128)(2,1)}, bf16[1,4,4,96,2304]{4,3,2,1,0:T(8,128)(2,1)}, bf16[1,4,4,96,2304]{4,3,2,1,0:T(8,128)(2,1)S(1)}) fusion(bf16[1,6,4,96,2304]{4,3,2,1,0:T(8,128)(2,1)} %slice_dynamic-update-slice_fusion), kind=kLoop, calls=%fused_computation.132 | loop fusion | bytes 42467328 | tf_op jit(solution)/shard_map/slice | solution.py:84
  58.6 2.9 %fusion.77 = f32[1536,128]{1,0:T(8,128)} fusion(bf16[1536,2304]{1,0:T(8,128)(2,1)S(1)} %bitcast.88, bf16[2304,128]{1,0:T(8,128)(2,1)S(1)} %bitcast.97), kind=kOutput, calls=%fused_computation.136 | convolution fusion | flops 905969664 | bytes 8454144 | tf_op jit(solution)/shard_map/dot_general | solution.py:85
  61.5 8.0 %conditional.1 = (f32[1,1,4,96,128]{4,3,2,1,0:T(8,128)S(1)}) conditional(s32[]{:T(128)} %convert_element_type.23, () %tuple.20, (bf16[1,6,4,96,2304]{4,3,2,1,0:T(8,128)(2,1)}, bf16[3,9,256,128]{2,3,1,0:T(8,128)(2,1)S(1)}) %tuple.47), branch_computations={%region_6.7_spmd, %region_7.8_spmd} | conditional | flops 679575552 | bytes 21037064 | solution.py:101
  61.5 2.3 %copy.14 = bf16[3,9,256,128]{3,2,1,0:T(8,128)(2,1)} copy(bf16[3,9,256,128]{2,3,1,0:T(8,128)(2,1)S(1)} %get-tuple-element.30) | data formatting | bytes 3538944 | tf_op jit(solution)/shard_map
  63.8 1.3 fusion.72
  65.2 2.3 %fusion.71 = (bf16[1,1,4,96,2304]{4,3,2,1,0:T(8,128)(2,1)S(1)}, bf16[1,1,4,96,2304]{4,3,2,1,0:T(8,128)(2,1)S(1)}) fusion(bf16[1,6,4,96,2304]{4,3,2,1,0:T(8,128)(2,1)} %get-tuple-element.21), kind=kLoop, calls=%fused_computation.130 | loop fusion | bytes 7077888 | tf_op jit(solution)/shard_map/cond/branch_1_fun/slice | solution.py:92
  67.4 0.6 fusion.75
  68.0 0.6 convolution_add_fusion.1
  68.7 0.6 convolution_add_fusion
  69.5 5.4 %convolution_add_fusion.4 = f32[1536,128]{1,0:T(8,128)S(1)} fusion(f32[1536,128]{1,0:T(8,128)} %fusion.77, bf16[1536,2304]{1,0:T(8,128)(2,1)} %bitcast.81, bf16[2304,128]{1,0:T(8,128)(2,1)} %bitcast.93), kind=kOutput, calls=%fused_computation.39 | convolution fusion | flops 906166272 | bytes 9240576 | tf_op jit(solution)/shard_map/dot_general | solution.py:85
  75.0 5.2 %convolution_add_fusion.3 = f32[1536,128]{1,0:T(8,128)S(1)} fusion(f32[1536,128]{1,0:T(8,128)S(1)} %convolution_add_fusion.4, bf16[1536,2304]{1,0:T(8,128)(2,1)} %bitcast.80, bf16[2304,128]{1,0:T(8,128)(2,1)} %bitcast.92), kind=kOutput, calls=%fused_computation.38 | convolution fusion | flops 906166272 | bytes 9240576 | tf_op jit(solution)/shard_map/dot_general | solution.py:85
  80.3 1.4 fusion.69
  81.7 0.7 slice.232
  82.4 2.0 %collective-permute-start = (bf16[1,2,4,96,128]{4,3,2,1,0:T(8,128)(2,1)}, bf16[1,2,4,96,128]{4,3,2,1,0:T(8,128)(2,1)}, u32[]{:S(2)}, u32[]{:S(2)}) collective-permute-start(bf16[1,2,4,96,128]{4,3,2,1,0:T(8,128)(2,1)} %slice.232), channel_id=1, source_target_pairs={{0,1},{2,3},{4,5},{6,7},{8,9},{10,11},{12,13},{14,15},{16,17},{18,... | collective-permute-start | bytes 589832 | tf_op jit(solution)/shard_map/ppermute | solution.py:17
  84.4 3.5 %collective-permute-done = bf16[1,2,4,96,128]{4,3,2,1,0:T(8,128)(2,1)} collective-permute-done((bf16[1,2,4,96,128]{4,3,2,1,0:T(8,128)(2,1)}, bf16[1,2,4,96,128]{4,3,2,1,0:T(8,128)(2,1)}, u32[]{:S(2)}, u32[]{:S(2)}) %collective-permute-start) | collective-permute-done | bytes 196640 | tf_op jit(solution)/shard_map/ppermute | solution.py:17
  88.2 0.1 fusion.44
  88.3 0.2 fusion.45
  88.6 0.2 fusion.46
  88.8 0.1 fusion.47
  89.0 0.1 fusion.49
  89.2 0.1 fusion.50
  89.4 0.1 fusion.52
  89.5 0.2 fusion.53
  89.8 0.2 fusion.54
  90.0 0.1 fusion.55
  90.2 0.1 fusion.57
  90.4 0.1 fusion.58
  90.6 0.1 fusion.60
  90.7 0.2 fusion.61
  91.0 0.2 fusion.62
  91.2 0.1 fusion.63
  91.4 0.1 fusion.65
  91.6 4.0 %copy-done.5 = bf16[1,4,4,96,3456]{4,3,2,1,0:T(8,128)(2,1)} copy-done((bf16[1,4,4,96,3456]{4,3,2,1,0:T(8,128)(2,1)}, bf16[1,4,4,96,3456]{4,3,2,1,0:T(8,128)(2,1)S(1)}, u32[]{:S(2)}) %copy-start.5) | copy-done | bytes 10616856
  95.6 4.8 %fusion.2 = f32[3456,256]{1,0:T(8,128)} fusion(bf16[1,4,4,96,3456]{4,3,2,1,0:T(8,128)(2,1)S(1)} %fusion.65, bf16[1,4,4,96,256]{4,3,2,1,0:T(8,128)(2,1)S(1)} %copy-done.1), kind=kOutput, calls=%fused_computation.8 | convolution fusion | flops 2717908992 | bytes 14942208 | tf_op jit(solution)/shard_map/dot_general | solution.py:128
  100.5 1.3 broadcast_multiply_fusion.1
  102.2 6.3 %all-reduce.2 = (f32[1,32]{1,0:T(1,128)S(1)}, f32[1,32]{1,0:T(1,128)S(1)}) all-reduce(f32[1,32]{1,0:T(1,128)S(1)} %bitcast.101, f32[1,32]{1,0:T(1,128)S(1)} %bitcast.99), channel_id=1, replica_groups=mesh['dp'=16,'ctx'=2] {'ctx'}, use_global_device_ids=true, to_apply=%region_13.14 | all-reduce | flops 64 | bytes 512 | tf_op jit(solution)/shard_map/psum | solution.py:107
  108.9 2.3 %fusion.15 = bf16[1,4,4,96,128]{4,3,2,1,0:T(8,128)(2,1)} fusion(bf16[1,4,4,96,128]{4,3,2,1,0:T(8,128)(2,1)S(1)} %copy-done.2, bf16[1,4,4,96,256]{4,3,2,1,0:T(8,128)(2,1)S(1)} %copy-done.1, f32[1,4,4,96,128]{4,3,2,1,0:T(8,128)} %get-tuple-element.39, f32[128]{0:T(128)S(1)} %broadcast_in_dim.30, f32[128]{0:T(128)S(1)} %broadcast_in_dim.28, ...), kind=kOutput, calls=%fused_computation.47 | convolution fusion | flops 102432768 | bytes 2426880 | tf_op jit(solution)/shard_map/dot_general | solution.py:121
  111.2 61.0 %reduce-scatter.5.cloned.1.call-done = f32[216,256]{1,0:T(8,128)} async-done(((f32[3456,256]{1,0:T(8,128)}), f32[216,256]{1,0:T(8,128)}) %reduce-scatter.5.cloned.1.call-update) | async-done | bytes 221200 | tf_op jit(solution)/shard_map/reduce_scatter | solution.py:135
  172.3 5.7 %fusion.76 = f32[1536,256]{1,0:T(8,128)S(1)} fusion(bf16[1536,3456]{1,0:T(8,128)(2,1)} %bitcast.98, bf16[3456,256]{1,0:T(8,128)(2,1)S(1)} %copy-done.3), kind=kOutput, calls=%fused_computation.135 | convolution fusion | flops 2717908992 | bytes 13959168 | tf_op jit(solution)/shard_map/dot_general | solution.py:64
  178.0 1.2 fusion.8
  179.2 5.3 %reduce-scatter.7.cloned.1.call-done = f32[216,128]{1,0:T(8,128)} async-done(((f32[216,256]{1,0:T(8,128)}), f32[216,128]{1,0:T(8,128)}) %reduce-scatter.7.cloned.1.call-update) | async-done | bytes 110608 | tf_op jit(solution)/shard_map/reduce_scatter | solution.py:139
  184.5 1.5 broadcast_multiply_fusion
  (56 shorter events, 2.7 us)
Async XLA Ops:
  7.2 101.7 %copy-start = (bf16[128,256]{1,0:T(8,128)(2,1)S(1)}, bf16[128,256]{1,0:T(8,128)(2,1)}, u32[]{:S(2)}) copy-start(bf16[128,256]{1,0:T(8,128)(2,1)} %param.14) | copy-start | bytes 196612
  7.2 77.2 %reduce-scatter.9.cloned.1.call-start = ((), (), s32[]{:S(2)}) async-start(), calls=%async_computation.6 | async-start | bytes 139264 | tf_op jit(solution)/shard_map/reduce_scatter | solution.py:136
  9.4 27.5 %copy-start.1 = (bf16[1,4,4,96,256]{4,3,2,1,0:T(8,128)(2,1)S(1)}, bf16[1,4,4,96,256]{4,3,2,1,0:T(8,128)(2,1)}, u32[]{:S(2)}) copy-start(bf16[1,4,4,96,256]{4,3,2,1,0:T(8,128)(2,1)} %param.15) | copy-start | bytes 2359300
  9.5 91.0 %reduce-scatter.11.cloned.1.call-start = ((), (), s32[]{:S(2)}) async-start(), calls=%async_computation.7 | async-start | bytes 12288 | tf_op jit(solution)/shard_map/reduce_scatter | solution.py:140
  10.6 18.6 %collective-permute-start.1 = (bf16[1,2,4,96,256]{4,3,2,1,0:T(8,128)(2,1)S(1)}, bf16[1,2,4,96,256]{4,3,2,1,0:T(8,128)(2,1)S(1)}, u32[]{:S(2)}, u32[]{:S(2)}) collective-permute-start(bf16[1,2,4,96,256]{4,3,2,1,0:T(8,128)(2,1)S(1)} %slice.213), channel_id=1, source_target_pairs={{1,0},{3,2},{5,4},{7,6},{9,8},{11,10},{13,12},{15,14},{17,16},{19,... | collective-permute-start | bytes 1179656 | tf_op jit(solution)/shard_map/ppermute | solution.py:17
  44.5 14.1 %copy-start.3 = (bf16[3456,256]{1,0:T(8,128)(2,1)S(1)}, bf16[3456,256]{1,0:T(8,128)(2,1)}, u32[]{:S(2)}) copy-start(bf16[3456,256]{1,0:T(8,128)(2,1)} %param.13) | copy-start | bytes 5308420
  44.5 14.1 %copy-start.4 = (bf16[1,9,256,128]{3,2,1,0:T(8,128)(2,1)S(1)}, bf16[1,9,256,128]{3,2,1,0:T(8,128)(2,1)}, u32[]{:S(2)}) copy-start(bf16[1,9,256,128]{3,2,1,0:T(8,128)(2,1)} %copy.11) | copy-start | bytes 1769476
  69.5 10.8 %copy-start.2 = (bf16[1,4,4,96,128]{4,3,2,1,0:T(8,128)(2,1)S(1)}, bf16[1,4,4,96,128]{4,3,2,1,0:T(8,128)(2,1)}, u32[]{:S(2)}) copy-start(bf16[1,4,4,96,128]{4,3,2,1,0:T(8,128)(2,1)} %param.10) | copy-start | bytes 1179652
  69.5 10.8 %copy-start.6 = (f32[128]{0:T(128)S(1)}, f32[128]{0:T(128)}, u32[]{:S(2)}) copy-start(f32[128]{0:T(128)} %param.12) | copy-start | bytes 1540
  69.5 10.8 %copy-start.7 = (f32[128]{0:T(128)S(1)}, f32[128]{0:T(128)}, u32[]{:S(2)}) copy-start(f32[128]{0:T(128)} %param.11) | copy-start | bytes 1540
  82.4 5.5 %collective-permute-start = (bf16[1,2,4,96,128]{4,3,2,1,0:T(8,128)(2,1)}, bf16[1,2,4,96,128]{4,3,2,1,0:T(8,128)(2,1)}, u32[]{:S(2)}, u32[]{:S(2)}) collective-permute-start(bf16[1,2,4,96,128]{4,3,2,1,0:T(8,128)(2,1)} %slice.232), channel_id=1, source_target_pairs={{0,1},{2,3},{4,5},{6,7},{8,9},{10,11},{12,13},{14,15},{16,17},{18,... | collective-permute-start | bytes 589832 | tf_op jit(solution)/shard_map/ppermute | solution.py:17
  84.4 87.8 %reduce-scatter.5.cloned.1.call-start = ((), (), s32[]{:S(2)}) async-start(), calls=%async_computation.4 | async-start | bytes 3760128 | tf_op jit(solution)/shard_map/reduce_scatter | solution.py:135
  91.6 4.0 %copy-start.5 = (bf16[1,4,4,96,3456]{4,3,2,1,0:T(8,128)(2,1)}, bf16[1,4,4,96,3456]{4,3,2,1,0:T(8,128)(2,1)S(1)}, u32[]{:S(2)}) copy-start(bf16[1,4,4,96,3456]{4,3,2,1,0:T(8,128)(2,1)S(1)} %fusion.65) | copy-start | bytes 31850500
  100.4 84.0 %reduce-scatter.7.cloned.1.call-start = ((), (), s32[]{:S(2)}) async-start(), calls=%async_computation.5 | async-start | bytes 331776 | tf_op jit(solution)/shard_map/reduce_scatter | solution.py:139
Sparse Core Ops, SparseCore 0:
  11.5 57.7 reduce-scatter.8
  84.5 10.8 reduce-scatter.10
  100.5 71.6 reduce-scatter.4
  174.3 10.1 reduce-scatter.6
where the time goes:
time: 193 us
  waiting for transfers between devices  69.9 us (36%)
  local copies, waits for them, and re-layouts  48.3 us (25%)
  matrix products  31.8 us (16%)
  blocking collectives  16.8 us (9%)
  between operations  14.1 us (7%)
  other arithmetic  8 us (4%)
  starting transfers between devices  3.41 us (2%)
    reduce_scatter x1, waiting for transfers between devices, body(): lax.psum_scatter(conv_part, 'dp', scatter_dimension=0, tiled=True)  61 us
    unnamed x49, local copies, waits for them, and re-layouts  19.4 us
    slice x1, local copies, waits for them, and re-layouts, body(): spatial[:, 2 - tap_t:2 - tap_t + frames].reshape(-1, KS * KS * out_width)  14 us
    dot_general x3, matrix products, body(): jnp.dot(block, w_back[tap_t], preferred_element_type=jnp.float32)  13.6 us
    psum x1, blocking collectives, group_stats(): lax.psum((jnp.sum(widened, axis=(1, 2, 3, 5)), jnp.sum(widened * widened,...  10.5 us
    psum x1, blocking collectives, body(): lax.psum((jnp.sum(grouped_grad, axis=(1, 2, 3, 5)), jnp.sum(grouped_grad...  6.31 us
    dot_general x1, matrix products, body(): result = jnp.dot(columns, conv_weight, preferred_element_type=jnp.float32)  5.7 us
    reduce_scatter x1, waiting for transfers between devices, body(): lax.psum_scatter(conv_part, 'ctx', scatter_dimension=1, tiled=True)  5.27 us
  transfers between devices with their start and end apart: 6, of which 3 were waited for; matrix products, arithmetic and copies ran while one was open for 42% of the time, Pallas kernels for 0%

commit v1 on v0

v1 whole, which is shorter than its diff:
```python
import functools
import math

import jax
import jax.numpy as jnp
from jax import lax
from jax.experimental import pallas as pl
from jax.experimental.pallas import tpu as pltpu
from jax.sharding import PartitionSpec as P

GROUPS = 32
KT = 3
KS = 3
TAPS = KT * KS * KS
VMEM_BYTES = 48 * 1024 * 1024

epsilon = 1e-06
f32 = jnp.float32
bf16 = jnp.bfloat16


def call(kernel, outs, scratch=(), flops=0, moved=0):
    return pl.pallas_call(
        kernel,
        out_shape=outs,
        scratch_shapes=list(scratch),
        compiler_params=pltpu.CompilerParams(vmem_limit_bytes=VMEM_BYTES),
        cost_estimate=pl.CostEstimate(flops=flops, bytes_accessed=moved, transcendentals=0),
    )


def group_totals(rows):
    width = rows.shape[1]
    per_group = width // GROUPS
    row = lax.broadcasted_iota(jnp.int32, (width, width), 0) // per_group
    col = lax.broadcasted_iota(jnp.int32, (width, width), 1) // per_group
    same = (row == col).astype(f32)
    return lax.dot_general(
        rows, same, (((1,), (0,)), ((), ())), precision=lax.Precision.HIGHEST, preferred_element_type=f32
    )


def two_rows(first, second):
    at = lax.broadcasted_iota(jnp.int32, (8, first.shape[1]), 0)
    return jnp.where(at == 0, first, jnp.where(at == 1, second, 0.0))


def column_totals(value):
    return jnp.sum(value, axis=0, keepdims=True)


def stats_kernel(clip_ref, out_ref):
    frames = clip_ref.shape[0]
    width = clip_ref.shape[-1]
    total = jnp.zeros((1, width), f32)
    square = jnp.zeros((1, width), f32)
    for frame in range(frames):
        value = clip_ref[frame].reshape(-1, width).astype(f32)
        total = total + column_totals(value)
        square = square + column_totals(value * value)
    out_ref[...] = group_totals(two_rows(total, square))


def moments(stats_a, stats_b, members):
    totals = stats_a[...] + stats_b[...]
    mean = totals[0:1] / members
    variance = totals[1:2] / members - mean * mean
    return mean, lax.rsqrt(variance + epsilon)


def shift_columns(value, step):
    rows, cols, width = value.shape
    flat = value.reshape(rows * cols, width)
    rolled = pltpu.roll(flat, (-step) % (rows * cols), 0).reshape(rows, cols, width)
    at = lax.broadcasted_iota(jnp.int32, (rows, cols, width), 1)
    edge = cols - 1 if step == 1 else 0
    return jnp.where(at == edge, 0.0, rolled)


def place(padded, frame, value):
    rows, cols, width = value.shape
    for j, step in enumerate((-1, 0, 1)):
        moved = value if step == 0 else shift_columns(value, step)
        padded[j, frame, 1 : rows + 1] = moved.astype(bf16)


def clear_edges(padded):
    rows = padded.shape[2]
    zero = jnp.zeros(padded.shape[:2] + padded.shape[3:], bf16)
    padded[:, :, 0] = zero
    padded[:, :, rows - 1] = zero


def fill_hidden(padded, clip_ref, halo_ref, mean, inv, gain, bias, at_start):
    clear_edges(padded)
    frames = clip_ref.shape[0]
    lead = halo_ref.shape[0]
    for frame in range(frames + lead):
        if frame < lead:
            value = jnp.where(at_start, clip_ref[0].astype(f32), halo_ref[frame].astype(f32))
        else:
            value = clip_ref[frame - lead].astype(f32)
        affine = (value - mean) * inv * gain + bias
        hidden = affine * jax.nn.sigmoid(affine)
        place(padded, frame, hidden)


def tap_block(padded, frames, rows, t, i):
    width = padded.shape[-1]
    return [padded[j, t : t + frames, i : i + rows].reshape(-1, width) for j in range(KS)]


def weight_kernel(
    members, split,
    clip_ref, halo_ref, stats_a, stats_b, gain_ref, bias_ref, cot_ref,
    *rest,
):
    outs, (padded, total) = rest[:-2], rest[-2:]
    frames, rows, cols, width = clip_ref.shape
    out_width = cot_ref.shape[-1]
    at_start = lax.axis_index("ctx") == 0
    mean, inv = moments(stats_a, stats_b, members)
    fill_hidden(padded, clip_ref, halo_ref, mean, inv, gain_ref[...], bias_ref[...], at_start)
    cot_t = cot_ref[...].reshape(-1, out_width).T
    pieces = []
    for t in range(KT):
        for i in range(KS):
            pieces.append((t, i))
    begin = 0
    for at in range(0, len(pieces), 2):
        parts = []
        for t, i in pieces[at : at + 2]:
            parts += tap_block(padded, frames, rows, t, i)
        if at + 2 > len(pieces):
            parts.append(clip_ref[...].reshape(-1, width))
        taps = jnp.concatenate(parts, axis=1)
        part = lax.dot_general(cot_t, taps, (((1,), (0,)), ((), ())), preferred_element_type=f32)
        part = part.T
        stop = begin + part.shape[0]
        if split is None:
            outs[0][begin:stop, :] = part
        else:
            scatter_rows(total, part, begin, split)
        begin = stop
    if split is not None:
        own_ref, send_ref = outs
        core = lax.rem(lax.axis_index("dp"), 2)
        halves, blocks = total.shape[0], total.shape[1] // 2
        for half in range(halves):
            for k in range(blocks):
                own_ref[half, k] = total[half, 2 * k + core]
                send_ref[half, k] = total[half, 2 * k + 1 - core].astype(bf16)


def scatter_rows(total, part, begin, split):
    conv_rows, short_rows, conv_all = split
    halves = total.shape[0]
    row, stop = begin, begin + part.shape[0]
    width = total.shape[-1]
    while row < stop:
        if row < conv_all:
            block, offset = divmod(row, conv_rows)
            count = min(conv_rows - offset, stop - row, conv_all - row)
            target = offset
        else:
            block, offset = divmod(row - conv_all, short_rows)
            count = min(short_rows - offset, stop - row)
            target = conv_rows + offset
        for half in range(halves):
            total[half, block, target : target + count, :] = part[
                row - begin : row - begin + count, half * width : (half + 1) * width
            ]
        row += count


def forward_kernel(
    members,
    clip_ref, halo_ref, stats_a, stats_b, gain_ref, bias_ref, weight_ref, short_ref, after_ref,
    out_ref, padded,
):
    frames, rows, cols, width = clip_ref.shape
    at_start = lax.axis_index("ctx") == 0
    mean, inv = moments(stats_a, stats_b, members)
    fill_hidden(padded, clip_ref, halo_ref, mean, inv, gain_ref[...], bias_ref[...], at_start)
    for frame in range(frames):
        parts = []
        for t in range(KT):
            for i in range(KS):
                for j in range(KS):
                    parts.append(padded[j, frame + t, i : i + rows].reshape(-1, width))
        split = len(parts) * width
        result = jnp.dot(jnp.concatenate(parts, axis=1), weight_ref[...], preferred_element_type=f32)
        result = result + jnp.dot(
            clip_ref[frame].reshape(-1, width), short_ref[...], preferred_element_type=f32
        )
        out_ref[frame] = result.astype(bf16).reshape(rows, cols, -1)


def back_weights(weight_ref, width, taps_t):
    bands = []
    for t in taps_t:
        bands.append(
            jnp.concatenate(
                [weight_ref[(t * KS * KS + q) * width : (t * KS * KS + q + 1) * width, :] for q in range(KS * KS)],
                axis=1,
            )
        )
    return jnp.concatenate(bands, axis=0) if len(bands) > 1 else bands[0]


def fill_cot(padded, cot_ref):
    clear_edges(padded)
    for frame in range(cot_ref.shape[0]):
        place(padded, frame, cot_ref[frame].astype(f32))


def spatial_block(padded, frame, rows):
    out_width = padded.shape[-1]
    parts = []
    for i in range(KS):
        for j in range(KS):
            parts.append(padded[2 - j, frame, 2 - i : 2 - i + rows].reshape(-1, out_width))
    return jnp.concatenate(parts, axis=1)


def back_dot(block, weights):
    return lax.dot_general(block, weights, (((1,), (1,)), ((), ())), preferred_element_type=f32)


def back_own_kernel(cot_ref, weight_ref, out_ref, padded):
    frames, rows, cols, out_width = cot_ref.shape
    width = out_ref.shape[-1]
    at_start = lax.axis_index("ctx") == 0
    fill_cot(padded, cot_ref)
    late = back_weights(weight_ref, width, (2, 1))
    early = back_weights(weight_ref, width, (0,))
    for frame in range(frames):
        block = spatial_block(padded, frame, rows)
        both = back_dot(block, late)
        y2, y1 = both[:, :width], both[:, width:]
        y0 = back_dot(block, early)
        if frame == 0:
            out_ref[0] = y2 + jnp.where(at_start, y1 + y0, 0.0)
        else:
            out_ref[frame] = y2
            out_ref[frame - 1] += y1
            if frame == 1:
                out_ref[0] += jnp.where(at_start, y0, 0.0)
            else:
                out_ref[frame - 2] += y0


def back_rest_kernel(
    members,
    part_ref, cot_ref, weight_ref, clip_ref, stats_a, stats_b, gain_ref, bias_ref,
    grad_ref, sums_ref, padded,
):
    frames, rows, cols, width = clip_ref.shape
    fill_cot(padded, cot_ref)
    late = back_weights(weight_ref, width, (1, 0))
    early = back_weights(weight_ref, width, (0,))
    both = back_dot(spatial_block(padded, 0, rows), late)
    y1, y0 = both[:, :width], both[:, width:]
    last = back_dot(spatial_block(padded, 1, rows), early)
    mean, inv = moments(stats_a, stats_b, members)
    total = jnp.zeros((1, width), f32)
    cross = jnp.zeros((1, width), f32)
    for frame in range(frames):
        grad = part_ref[frame]
        if frame == frames - 2:
            grad = grad + y0
        if frame == frames - 1:
            grad = grad + (y1 + last)
        standard = (clip_ref[frame].reshape(-1, width).astype(f32) - mean) * inv
        affine = standard * gain_ref[...] + bias_ref[...]
        logistic = jax.nn.sigmoid(affine)
        grad = grad * logistic * (1.0 + affine * (1.0 - logistic)) * gain_ref[...]
        grad_ref[frame] = grad
        total = total + column_totals(grad)
        cross = cross + column_totals(grad * standard)
    sums_ref[...] = group_totals(two_rows(total, cross))


def finish_kernel(
    members,
    grad_ref, sums_a, sums_b, clip_ref, stats_a, stats_b, cot_ref, short_ref,
    out_ref,
):
    frames, rows, cols, width = clip_ref.shape
    out_width = cot_ref.shape[-1]
    mean, inv = moments(stats_a, stats_b, members)
    sums = sums_a[...] + sums_b[...]
    mean_grad = sums[0:1] / members
    mean_cross = sums[1:2] / members
    for frame in range(frames):
        standard = (clip_ref[frame].reshape(-1, width).astype(f32) - mean) * inv
        shortcut = back_dot(cot_ref[frame].reshape(-1, out_width), short_ref[...])
        grad = (grad_ref[frame] - mean_grad - standard * mean_cross) * inv + shortcut
        out_ref[frame] = grad.astype(bf16).reshape(rows, cols, width)


def plane_kernel(own_ref, got_ref, keep_ref, x_ref, y_ref, xy_ref):
    halves, deep, wide = own_ref.shape[:3]
    x = lax.rem(lax.axis_index("dp") // 2, 2)
    y = lax.axis_index("ctx")
    for z in range(deep):
        for half, col, target in ((y, x, keep_ref), (y, 1 - x, x_ref), (1 - y, x, y_ref), (1 - y, 1 - x, xy_ref)):
            value = own_ref[half, z, col] + got_ref[half, z, col].astype(f32)
            target[z] = value.astype(target.dtype)


def line_kernel(keep_ref, x_ref, y_ref, xy_ref, own_ref, a_ref, b_ref, c_ref):
    z = lax.axis_index("dp") // 4
    for step, target in enumerate((own_ref, a_ref, b_ref, c_ref)):
        at = lax.bitwise_xor(z, step)
        value = keep_ref[at] + x_ref[at].astype(f32) + (y_ref[at].astype(f32) + xy_ref[at].astype(f32))
        target[...] = value.astype(target.dtype)


def last_kernel(scale, own_ref, a_ref, b_ref, c_ref, conv_ref, short_ref):
    value = own_ref[...] + a_ref[...].astype(f32) + (b_ref[...].astype(f32) + c_ref[...].astype(f32))
    value = value * scale
    conv_ref[...] = value[: conv_ref.shape[0]]
    short_ref[...] = value[conv_ref.shape[0] :]


def from_behind(value, axis, steps):
    count = lax.axis_size(axis)
    initial, last = (max(0, -steps), min(count, count - steps))
    return lax.ppermute(value, axis, [(source, source + steps) for source in range(initial, last)])


def others_total(value):
    count = lax.axis_size("ctx")
    total = None
    for step in range(1, count):
        got = lax.ppermute(value, "ctx", [(source, (source + step) % count) for source in range(count)])
        total = got if total is None else total + got
    return jnp.zeros_like(value) if total is None else total


def swap(value, dp_mask, ctx_mask=0):
    dp, ctx = lax.axis_size("dp"), lax.axis_size("ctx")
    pairs = []
    for source in range(dp * ctx):
        at, side = divmod(source, ctx)
        pairs.append((source, (at ^ dp_mask) * ctx + (side ^ ctx_mask)))
    return lax.ppermute(value, ("dp", "ctx"), pairs)


def reduce_staged(own, send, conv_rows, short_rows, scale):
    halves, blocks, rows, cols = own.shape
    got = swap(send, 1)
    shape = (halves, blocks // 2, 2, rows, cols)
    part = (blocks // 2, rows, cols)
    keep, to_x, to_y, to_xy = call(
        plane_kernel,
        [jax.ShapeDtypeStruct(part, f32)] + [jax.ShapeDtypeStruct(part, bf16)] * 3,
        moved=own.size * 8,
    )(own.reshape(shape), got.reshape(shape))
    from_x, from_y, from_xy = swap(to_x, 2), swap(to_y, 0, 1), swap(to_xy, 2, 1)
    mine, to_a, to_b, to_c = call(
        line_kernel,
        [jax.ShapeDtypeStruct(part[1:], f32)] + [jax.ShapeDtypeStruct(part[1:], bf16)] * 3,
        moved=keep.size * 12,
    )(keep, from_x, from_y, from_xy)
    from_a, from_b, from_c = swap(to_a, 4), swap(to_b, 8), swap(to_c, 12)
    return call(
        functools.partial(last_kernel, scale),
        [jax.ShapeDtypeStruct((conv_rows, cols), f32), jax.ShapeDtypeStruct((short_rows, cols), f32)],
        moved=mine.size * 12,
    )(mine, from_a, from_b, from_c)


def body(clip_in, norm_gain, norm_bias, conv_weight, short_weight, out_cotangent):
    batch_clips, frames, height, breadth, in_width = clip_in.shape
    assert batch_clips == 1
    out_width = conv_weight.shape[1]
    per_group = in_width // GROUPS
    dp_size, ctx_size = lax.axis_size("dp"), lax.axis_size("ctx")
    total_frames = frames * ctx_size
    members = total_frames * height * breadth * per_group
    scale = 1.0 / (batch_clips * dp_size * total_frames)
    places = frames * height * breadth
    clip = clip_in[0]
    cot = out_cotangent[0]
    gain = norm_gain.reshape(1, in_width)
    bias = norm_bias.reshape(1, in_width)
    conv_all = TAPS * in_width
    work = places * conv_all * out_width * 2

    halo = from_behind(clip[frames - 2 :], "ctx", 1)
    following = from_behind(cot[:2], "ctx", -1)
    stats = call(stats_kernel, jax.ShapeDtypeStruct((8, in_width), f32), moved=clip.size * 2)(clip)
    other = others_total(stats)

    back_part = call(
        back_own_kernel,
        jax.ShapeDtypeStruct((frames, height * breadth, in_width), f32),
        [pltpu.VMEM((KS, frames, height + 2, breadth, out_width), bf16)],
        flops=2 * work, moved=conv_weight.size * 2,
    )(cot, conv_weight)

    padded = pltpu.VMEM((KS, frames + 2, height + 2, breadth, in_width), bf16)
    staged = dp_size == 16 and ctx_size == 2
    conv_rows, short_rows = conv_all // dp_size, in_width // dp_size
    if staged:
        cols = out_width // ctx_size
        blocks = (ctx_size, dp_size // 2, conv_rows + short_rows, cols)
        outs = [jax.ShapeDtypeStruct(blocks, f32), jax.ShapeDtypeStruct(blocks, bf16)]
        total = pltpu.VMEM((ctx_size, dp_size, conv_rows + short_rows, cols), f32)
        split = (conv_rows, short_rows, conv_all)
    else:
        outs = [jax.ShapeDtypeStruct((conv_all + in_width, out_width), f32)]
        total = pltpu.VMEM((8, 128), f32)
        split = None
    parts = call(
        functools.partial(weight_kernel, members, split), outs, [padded, total], flops=work, moved=cot.size * 2
    )(clip, halo, stats, other, gain, bias, cot)
    if staged:
        conv_grad, short_grad = reduce_staged(*parts, conv_rows, short_rows, scale)
    else:
        summed = []
        for part in (parts[0][:conv_all], parts[0][conv_all:]):
            part = lax.psum_scatter(part, "dp", scatter_dimension=0, tiled=True)
            part = lax.psum_scatter(part, "ctx", scatter_dimension=1, tiled=True)
            summed.append(part * scale)
        conv_grad, short_grad = summed

    clip_out = call(
        functools.partial(forward_kernel, members),
        jax.ShapeDtypeStruct((frames, height, breadth, out_width), bf16),
        [padded],
        flops=work, moved=conv_weight.size * 2,
    )(clip, halo, stats, other, gain, bias, conv_weight, short_weight, stats)

    grad, sums = call(
        functools.partial(back_rest_kernel, members),
        [
            jax.ShapeDtypeStruct((frames, height * breadth, in_width), f32),
            jax.ShapeDtypeStruct((8, in_width), f32),
        ],
        [pltpu.VMEM((KS, 2, height + 2, breadth, out_width), bf16)],
        flops=work, moved=conv_weight.size * 2,
    )(back_part, following, conv_weight, clip, stats, other, gain, bias)
    other_sums = others_total(sums)
    clip_grad = call(
        functools.partial(finish_kernel, members),
        jax.ShapeDtypeStruct((frames, height, breadth, in_width), bf16),
        flops=work // 20, moved=cot.size * 4,
    )(grad, sums, other_sums, clip, stats, other, cot, short_weight)
    return (clip_out[None], clip_grad[None], conv_grad, short_grad)


def solution(mesh):
    return jax.shard_map(
        body,
        mesh=mesh,
        in_specs=(
            P("dp", "ctx", None, None, None),
            P(),
            P(),
            P(),
            P(),
            P("dp", "ctx", None, None, None),
        ),
        out_specs=(
            P("dp", "ctx", None, None, None),
            P("dp", "ctx", None, None, None),
            P("dp", "ctx"),
            P("dp", "ctx"),
        ),
        check_vma=False,
    )
```

time: 193 us -> 52.2 us (0.27)
  waiting for transfers between devices: 69.9 us -> 15.3 us
  local copies, waits for them, and re-layouts: 48.3 us -> 4.43 us
  matrix products: 31.8 us -> 0 us
  blocking collectives: 16.8 us -> 0 us
  Pallas kernels: 0 us -> 16.3 us
  between operations: 14.1 us -> 0.75 us
  starting transfers between devices: 3.41 us -> 15.2 us
  other arithmetic: 8 us -> 0 us
    reduce_scatter x4 -> x0, waiting for transfers between devices: 66.3 us -> none  [the longest x1 61 us: body(): lax.psum_scatter(conv_part, 'dp', scatter_dimension=0, tiled=True)]
    dot_general x11 -> x0, matrix products: 31.8 us -> none  [the longest x3 13.6 us: body(): jnp.dot(block, w_back[tap_t], preferred_element_type=jnp.float32)]
    slice x10 -> x2, local copies, waits for them, and re-layouts: 24.2 us -> 0.97 us  [the longest x1 0.94 us: body(): halo = from_behind(clip[frames - 2:], 'ctx', 1)]
    psum x2 -> x0, blocking collectives: 16.8 us -> none  [the longest x1 10.5 us: group_stats(): lax.psum((jnp.sum(widened, axis=(1, 2, 3, 5)), jnp.sum(widened * widened,...]
    pallas_call x0 -> x9, Pallas kernels: none -> 16.3 us  [the longest x1 4.18 us: body(): call(functools.partial(forward_kernel, members), jax.ShapeDtypeStruct((fr...]
    unnamed x49 -> x20, local copies, waits for them, and re-layouts: 19.4 us -> 3.46 us
    ppermute x0 -> x9, waiting for transfers between devices: none -> 11.4 us  [the longest x7 7.76 us: swap(): return lax.ppermute(value, ('dp', 'ctx'), pairs)]
    ppermute x0 -> x9, starting transfers between devices: none -> 8.8 us  [the longest x7 8.79 us: swap(): return lax.ppermute(value, ('dp', 'ctx'), pairs)]
  transfers between devices with their start and end apart: 6 -> 11, of which waited for: 3 -> 3; matrix products, arithmetic and copies ran while one was open for 42% -> 0% of each run, Pallas kernels for 0% -> 22%
where the time goes in v1:
time: 52.2 us; the launch traced here: 52 us
  Pallas kernels  16.3 us (31%)
  waiting for transfers between devices  15.3 us (29%)
  starting transfers between devices  15.2 us (29%)
  local copies, waits for them, and re-layouts  4.43 us (8%)
  between operations  0.75 us (1%)
    ppermute x7, starting transfers between devices, swap(): return lax.ppermute(value, ('dp', 'ctx'), pairs)  8.79 us
    ppermute x7, waiting for transfers between devices, swap(): return lax.ppermute(value, ('dp', 'ctx'), pairs)  7.76 us
    ppermute x2, starting transfers between devices, from_behind(): lax.ppermute(value, axis, [(source, source + steps) for source in range(i...  6.36 us
    pallas_call x1, Pallas kernels, body(): call(functools.partial(forward_kernel, members), jax.ShapeDtypeStruct((fr...  4.18 us
    pallas_call x1, Pallas kernels, body(): call(functools.partial(weight_kernel, members, split), outs, [padded, tot...  4.15 us
    ppermute x2, waiting for transfers between devices, from_behind(): lax.ppermute(value, axis, [(source, source + steps) for source in range(i...  3.94 us
    pallas_call x1, Pallas kernels, body(): call(back_own_kernel, jax.ShapeDtypeStruct((frames, height * breadth, in_...  3.87 us
    ppermute x2, waiting for transfers between devices, others_total(): lax.ppermute(value, 'ctx', [(source, (source + step) % count) for source...  3.62 us
  transfers between devices with their start and end apart: 11, of which 3 were waited for; matrix products, arithmetic and copies ran while one was open for 0% of the time, Pallas kernels for 22%

profile of v1, /device:TPU:0, one launch (start us, length us, event | category | flops | bytes accessed | tf_op | source)
XLA Modules:
  0.0 52.0 jit_solution(11742509167282743662)
XLA Ops:
  0.6 0.9 %slice_bitcast_fusion.1 = bf16[2,4,96,128]{3,2,1,0:T(8,128)(2,1)S(1)} fusion(bf16[1,4,4,96,128]{4,3,2,1,0:T(8,128)(2,1)} %param.6), kind=kLoop, calls=%fused_computation.1 | loop fusion | bytes 393216 | tf_op jit(solution)/shard_map/slice | solution.py:392
  1.6 4.9 %collective-permute-start = (bf16[2,4,96,128]{3,2,1,0:T(8,128)(2,1)S(1)}, bf16[2,4,96,128]{3,2,1,0:T(8,128)(2,1)S(1)}, u32[]{:S(2)}, u32[]{:S(2)}) collective-permute-start(bf16[2,4,96,128]{3,2,1,0:T(8,128)(2,1)S(1)} %slice_bitcast_fusion.1), channel_id=1, source_target_pairs={{0,1},{2,3},{4,5},{6,7},{8,9},{10,11},{12,13},{14,15},{16,17},{18,... | collective-permute-start | bytes 589832 | tf_op jit(solution)/shard_map/ppermute | solution.py:330
  6.5 0.0 copy-start
  6.5 1.0 %copy-done = bf16[1,4,4,96,128]{4,3,2,1,0:T(8,128)(2,1)S(1)} copy-done((bf16[1,4,4,96,128]{4,3,2,1,0:T(8,128)(2,1)S(1)}, bf16[1,4,4,96,128]{4,3,2,1,0:T(8,128)(2,1)}, u32[]{:S(2)}) %copy-start) | copy-done | bytes 393240
  7.5 0.3 shard_map.93.stats_a.after_ref
  7.7 0.0 collective-permute-start.1
  7.8 3.6 %collective-permute-done.1.stats_b = f32[8,128]{1,0:T(8,128)S(1)} collective-permute-done((f32[8,128]{1,0:T(8,128)S(1)}, f32[8,128]{1,0:T(8,128)S(1)}, u32[]{:S(2)}, u32[]{:S(2)}) %collective-permute-start.1) | collective-permute-done | bytes 4128 | tf_op jit(solution)/shard_map/ppermute | solution.py:337
  11.4 0.0 collective-permute-done.halo_ref
  11.4 0.0 copy-start.2
  11.4 1.1 %copy-done.2 = bf16[1,4,4,96,256]{4,3,2,1,0:T(8,128)(2,1)S(1)} copy-done((bf16[1,4,4,96,256]{4,3,2,1,0:T(8,128)(2,1)S(1)}, bf16[1,4,4,96,256]{4,3,2,1,0:T(8,128)(2,1)}, u32[]{:S(2)}) %copy-start.2) | copy-done | bytes 786456
  12.5 0.0 copy-start.6
  12.5 0.7 %copy-done.6 = f32[128]{0:T(128)S(1)} copy-done((f32[128]{0:T(128)S(1)}, f32[128]{0:T(128)}, u32[]{:S(2)}) %copy-start.6) | copy-done | bytes 536
  13.2 0.0 copy-start.8
  13.2 0.7 %copy-done.8 = f32[128]{0:T(128)S(1)} copy-done((f32[128]{0:T(128)S(1)}, f32[128]{0:T(128)}, u32[]{:S(2)}) %copy-start.8) | copy-done | bytes 536
  13.8 0.0 copy-start.3
  13.8 0.0 copy-start.5
  13.8 4.2 %shard_map.98 = (f32[2,8,224,128]{3,2,1,0:T(8,128)S(1)}, bf16[2,8,224,128]{3,2,1,0:T(8,128)(2,1)S(1)}) custom-call(bf16[4,4,96,128]{3,2,1,0:T(8,128)(2,1)S(1)} %bitcast.13, bf16[2,4,96,128]{3,2,1,0:T(8,128)(2,1)S(1)} %collective-permute-done.halo_ref, f32[8,128]{1,0:T(8,128)S(1)} %shard_map.93.stats_a.after_ref, ...), custom_call_target="tpu_custom_call" | custom-call | flops 2717908992 | bytes 786432 | tf_op jit(solution)/shard_map/pallas_call | solution.py:417
  18.0 0.1 collective-permute-start.4
  18.1 1.5 %collective-permute-start.2 = (bf16[2,4,96,256]{3,2,1,0:T(8,128)(2,1)S(1)}, bf16[2,4,96,256]{3,2,1,0:T(8,128)(2,1)S(1)}, u32[]{:S(2)}, u32[]{:S(2)}) collective-permute-start(bf16[2,4,96,256]{3,2,1,0:T(8,128)(2,1)S(1)} %slice_bitcast_fusion), channel_id=1, source_target_pairs={{1,0},{3,2},{5,4},{7,6},{9,8},{11,10},{13,12},{15,14},{17,16},{19,... | collective-permute-start | bytes 1179656 | tf_op jit(solution)/shard_map/ppermute | solution.py:330
  19.6 0.0 copy-done.3
  19.6 0.0 copy-done.5
  19.6 3.9 %shard_map.95.part_ref = f32[4,384,128]{2,1,0:T(8,128)S(1)} custom-call(bf16[4,4,96,256]{3,2,1,0:T(8,128)(2,1)S(1)} %bitcast.19, bf16[3456,256]{1,0:T(8,128)(2,1)S(1)} %copy-done.5), custom_call_target="tpu_custom_call" | custom-call | flops 5435817984 | bytes 1769472 | tf_op jit(solution)/shard_map/pallas_call | solution.py:397
  23.5 0.0 copy-start.1
  23.5 0.0 collective-permute-done.4
  23.5 0.2 shard_map.99
  23.7 1.6 %collective-permute-start.5 = (bf16[4,224,128]{2,1,0:T(8,128)(2,1)S(1)}, bf16[4,224,128]{2,1,0:T(8,128)(2,1)S(1)}, u32[]{:S(2)}, u32[]{:S(2)}) collective-permute-start(bf16[4,224,128]{2,1,0:T(8,128)(2,1)S(1)} %get-tuple-element.23), channel_id=1, source_target_pairs={{0,4},{1,5},{2,6},{3,7},{4,0},{5,1},{6,2},{7,3},{8,12},{9,13},{10,... | collective-permute-start | bytes 688136 | tf_op jit(solution)/shard_map/ppermute | solution.py:348
  25.2 2.7 %collective-permute-start.6 = (bf16[4,224,128]{2,1,0:T(8,128)(2,1)S(1)}, bf16[4,224,128]{2,1,0:T(8,128)(2,1)S(1)}, u32[]{:S(2)}, u32[]{:S(2)}) collective-permute-start(bf16[4,224,128]{2,1,0:T(8,128)(2,1)S(1)} %get-tuple-element.24), channel_id=1, source_target_pairs={{0,1},{1,0},{2,3},{3,2},{4,5},{5,4},{6,7},{7,6},{8,9},{9,8},{10,11... | collective-permute-start | bytes 688136 | tf_op jit(solution)/shard_map/ppermute | solution.py:348
  27.9 0.0 copy-start.4
  27.9 0.0 copy-start.7
  27.9 0.0 copy-start.9
  27.9 0.0 collective-permute-start.7
  28.0 3.9 %collective-permute-done.2.cot_ref = bf16[2,4,96,256]{3,2,1,0:T(8,128)(2,1)S(1)} collective-permute-done((bf16[2,4,96,256]{3,2,1,0:T(8,128)(2,1)S(1)}, bf16[2,4,96,256]{3,2,1,0:T(8,128)(2,1)S(1)}, u32[]{:S(2)}, u32[]{:S(2)}) %collective-permute-start.2) | collective-permute-done | bytes 393248 | tf_op jit(solution)/shard_map/ppermute | solution.py:330
  31.9 0.0 copy-done.1
  31.9 1.7 %shard_map.96 = (f32[4,384,128]{2,1,0:T(8,128)S(1)}, f32[8,128]{1,0:T(8,128)S(1)}) custom-call(f32[4,384,128]{2,1,0:T(8,128)S(1)} %shard_map.95.part_ref, bf16[2,4,96,256]{3,2,1,0:T(8,128)(2,1)S(1)} %collective-permute-done.2.cot_ref, bf16[3456,256]{1,0:T(8,128)(2,1)S(1)} %copy-done.5, bf16[4,4,96,128]{3,2,1,0:T(8,128)(2,1)S(1)} %bitcast.14, ...), custom_call_target="tpu_custom_call" | custom-call | flops 2717908992 | bytes 1769472 | tf_op jit(solution)/shard_map/pallas_call | solution.py:437
  33.6 0.0 collective-permute-start.3
  33.6 0.0 collective-permute-done.5.x_ref
  33.6 7.7 %collective-permute-done.6.y_ref = bf16[4,224,128]{2,1,0:T(8,128)(2,1)S(1)} collective-permute-done((bf16[4,224,128]{2,1,0:T(8,128)(2,1)S(1)}, bf16[4,224,128]{2,1,0:T(8,128)(2,1)S(1)}, u32[]{:S(2)}, u32[]{:S(2)}) %collective-permute-start.6) | collective-permute-done | bytes 229408 | tf_op jit(solution)/shard_map/ppermute | solution.py:348
  41.4 0.0 collective-permute-done.7.xy_ref
  41.4 0.1 shard_map.100
  41.5 3.7 %collective-permute-start.10 = (bf16[224,128]{1,0:T(8,128)(2,1)S(1)}, bf16[224,128]{1,0:T(8,128)(2,1)S(1)}, u32[]{:S(2)}, u32[]{:S(2)}) collective-permute-start(bf16[224,128]{1,0:T(8,128)(2,1)S(1)} %get-tuple-element.29), channel_id=1, source_target_pairs={{0,24},{1,25},{2,26},{3,27},{4,28},{5,29},{6,30},{7,31},{8,16},{9,... | collective-permute-start | bytes 172040 | tf_op jit(solution)/shard_map/ppermute | solution.py:348
  45.2 0.0 collective-permute-start.8
  45.2 0.8 %collective-permute-start.9 = (bf16[224,128]{1,0:T(8,128)(2,1)S(1)}, bf16[224,128]{1,0:T(8,128)(2,1)S(1)}, u32[]{:S(2)}, u32[]{:S(2)}) collective-permute-start(bf16[224,128]{1,0:T(8,128)(2,1)S(1)} %get-tuple-element.28), channel_id=1, source_target_pairs={{0,16},{1,17},{2,18},{3,19},{4,20},{5,21},{6,22},{7,23},{8,24},{9,... | collective-permute-start | bytes 172040 | tf_op jit(solution)/shard_map/ppermute | solution.py:348
  46.0 0.0 copy-done.4
  46.0 0.0 copy-done.7
  46.0 0.0 copy-done.9
  46.0 4.2 %shard_map.94 = bf16[4,4,96,256]{3,2,1,0:T(8,128)(2,1)} custom-call(bf16[4,4,96,128]{3,2,1,0:T(8,128)(2,1)S(1)} %bitcast.15, bf16[2,4,96,128]{3,2,1,0:T(8,128)(2,1)S(1)} %collective-permute-done.halo_ref, f32[8,128]{1,0:T(8,128)S(1)} %shard_map.93.stats_a.after_ref, f32[8,128]{1,0:T(8,128)S(1)} %collective-permute-done.1.stats_b, f32[1,128]{1,0:T(1,128)S(1)} %bitcast.24, ...), custom_call_target="tpu_custom_call" | custom-call | flops 2717908992 | bytes 1769472 | tf_op jit(solution)/shard_map/pallas_call | solution.py:430
  50.1 0.0 collective-permute-done.3.sums_b
  50.1 1.1 %shard_map.97 = bf16[4,4,96,128]{3,2,1,0:T(8,128)(2,1)} custom-call(f32[4,384,128]{2,1,0:T(8,128)S(1)} %get-tuple-element.18.grad_ref, f32[8,128]{1,0:T(8,128)S(1)} %get-tuple-element.19.sums_a, f32[8,128]{1,0:T(8,128)S(1)} %collective-permute-done.3.sums_b, bf16[4,4,96,128]{3,2,1,0:T(8,128)(2,1)S(1)} %bitcast.16, f32[8,128]{1,0:T(8,128)S(1)} %shard_map.93.stats_a.after_ref, ...), custom_call_target="tpu_custom_call" | custom-call | flops 135895456 | bytes 1572864 | tf_op jit(solution)/shard_map/pallas_call | solution.py:447
  51.3 0.0 collective-permute-done.10.c_ref
  51.3 0.0 collective-permute-done.8.a_ref
  51.3 0.0 collective-permute-done.9.b_ref
  51.3 0.7 %shard_map.101 = (f32[216,128]{1,0:T(8,128)}, f32[8,128]{1,0:T(8,128)}) custom-call(f32[224,128]{1,0:T(8,128)S(1)} %get-tuple-element.26.own_ref, bf16[224,128]{1,0:T(8,128)(2,1)S(1)} %collective-permute-done.8.a_ref, bf16[224,128]{1,0:T(8,128)(2,1)S(1)} %collective-permute-done.9.b_ref, bf16[224,128]{1,0:T(8,128)(2,1)S(1)} %collective-permute-done.10.c_ref), custom_call_target="tpu_custom_call" | custom-call | bytes 344064 | tf_op jit(solution)/shard_map/pallas_call | solution.py:368
  (1 shorter events, 0.0 us)
Async XLA Ops:
  1.6 9.8 %collective-permute-start = (bf16[2,4,96,128]{3,2,1,0:T(8,128)(2,1)S(1)}, bf16[2,4,96,128]{3,2,1,0:T(8,128)(2,1)S(1)}, u32[]{:S(2)}, u32[]{:S(2)}) collective-permute-start(bf16[2,4,96,128]{3,2,1,0:T(8,128)(2,1)S(1)} %slice_bitcast_fusion.1), channel_id=1, source_target_pairs={{0,1},{2,3},{4,5},{6,7},{8,9},{10,11},{12,13},{14,15},{16,17},{18,... | collective-permute-start | bytes 589832 | tf_op jit(solution)/shard_map/ppermute | solution.py:330
  6.5 1.0 %copy-start = (bf16[1,4,4,96,128]{4,3,2,1,0:T(8,128)(2,1)S(1)}, bf16[1,4,4,96,128]{4,3,2,1,0:T(8,128)(2,1)}, u32[]{:S(2)}) copy-start(bf16[1,4,4,96,128]{4,3,2,1,0:T(8,128)(2,1)} %param.6) | copy-start | bytes 1179652
  7.7 3.6 %collective-permute-start.1 = (f32[8,128]{1,0:T(8,128)S(1)}, f32[8,128]{1,0:T(8,128)S(1)}, u32[]{:S(2)}, u32[]{:S(2)}) collective-permute-start(f32[8,128]{1,0:T(8,128)S(1)} %shard_map.93.stats_a.after_ref), channel_id=1, source_target_pairs={{0,1},{1,0},{2,3},{3,2},{4,5},{5,4},{6,7},{7,6},{8,9},{9,8},{10,11... | collective-permute-start | bytes 12296 | tf_op jit(solution)/shard_map/ppermute | solution.py:337
  11.4 1.1 %copy-start.2 = (bf16[1,4,4,96,256]{4,3,2,1,0:T(8,128)(2,1)S(1)}, bf16[1,4,4,96,256]{4,3,2,1,0:T(8,128)(2,1)}, u32[]{:S(2)}) copy-start(bf16[1,4,4,96,256]{4,3,2,1,0:T(8,128)(2,1)} %param.11) | copy-start | bytes 2359300
  12.5 0.7 %copy-start.6 = (f32[128]{0:T(128)S(1)}, f32[128]{0:T(128)}, u32[]{:S(2)}) copy-start(f32[128]{0:T(128)} %param.7) | copy-start | bytes 1540
  13.2 0.7 %copy-start.8 = (f32[128]{0:T(128)S(1)}, f32[128]{0:T(128)}, u32[]{:S(2)}) copy-start(f32[128]{0:T(128)} %param.8) | copy-start | bytes 1540
  13.8 5.8 %copy-start.3 = (bf16[1,4,4,96,256]{4,3,2,1,0:T(8,128)(2,1)S(1)}, bf16[1,4,4,96,256]{4,3,2,1,0:T(8,128)(2,1)}, u32[]{:S(2)}) copy-start(bf16[1,4,4,96,256]{4,3,2,1,0:T(8,128)(2,1)} %param.11) | copy-start | bytes 2359300
  13.8 5.8 %copy-start.5 = (bf16[3456,256]{1,0:T(8,128)(2,1)S(1)}, bf16[3456,256]{1,0:T(8,128)(2,1)}, u32[]{:S(2)}) copy-start(bf16[3456,256]{1,0:T(8,128)(2,1)} %weight_ref.5) | copy-start | bytes 5308420
  18.0 5.5 %collective-permute-start.4 = (bf16[2,8,224,128]{3,2,1,0:T(8,128)(2,1)S(1)}, bf16[2,8,224,128]{3,2,1,0:T(8,128)(2,1)S(1)}, u32[]{:S(2)}, u32[]{:S(2)}) collective-permute-start(bf16[2,8,224,128]{3,2,1,0:T(8,128)(2,1)S(1)} %get-tuple-element.21), channel_id=1, source_target_pairs={{0,2},{1,3},{2,0},{3,1},{4,6},{5,7},{6,4},{7,5},{8,10},{9,11},{10,... | collective-permute-start | bytes 2752520 | tf_op jit(solution)/shard_map/ppermute | solution.py:348
  18.1 13.8 %collective-permute-start.2 = (bf16[2,4,96,256]{3,2,1,0:T(8,128)(2,1)S(1)}, bf16[2,4,96,256]{3,2,1,0:T(8,128)(2,1)S(1)}, u32[]{:S(2)}, u32[]{:S(2)}) collective-permute-start(bf16[2,4,96,256]{3,2,1,0:T(8,128)(2,1)S(1)} %slice_bitcast_fusion), channel_id=1, source_target_pairs={{1,0},{3,2},{5,4},{7,6},{9,8},{11,10},{13,12},{15,14},{17,16},{19,... | collective-permute-start | bytes 1179656 | tf_op jit(solution)/shard_map/ppermute | solution.py:330
  23.5 8.4 %copy-start.1 = (bf16[1,4,4,96,128]{4,3,2,1,0:T(8,128)(2,1)S(1)}, bf16[1,4,4,96,128]{4,3,2,1,0:T(8,128)(2,1)}, u32[]{:S(2)}) copy-start(bf16[1,4,4,96,128]{4,3,2,1,0:T(8,128)(2,1)} %param.6) | copy-start | bytes 1179652
  23.7 9.9 %collective-permute-start.5 = (bf16[4,224,128]{2,1,0:T(8,128)(2,1)S(1)}, bf16[4,224,128]{2,1,0:T(8,128)(2,1)S(1)}, u32[]{:S(2)}, u32[]{:S(2)}) collective-permute-start(bf16[4,224,128]{2,1,0:T(8,128)(2,1)S(1)} %get-tuple-element.23), channel_id=1, source_target_pairs={{0,4},{1,5},{2,6},{3,7},{4,0},{5,1},{6,2},{7,3},{8,12},{9,13},{10,... | collective-permute-start | bytes 688136 | tf_op jit(solution)/shard_map/ppermute | solution.py:348
  25.2 16.1 %collective-permute-start.6 = (bf16[4,224,128]{2,1,0:T(8,128)(2,1)S(1)}, bf16[4,224,128]{2,1,0:T(8,128)(2,1)S(1)}, u32[]{:S(2)}, u32[]{:S(2)}) collective-permute-start(bf16[4,224,128]{2,1,0:T(8,128)(2,1)S(1)} %get-tuple-element.24), channel_id=1, source_target_pairs={{0,1},{1,0},{2,3},{3,2},{4,5},{5,4},{6,7},{7,6},{8,9},{9,8},{10,11... | collective-permute-start | bytes 688136 | tf_op jit(solution)/shard_map/ppermute | solution.py:348
  27.9 18.0 %copy-start.4 = (bf16[128,256]{1,0:T(8,128)(2,1)S(1)}, bf16[128,256]{1,0:T(8,128)(2,1)}, u32[]{:S(2)}) copy-start(bf16[128,256]{1,0:T(8,128)(2,1)} %short_ref.3) | copy-start | bytes 196612
  27.9 18.0 %copy-start.7 = (f32[128]{0:T(128)S(1)}, f32[128]{0:T(128)}, u32[]{:S(2)}) copy-start(f32[128]{0:T(128)} %param.7) | copy-start | bytes 1540
  27.9 18.0 %copy-start.9 = (f32[128]{0:T(128)S(1)}, f32[128]{0:T(128)}, u32[]{:S(2)}) copy-start(f32[128]{0:T(128)} %param.8) | copy-start | bytes 1540
  27.9 13.5 %collective-permute-start.7 = (bf16[4,224,128]{2,1,0:T(8,128)(2,1)S(1)}, bf16[4,224,128]{2,1,0:T(8,128)(2,1)S(1)}, u32[]{:S(2)}, u32[]{:S(2)}) collective-permute-start(bf16[4,224,128]{2,1,0:T(8,128)(2,1)S(1)} %get-tuple-element.25), channel_id=1, source_target_pairs={{0,5},{1,4},{2,7},{3,6},{4,1},{5,0},{6,3},{7,2},{8,13},{9,12},{10,... | collective-permute-start | bytes 688136 | tf_op jit(solution)/shard_map/ppermute | solution.py:348
  33.6 16.5 %collective-permute-start.3 = (f32[8,128]{1,0:T(8,128)S(1)}, f32[8,128]{1,0:T(8,128)S(1)}, u32[]{:S(2)}, u32[]{:S(2)}) collective-permute-start(f32[8,128]{1,0:T(8,128)S(1)} %get-tuple-element.19.sums_a), channel_id=1, source_target_pairs={{0,1},{1,0},{2,3},{3,2},{4,5},{5,4},{6,7},{7,6},{8,9},{9,8},{10,11... | collective-permute-start | bytes 12296 | tf_op jit(solution)/shard_map/ppermute | solution.py:337
  41.5 9.8 %collective-permute-start.10 = (bf16[224,128]{1,0:T(8,128)(2,1)S(1)}, bf16[224,128]{1,0:T(8,128)(2,1)S(1)}, u32[]{:S(2)}, u32[]{:S(2)}) collective-permute-start(bf16[224,128]{1,0:T(8,128)(2,1)S(1)} %get-tuple-element.29), channel_id=1, source_target_pairs={{0,24},{1,25},{2,26},{3,27},{4,28},{5,29},{6,30},{7,31},{8,16},{9,... | collective-permute-start | bytes 172040 | tf_op jit(solution)/shard_map/ppermute | solution.py:348
  45.2 6.1 %collective-permute-start.8 = (bf16[224,128]{1,0:T(8,128)(2,1)S(1)}, bf16[224,128]{1,0:T(8,128)(2,1)S(1)}, u32[]{:S(2)}, u32[]{:S(2)}) collective-permute-start(bf16[224,128]{1,0:T(8,128)(2,1)S(1)} %get-tuple-element.27), channel_id=1, source_target_pairs={{0,8},{1,9},{2,10},{3,11},{4,12},{5,13},{6,14},{7,15},{8,0},{9,1},... | collective-permute-start | bytes 172040 | tf_op jit(solution)/shard_map/ppermute | solution.py:348
  45.2 6.1 %collective-permute-start.9 = (bf16[224,128]{1,0:T(8,128)(2,1)S(1)}, bf16[224,128]{1,0:T(8,128)(2,1)S(1)}, u32[]{:S(2)}, u32[]{:S(2)}) collective-permute-start(bf16[224,128]{1,0:T(8,128)(2,1)S(1)} %get-tuple-element.28), channel_id=1, source_target_pairs={{0,16},{1,17},{2,18},{3,19},{4,20},{5,21},{6,22},{7,23},{8,24},{9,... | collective-permute-start | bytes 172040 | tf_op jit(solution)/shard_map/ppermute | solution.py:348

commit v2 on v1

--- a/solution.py
+++ b/solution.py
@@ -1,5 +1,4 @@
 import functools
-import math
 
 import jax
 import jax.numpy as jnp
@@ -12,17 +11,19 @@
 KT = 3
 KS = 3
 TAPS = KT * KS * KS
-VMEM_BYTES = 48 * 1024 * 1024
+VMEM_BYTES = 28 * 1024 * 1024
 
 epsilon = 1e-06
 f32 = jnp.float32
 bf16 = jnp.bfloat16
 
 
-def call(kernel, outs, scratch=(), flops=0, moved=0):
+def call(kernel, outs, scratch=(), flops=0, moved=0, in_specs=None):
+    specs = {} if in_specs is None else {"in_specs": in_specs}
     return pl.pallas_call(
         kernel,
         out_shape=outs,
+        **specs,
         scratch_shapes=list(scratch),
         compiler_params=pltpu.CompilerParams(vmem_limit_bytes=VMEM_BYTES),
         cost_estimate=pl.CostEstimate(flops=flops, bytes_accessed=moved, transcendentals=0),
@@ -49,20 +50,40 @@
     return jnp.sum(value, axis=0, keepdims=True)
 
 
-def stats_kernel(clip_ref, out_ref):
-    frames = clip_ref.shape[0]
-    width = clip_ref.shape[-1]
+def in_pieces(value):
+    high = value.astype(bf16)
+    rest = value - high.astype(f32)
+    middle = rest.astype(bf16)
+    low = (rest - middle.astype(f32)).astype(bf16)
+    return high, middle, low
+
+
+def pieces_block(totals):
+    pieces = [piece[0:2].astype(f32) for piece in in_pieces(totals)]
+    zero = jnp.zeros((10, totals.shape[1]), f32)
+    return jnp.concatenate(pieces + [zero], axis=0).astype(bf16)
+
+
+def start_kernel(clip_ref, stats_ref, parcel_ref):
+    frames, rows, cols, width = clip_ref.shape
+    places = rows * cols
     total = jnp.zeros((1, width), f32)
     square = jnp.zeros((1, width), f32)
     for frame in range(frames):
         value = clip_ref[frame].reshape(-1, width).astype(f32)
         total = total + column_totals(value)
         square = square + column_totals(value * value)
-    out_ref[...] = group_totals(two_rows(total, square))
-
-
-def moments(stats_a, stats_b, members):
-    totals = stats_a[...] + stats_b[...]
+    totals = group_totals(two_rows(total, square))
+    stats_ref[...] = totals
+    lead = KT - 1
+    for frame in range(lead):
+        parcel_ref[frame * places : (frame + 1) * places] = clip_ref[frames - lead + frame].reshape(places, width)
+    parcel_ref[lead * places :] = pieces_block(totals)
+
+
+def moments(stats, parcel, members):
+    pieces = parcel[parcel.shape[0] - 16 :].astype(f32)
+    totals = stats[0:2] + (pieces[0:2] + (pieces[2:4] + pieces[4:6]))
     mean = totals[0:1] / members
     variance = totals[1:2] / members - mean * mean
     return mean, lax.rsqrt(variance + epsilon)
@@ -91,18 +112,24 @@
     padded[:, :, rows - 1] = zero
 
 
-def fill_hidden(padded, clip_ref, halo_ref, mean, inv, gain, bias, at_start):
+def hidden_of(value, mean, inv, gain, bias):
+    affine = (value.astype(f32) - mean) * inv * gain + bias
+    return affine * jax.nn.sigmoid(affine)
+
+
+def fill_hidden(padded, clip_ref, parcel_ref, mean, inv, gain, bias):
     clear_edges(padded)
-    frames = clip_ref.shape[0]
-    lead = halo_ref.shape[0]
+    frames, rows, cols, width = clip_ref.shape
+    places = rows * cols
+    lead = KT - 1
+    at_start = lax.axis_index("ctx") == 0
     for frame in range(frames + lead):
         if frame < lead:
-            value = jnp.where(at_start, clip_ref[0].astype(f32), halo_ref[frame].astype(f32))
+            before = parcel_ref[frame * places : (frame + 1) * places].reshape(rows, cols, width)
+            value = jnp.where(at_start, clip_ref[0].astype(f32), before.astype(f32))
         else:
             value = clip_ref[frame - lead].astype(f32)
-        affine = (value - mean) * inv * gain + bias
-        hidden = affine * jax.nn.sigmoid(affine)
-        place(padded, frame, hidden)
+        place(padded, frame, hidden_of(value, mean, inv, gain, bias))
 
 
 def tap_block(padded, frames, rows, t, i):
@@ -112,38 +139,31 @@
 
 def weight_kernel(
     members, split,
-    clip_ref, halo_ref, stats_a, stats_b, gain_ref, bias_ref, cot_ref,
-    *rest,
+    clip_ref, parcel_ref, stats_ref, gain_ref, bias_ref, cot_ref,
+    padded, *rest,
 ):
-    outs, (padded, total) = rest[:-2], rest[-2:]
     frames, rows, cols, width = clip_ref.shape
     out_width = cot_ref.shape[-1]
-    at_start = lax.axis_index("ctx") == 0
-    mean, inv = moments(stats_a, stats_b, members)
-    fill_hidden(padded, clip_ref, halo_ref, mean, inv, gain_ref[...], bias_ref[...], at_start)
+    mean, inv = moments(stats_ref, parcel_ref, members)
+    fill_hidden(padded, clip_ref, parcel_ref, mean, inv, gain_ref[...], bias_ref[...])
     cot_t = cot_ref[...].reshape(-1, out_width).T
-    pieces = []
-    for t in range(KT):
-        for i in range(KS):
-            pieces.append((t, i))
+    pieces = [(t, i) for t in range(KT) for i in range(KS)]
     begin = 0
+    total = rest[-1]
     for at in range(0, len(pieces), 2):
         parts = []
         for t, i in pieces[at : at + 2]:
             parts += tap_block(padded, frames, rows, t, i)
         if at + 2 > len(pieces):
             parts.append(clip_ref[...].reshape(-1, width))
-        taps = jnp.concatenate(parts, axis=1)
-        part = lax.dot_general(cot_t, taps, (((1,), (0,)), ((), ())), preferred_element_type=f32)
-        part = part.T
-        stop = begin + part.shape[0]
+        part = jnp.dot(cot_t, jnp.concatenate(parts, axis=1), preferred_element_type=f32).T
         if split is None:
-            outs[0][begin:stop, :] = part
+            rest[0][begin : begin + part.shape[0], :] = part
         else:
             scatter_rows(total, part, begin, split)
-        begin = stop
+        begin += part.shape[0]
     if split is not None:
-        own_ref, send_ref = outs
+        own_ref, send_ref = rest[:-1]
         core = lax.rem(lax.axis_index("dp"), 2)
         halves, blocks = total.shape[0], total.shape[1] // 2
         for half in range(halves):
@@ -173,22 +193,14 @@
         row += count
 
 
-def forward_kernel(
-    members,
-    clip_ref, halo_ref, stats_a, stats_b, gain_ref, bias_ref, weight_ref, short_ref, after_ref,
-    out_ref, padded,
-):
+def forward_kernel(padded, clip_ref, weight_ref, short_ref, out_ref):
     frames, rows, cols, width = clip_ref.shape
-    at_start = lax.axis_index("ctx") == 0
-    mean, inv = moments(stats_a, stats_b, members)
-    fill_hidden(padded, clip_ref, halo_ref, mean, inv, gain_ref[...], bias_ref[...], at_start)
     for frame in range(frames):
         parts = []
         for t in range(KT):
             for i in range(KS):
                 for j in range(KS):
                     parts.append(padded[j, frame + t, i : i + rows].reshape(-1, width))
-        split = len(parts) * width
         result = jnp.dot(jnp.concatenate(parts, axis=1), weight_ref[...], preferred_element_type=f32)
         result = result + jnp.dot(
             clip_ref[frame].reshape(-1, width), short_ref[...], preferred_element_type=f32
@@ -227,7 +239,7 @@
     return lax.dot_general(block, weights, (((1,), (1,)), ((), ())), preferred_element_type=f32)
 
 
-def back_own_kernel(cot_ref, weight_ref, out_ref, padded):
+def back_kernel(cot_ref, weight_ref, out_ref, before_ref, padded):
     frames, rows, cols, out_width = cot_ref.shape
     width = out_ref.shape[-1]
     at_start = lax.axis_index("ctx") == 0
@@ -240,37 +252,34 @@
         y2, y1 = both[:, :width], both[:, width:]
         y0 = back_dot(block, early)
         if frame == 0:
-            out_ref[0] = y2 + jnp.where(at_start, y1 + y0, 0.0)
+            lead, next_lead = y0, y1
+            out_ref[0] = y2
         else:
             out_ref[frame] = y2
             out_ref[frame - 1] += y1
             if frame == 1:
-                out_ref[0] += jnp.where(at_start, y0, 0.0)
+                next_lead = next_lead + y0
+                before_ref[0] = lead.astype(bf16)
+                before_ref[1] = next_lead.astype(bf16)
+                out_ref[0] += jnp.where(at_start, lead + next_lead, 0.0)
             else:
                 out_ref[frame - 2] += y0
 
 
-def back_rest_kernel(
+def activation_kernel(
     members,
-    part_ref, cot_ref, weight_ref, clip_ref, stats_a, stats_b, gain_ref, bias_ref,
-    grad_ref, sums_ref, padded,
+    part_ref, after_ref, clip_ref, parcel_ref, stats_ref, gain_ref, bias_ref,
+    grad_ref, sums_ref,
 ):
     frames, rows, cols, width = clip_ref.shape
-    fill_cot(padded, cot_ref)
-    late = back_weights(weight_ref, width, (1, 0))
-    early = back_weights(weight_ref, width, (0,))
-    both = back_dot(spatial_block(padded, 0, rows), late)
-    y1, y0 = both[:, :width], both[:, width:]
-    last = back_dot(spatial_block(padded, 1, rows), early)
-    mean, inv = moments(stats_a, stats_b, members)
+    mean, inv = moments(stats_ref, parcel_ref, members)
     total = jnp.zeros((1, width), f32)
     cross = jnp.zeros((1, width), f32)
+    ahead = after_ref.shape[0]
     for frame in range(frames):
         grad = part_ref[frame]
-        if frame == frames - 2:
-            grad = grad + y0
-        if frame == frames - 1:
-            grad = grad + (y1 + last)
+        if frame >= frames - ahead:
+            grad = grad + after_ref[frame - (frames - ahead)].astype(f32)
         standard = (clip_ref[frame].reshape(-1, width).astype(f32) - mean) * inv
         affine = standard * gain_ref[...] + bias_ref[...]
         logistic = jax.nn.sigmoid(affine)
@@ -283,12 +292,12 @@
 
 def finish_kernel(
     members,
-    grad_ref, sums_a, sums_b, clip_ref, stats_a, stats_b, cot_ref, short_ref,
+    grad_ref, sums_a, sums_b, clip_ref, parcel_ref, stats_ref, cot_ref, short_ref,
     out_ref,
 ):
     frames, rows, cols, width = clip_ref.shape
     out_width = cot_ref.shape[-1]
-    mean, inv = moments(stats_a, stats_b, members)
+    mean, inv = moments(stats_ref, parcel_ref, members)
     sums = sums_a[...] + sums_b[...]
     mean_grad = sums[0:1] / members
     mean_cross = sums[1:2] / members
@@ -309,7 +318,7 @@
             target[z] = value.astype(target.dtype)
 
 
-def line_kernel(keep_ref, x_ref, y_ref, xy_ref, own_ref, a_ref, b_ref, c_ref):
+def line_kernel(keep_ref, xy_ref, x_ref, y_ref, own_ref, a_ref, b_ref, c_ref):
     z = lax.axis_index("dp") // 4
     for step, target in enumerate((own_ref, a_ref, b_ref, c_ref)):
         at = lax.bitwise_xor(z, step)
@@ -348,23 +357,28 @@
     return lax.ppermute(value, ("dp", "ctx"), pairs)
 
 
-def reduce_staged(own, send, conv_rows, short_rows, scale):
+def sort_plane(own, got):
     halves, blocks, rows, cols = own.shape
-    got = swap(send, 1)
     shape = (halves, blocks // 2, 2, rows, cols)
     part = (blocks // 2, rows, cols)
-    keep, to_x, to_y, to_xy = call(
+    return call(
         plane_kernel,
         [jax.ShapeDtypeStruct(part, f32)] + [jax.ShapeDtypeStruct(part, bf16)] * 3,
         moved=own.size * 8,
     )(own.reshape(shape), got.reshape(shape))
-    from_x, from_y, from_xy = swap(to_x, 2), swap(to_y, 0, 1), swap(to_xy, 2, 1)
-    mine, to_a, to_b, to_c = call(
+
+
+def sort_line(keep, *planes):
+    part = keep.shape[1:]
+    return call(
         line_kernel,
-        [jax.ShapeDtypeStruct(part[1:], f32)] + [jax.ShapeDtypeStruct(part[1:], bf16)] * 3,
+        [jax.ShapeDtypeStruct(part, f32)] + [jax.ShapeDtypeStruct(part, bf16)] * 3,
         moved=keep.size * 12,
-    )(keep, from_x, from_y, from_xy)
-    from_a, from_b, from_c = swap(to_a, 4), swap(to_b, 8), swap(to_c, 12)
+    )(keep, *planes)
+
+
+def add_line(mine, from_a, from_b, from_c, conv_rows, short_rows, scale):
+    cols = mine.shape[1]
     return call(
         functools.partial(last_kernel, scale),
         [jax.ShapeDtypeStruct((conv_rows, cols), f32), jax.ShapeDtypeStruct((short_rows, cols), f32)],
@@ -389,36 +403,79 @@
     conv_all = TAPS * in_width
     work = places * conv_all * out_width * 2
 
-    halo = from_behind(clip[frames - 2 :], "ctx", 1)
-    following = from_behind(cot[:2], "ctx", -1)
-    stats = call(stats_kernel, jax.ShapeDtypeStruct((8, in_width), f32), moved=clip.size * 2)(clip)
-    other = others_total(stats)
-
-    back_part = call(
-        back_own_kernel,
-        jax.ShapeDtypeStruct((frames, height * breadth, in_width), f32),
+    lead = KT - 1
+    stats, parcel = call(
+        start_kernel,
+        [
+            jax.ShapeDtypeStruct((8, in_width), f32),
+            jax.ShapeDtypeStruct((lead * height * breadth + 16, in_width), bf16),
+        ],
+        flops=work, moved=clip.size * 2,
+    )(clip)
+    if ctx_size == 2:
+        before = lax.ppermute(parcel, "ctx", [(0, 1), (1, 0)])
+    else:
+        before = from_behind(clip[frames - lead :], "ctx", 1).reshape(-1, in_width)
+        before = jnp.concatenate([before, pieces_block(others_total(stats))], axis=0)
+
+    back_part, leading = call(
+        back_kernel,
+        [
+            jax.ShapeDtypeStruct((frames, height * breadth, in_width), f32),
+            jax.ShapeDtypeStruct((lead, height * breadth, in_width), bf16),
+        ],
         [pltpu.VMEM((KS, frames, height + 2, breadth, out_width), bf16)],
         flops=2 * work, moved=conv_weight.size * 2,
     )(cot, conv_weight)
-
-    padded = pltpu.VMEM((KS, frames + 2, height + 2, breadth, in_width), bf16)
+    before, back_part = lax.optimization_barrier((before, back_part))
+    after = from_behind(leading, "ctx", -1)
+
     staged = dp_size == 16 and ctx_size == 2
     conv_rows, short_rows = conv_all // dp_size, in_width // dp_size
     if staged:
         cols = out_width // ctx_size
         blocks = (ctx_size, dp_size // 2, conv_rows + short_rows, cols)
         outs = [jax.ShapeDtypeStruct(blocks, f32), jax.ShapeDtypeStruct(blocks, bf16)]
-        total = pltpu.VMEM((ctx_size, dp_size, conv_rows + short_rows, cols), f32)
+        scratch = [pltpu.VMEM((ctx_size, dp_size, conv_rows + short_rows, cols), f32)]
         split = (conv_rows, short_rows, conv_all)
     else:
         outs = [jax.ShapeDtypeStruct((conv_all + in_width, out_width), f32)]
-        total = pltpu.VMEM((8, 128), f32)
+        scratch = []
         split = None
-    parts = call(
-        functools.partial(weight_kernel, members, split), outs, [padded, total], flops=work, moved=cot.size * 2
-    )(clip, halo, stats, other, gain, bias, cot)
+    hidden, *parts = call(
+        functools.partial(weight_kernel, members, split),
+        [jax.ShapeDtypeStruct((KS, frames + KT - 1, height + 2, breadth, in_width), bf16)] + outs,
+        scratch,
+        flops=work, moved=cot.size * 2,
+    )(clip, before, stats, gain, bias, cot)
+
+    after, *parts = lax.optimization_barrier((after, *parts))
+    grad, sums = call(
+        functools.partial(activation_kernel, members),
+        [
+            jax.ShapeDtypeStruct((frames, height * breadth, in_width), f32),
+            jax.ShapeDtypeStruct((8, in_width), f32),
+        ],
+        flops=work, moved=conv_weight.size * 2,
+    )(back_part, after, clip, before, stats, gain, bias)
     if staged:
-        conv_grad, short_grad = reduce_staged(*parts, conv_rows, short_rows, scale)
+        own, got, sums = lax.optimization_barrier((parts[0], swap(parts[1], 1), sums))
+        keep, to_x, to_y, to_xy = sort_plane(own, got)
+        from_xy, from_x, from_y = swap(to_xy, 2, 1), swap(to_x, 2), swap(to_y, 0, 1)
+        planes = (from_xy, from_x, from_y)
+        hidden, keep = lax.optimization_barrier((hidden, keep))
+    other_sums = others_total(sums)
+    clip_out = call(
+        forward_kernel,
+        jax.ShapeDtypeStruct((frames, height, breadth, out_width), bf16),
+        flops=work, moved=conv_weight.size * 2,
+    )(hidden, clip, conv_weight, short_weight)
+    if staged:
+        *planes, clip_out, other_sums = lax.optimization_barrier((*planes, clip_out, other_sums))
+        mine, *lines = sort_line(keep, *planes)
+        lines = (swap(lines[2], 12), swap(lines[1], 8), swap(lines[0], 4))
+        conv_grad, short_grad = add_line(mine, *lines, conv_rows, short_rows, scale)
+        grad, mine = lax.optimization_barrier((grad, mine))
     else:
         summed = []
         for part in (parts[0][:conv_all], parts[0][conv_all:]):
@@ -427,28 +484,11 @@
             summed.append(part * scale)
         conv_grad, short_grad = summed
 
-    clip_out = call(
-        functools.partial(forward_kernel, members),
-        jax.ShapeDtypeStruct((frames, height, breadth, out_width), bf16),
-        [padded],
-        flops=work, moved=conv_weight.size * 2,
-    )(clip, halo, stats, other, gain, bias, conv_weight, short_weight, stats)
-
-    grad, sums = call(
-        functools.partial(back_rest_kernel, members),
-        [
-            jax.ShapeDtypeStruct((frames, height * breadth, in_width), f32),
-            jax.ShapeDtypeStruct((8, in_width), f32),
-        ],
-        [pltpu.VMEM((KS, 2, height + 2, breadth, out_width), bf16)],
-        flops=work, moved=conv_weight.size * 2,
-    )(back_part, following, conv_weight, clip, stats, other, gain, bias)
-    other_sums = others_total(sums)
     clip_grad = call(
         functools.partial(finish_kernel, members),
         jax.ShapeDtypeStruct((frames, height, breadth, in_width), bf16),
         flops=work // 20, moved=cot.size * 4,
-    )(grad, sums, other_sums, clip, stats, other, cot, short_weight)
+    )(grad, sums, other_sums, clip, before, stats, cot, short_weight)
     return (clip_out[None], clip_grad[None], conv_grad, short_grad)
 
 

time: 52.2 us -> 43.4 us (0.83)
  local copies, waits for them, and re-layouts: 4.43 us -> 1.01 us
  starting transfers between devices: 15.2 us -> 12.5 us
  waiting for transfers between devices: 15.3 us -> 13.8 us
  Pallas kernels: 16.3 us -> 15.3 us
    ppermute x2 -> x1, starting transfers between devices: 6.36 us -> 1.29 us  [from_behind(): lax.ppermute(value, axis, [(source, source + steps) for source in range(i...]
    ppermute x2 -> x1, waiting for transfers between devices: 3.62 us -> 0.01 us  [others_total(): lax.ppermute(value, 'ctx', [(source, (source + step) % count) for source...]
    ppermute x7, waiting for transfers between devices: 7.76 us -> 11.1 us  [swap(): return lax.ppermute(value, ('dp', 'ctx'), pairs)]
    ppermute x0 -> x1, starting transfers between devices: none -> 2.97 us  [body(): before = lax.ppermute(parcel, 'ctx', [(0, 1), (1, 0)])]
    unnamed x20 -> x12, local copies, waits for them, and re-layouts: 3.46 us -> 1.01 us
    ppermute x2 -> x1, waiting for transfers between devices: 3.94 us -> 2.71 us  [from_behind(): lax.ppermute(value, axis, [(source, source + steps) for source in range(i...]
    pallas_call x8, Pallas kernels: 15.2 us -> 14.1 us  [the longest x1 4.21 us: body(): call(functools.partial(weight_kernel, members, split), [jax.ShapeDtypeStr...]
    slice x2 -> x0, local copies, waits for them, and re-layouts: 0.97 us -> none  [the longest x1 0.94 us: body(): halo = from_behind(clip[frames - 2:], 'ctx', 1)]
  transfers between devices with their start and end apart: 11 -> 10, of which waited for: 3 -> 6; matrix products, arithmetic and copies ran while one was open for 0% -> 0% of each run, Pallas kernels for 22% -> 32%
where the time goes in v2:
time: 43.4 us; the launch traced here: 43.3 us
  Pallas kernels  15.3 us (35%)
  waiting for transfers between devices  13.8 us (32%)
  starting transfers between devices  12.5 us (29%)
  local copies, waits for them, and re-layouts  1.01 us (2%)
  between operations  0.71 us (2%)
    ppermute x7, waiting for transfers between devices, swap(): return lax.ppermute(value, ('dp', 'ctx'), pairs)  11.1 us
    ppermute x7, starting transfers between devices, swap(): return lax.ppermute(value, ('dp', 'ctx'), pairs)  8.15 us
    pallas_call x1, Pallas kernels, body(): call(functools.partial(weight_kernel, members, split), [jax.ShapeDtypeStr...  4.21 us
    pallas_call x1, Pallas kernels, body(): call(forward_kernel, jax.ShapeDtypeStruct((frames, height, breadth, out_w...  4.07 us
    pallas_call x1, Pallas kernels, body(): call(back_kernel, [jax.ShapeDtypeStruct((frames, height * breadth, in_wid...  3.86 us
    ppermute x1, starting transfers between devices, body(): before = lax.ppermute(parcel, 'ctx', [(0, 1), (1, 0)])  2.97 us
    ppermute x1, waiting for transfers between devices, from_behind(): lax.ppermute(value, axis, [(source, source + steps) for source in range(i...  2.71 us
    ppermute x1, starting transfers between devices, from_behind(): lax.ppermute(value, axis, [(source, source + steps) for source in range(i...  1.29 us
  transfers between devices with their start and end apart: 10, of which 6 were waited for; matrix products, arithmetic and copies ran while one was open for 0% of the time, Pallas kernels for 32%

profile of v2, /device:TPU:0, one launch (start us, length us, event | category | flops | bytes accessed | tf_op | source)
XLA Modules:
  0.0 43.3 jit_solution(14077092496219344762)
XLA Ops:
  0.6 0.0 copy-start.1
  0.6 1.0 %copy-done.1 = bf16[1,4,4,96,128]{4,3,2,1,0:T(8,128)(2,1)S(1)} copy-done((bf16[1,4,4,96,128]{4,3,2,1,0:T(8,128)(2,1)S(1)}, bf16[1,4,4,96,128]{4,3,2,1,0:T(8,128)(2,1)}, u32[]{:S(2)}) %copy-start.1) | copy-done | bytes 393240
  1.6 0.0 copy-start
  1.6 0.0 copy-start.3
  1.6 0.3 shard_map.94
  1.9 3.0 %collective-permute-start.1 = (bf16[784,128]{1,0:T(8,128)(2,1)S(1)}, bf16[784,128]{1,0:T(8,128)(2,1)S(1)}, u32[]{:S(2)}, u32[]{:S(2)}) collective-permute-start(bf16[784,128]{1,0:T(8,128)(2,1)S(1)} %get-tuple-element.40), channel_id=1, source_target_pairs={{0,1},{1,0},{2,3},{3,2},{4,5},{5,4},{6,7},{7,6},{8,9},{9,8},{10,11... | collective-permute-start | bytes 602120 | tf_op jit(solution)/shard_map/ppermute | solution.py:416
  4.9 0.0 copy-done
  4.9 0.0 copy-done.3
  4.9 0.0 copy-start.4
  4.9 0.0 copy-start.5
  4.9 3.9 %shard_map.93 = (f32[4,384,128]{2,1,0:T(8,128)S(1)}, bf16[2,384,128]{2,1,0:T(8,128)(2,1)S(1)}) custom-call(bf16[4,4,96,256]{3,2,1,0:T(8,128)(2,1)S(1)} %bitcast.10, bf16[3456,256]{1,0:T(8,128)(2,1)S(1)} %copy-done.3), custom_call_target="tpu_custom_call" | custom-call | flops 5435817984 | bytes 1769472 | tf_op jit(solution)/shard_map/pallas_call | solution.py:421
  8.8 1.3 %collective-permute-start = (bf16[2,384,128]{2,1,0:T(8,128)(2,1)S(1)}, bf16[2,384,128]{2,1,0:T(8,128)(2,1)S(1)}, u32[]{:S(2)}, u32[]{:S(2)}) collective-permute-start(bf16[2,384,128]{2,1,0:T(8,128)(2,1)S(1)} %get-tuple-element.39), channel_id=1, source_target_pairs={{1,0},{3,2},{5,4},{7,6},{9,8},{11,10},{13,12},{15,14},{17,16},{19,... | collective-permute-start | bytes 589832 | tf_op jit(solution)/shard_map/ppermute | solution.py:339
  10.1 0.0 collective-permute-done.1.parcel_ref
  10.1 0.0 copy-done.4
  10.1 0.0 copy-done.5
  10.1 4.2 %shard_map.95 = (bf16[3,6,6,96,128]{4,3,2,1,0:T(8,128)(2,1)S(1)}, f32[2,8,224,128]{3,2,1,0:T(8,128)S(1)}, bf16[2,8,224,128]{3,2,1,0:T(8,128)(2,1)S(1)}) custom-call(bf16[4,4,96,128]{3,2,1,0:T(8,128)(2,1)S(1)} %bitcast.14, bf16[784,128]{1,0:T(8,128)(2,1)S(1)} %collective-permute-done.1.parcel_ref, f32[8,128]{1,0:T(8,128)S(1)} %get-tuple-element.43.stats_ref, ...), custom_call_target="tpu_custom_call" | custom-call | flops 2717908992 | bytes 786432 | tf_op jit(solution)/shard_map/pallas_call | solution.py:445
  14.3 2.7 %collective-permute-done.after_ref = bf16[2,384,128]{2,1,0:T(8,128)(2,1)S(1)} collective-permute-done((bf16[2,384,128]{2,1,0:T(8,128)(2,1)S(1)}, bf16[2,384,128]{2,1,0:T(8,128)(2,1)S(1)}, u32[]{:S(2)}, u32[]{:S(2)}) %collective-permute-start) | collective-permute-done | bytes 196640 | tf_op jit(solution)/shard_map/ppermute | solution.py:339
  17.0 0.0 collective-permute-start.2
  17.0 0.7 %shard_map.96 = (f32[4,384,128]{2,1,0:T(8,128)S(1)}, f32[8,128]{1,0:T(8,128)S(1)}) custom-call(f32[4,384,128]{2,1,0:T(8,128)S(1)} %get-tuple-element.48.part_ref, bf16[2,384,128]{2,1,0:T(8,128)(2,1)S(1)} %collective-permute-done.after_ref, bf16[4,4,96,128]{3,2,1,0:T(8,128)(2,1)S(1)} %bitcast.15, bf16[784,128]{1,0:T(8,128)(2,1)S(1)} %collective-permute-done.1.parcel_ref, ...), custom_call_target="tpu_custom_call" | custom-call | flops 2717908992 | bytes 1769472 | tf_op jit(solution)/shard_map/pallas_call | solution.py:453
  17.8 0.0 copy-start.2
  17.8 1.7 %collective-permute-done.2 = bf16[2,8,224,128]{3,2,1,0:T(8,128)(2,1)S(1)} collective-permute-done((bf16[2,8,224,128]{3,2,1,0:T(8,128)(2,1)S(1)}, bf16[2,8,224,128]{3,2,1,0:T(8,128)(2,1)S(1)}, u32[]{:S(2)}, u32[]{:S(2)}) %collective-permute-start.2) | collective-permute-done | bytes 917536 | tf_op jit(solution)/shard_map/ppermute | solution.py:357
  19.5 0.2 shard_map.97
  19.7 0.1 collective-permute-start.6
  19.8 3.1 %collective-permute-start.3 = (bf16[4,224,128]{2,1,0:T(8,128)(2,1)S(1)}, bf16[4,224,128]{2,1,0:T(8,128)(2,1)S(1)}, u32[]{:S(2)}, u32[]{:S(2)}) collective-permute-start(bf16[4,224,128]{2,1,0:T(8,128)(2,1)S(1)} %get-tuple-element.53), channel_id=1, source_target_pairs={{0,5},{1,4},{2,7},{3,6},{4,1},{5,0},{6,3},{7,2},{8,13},{9,12},{10,... | collective-permute-start | bytes 688136 | tf_op jit(solution)/shard_map/ppermute | solution.py:357
  22.9 0.4 collective-permute-start.4
  23.2 0.2 collective-permute-start.5
  23.4 0.0 copy-done.2
  23.4 4.1 %shard_map.98 = bf16[4,4,96,256]{3,2,1,0:T(8,128)(2,1)} custom-call(bf16[3,6,6,96,128]{4,3,2,1,0:T(8,128)(2,1)S(1)} %get-tuple-element.58.padded, bf16[4,4,96,128]{3,2,1,0:T(8,128)(2,1)S(1)} %bitcast.16, bf16[3456,256]{1,0:T(8,128)(2,1)S(1)} %copy-done.3, bf16[128,256]{1,0:T(8,128)(2,1)S(1)} %copy-done.2), custom_call_target="tpu_custom_call" | custom-call | flops 2717908992 | bytes 1769472 | tf_op jit(solution)/shard_map/pallas_call | solution.py:468
  27.5 0.0 collective-permute-done.6.sums_b
  27.5 1.8 %collective-permute-done.3.xy_ref = bf16[4,224,128]{2,1,0:T(8,128)(2,1)S(1)} collective-permute-done((bf16[4,224,128]{2,1,0:T(8,128)(2,1)S(1)}, bf16[4,224,128]{2,1,0:T(8,128)(2,1)S(1)}, u32[]{:S(2)}, u32[]{:S(2)}) %collective-permute-start.3) | collective-permute-done | bytes 229408 | tf_op jit(solution)/shard_map/ppermute | solution.py:357
  29.3 4.2 %collective-permute-done.4.x_ref = bf16[4,224,128]{2,1,0:T(8,128)(2,1)S(1)} collective-permute-done((bf16[4,224,128]{2,1,0:T(8,128)(2,1)S(1)}, bf16[4,224,128]{2,1,0:T(8,128)(2,1)S(1)}, u32[]{:S(2)}, u32[]{:S(2)}) %collective-permute-start.4) | collective-permute-done | bytes 229408 | tf_op jit(solution)/shard_map/ppermute | solution.py:357
  33.5 0.0 collective-permute-done.5.y_ref
  33.5 0.1 shard_map.99
  33.7 3.8 %collective-permute-start.7 = (bf16[224,128]{1,0:T(8,128)(2,1)S(1)}, bf16[224,128]{1,0:T(8,128)(2,1)S(1)}, u32[]{:S(2)}, u32[]{:S(2)}) collective-permute-start(bf16[224,128]{1,0:T(8,128)(2,1)S(1)} %get-tuple-element.69), channel_id=1, source_target_pairs={{0,24},{1,25},{2,26},{3,27},{4,28},{5,29},{6,30},{7,31},{8,16},{9,... | collective-permute-start | bytes 172040 | tf_op jit(solution)/shard_map/ppermute | solution.py:357
  37.5 0.0 collective-permute-start.8
  37.5 0.6 %collective-permute-start.9 = (bf16[224,128]{1,0:T(8,128)(2,1)S(1)}, bf16[224,128]{1,0:T(8,128)(2,1)S(1)}, u32[]{:S(2)}, u32[]{:S(2)}) collective-permute-start(bf16[224,128]{1,0:T(8,128)(2,1)S(1)} %get-tuple-element.71), channel_id=1, source_target_pairs={{0,8},{1,9},{2,10},{3,11},{4,12},{5,13},{6,14},{7,15},{8,0},{9,1},... | collective-permute-start | bytes 172040 | tf_op jit(solution)/shard_map/ppermute | solution.py:357
  38.1 1.1 %shard_map.100 = bf16[4,4,96,128]{3,2,1,0:T(8,128)(2,1)} custom-call(f32[4,384,128]{2,1,0:T(8,128)S(1)} %get-tuple-element.67.grad_ref, f32[8,128]{1,0:T(8,128)S(1)} %get-tuple-element.59.sums_a, f32[8,128]{1,0:T(8,128)S(1)} %collective-permute-done.6.sums_b, bf16[4,4,96,128]{3,2,1,0:T(8,128)(2,1)S(1)} %bitcast.17, ...), custom_call_target="tpu_custom_call" | custom-call | flops 135895456 | bytes 1572864 | tf_op jit(solution)/shard_map/pallas_call | solution.py:487
  39.3 0.8 %collective-permute-done.7.a_ref = bf16[224,128]{1,0:T(8,128)(2,1)S(1)} collective-permute-done((bf16[224,128]{1,0:T(8,128)(2,1)S(1)}, bf16[224,128]{1,0:T(8,128)(2,1)S(1)}, u32[]{:S(2)}, u32[]{:S(2)}) %collective-permute-start.7) | collective-permute-done | bytes 57376 | tf_op jit(solution)/shard_map/ppermute | solution.py:357
  40.1 2.5 %collective-permute-done.8.b_ref = bf16[224,128]{1,0:T(8,128)(2,1)S(1)} collective-permute-done((bf16[224,128]{1,0:T(8,128)(2,1)S(1)}, bf16[224,128]{1,0:T(8,128)(2,1)S(1)}, u32[]{:S(2)}, u32[]{:S(2)}) %collective-permute-start.8) | collective-permute-done | bytes 57376 | tf_op jit(solution)/shard_map/ppermute | solution.py:357
  42.6 0.0 collective-permute-done.9.c_ref
  42.6 0.7 %shard_map.101 = (f32[216,128]{1,0:T(8,128)}, f32[8,128]{1,0:T(8,128)}) custom-call(f32[224,128]{1,0:T(8,128)S(1)} %get-tuple-element.66.own_ref, bf16[224,128]{1,0:T(8,128)(2,1)S(1)} %collective-permute-done.7.a_ref, bf16[224,128]{1,0:T(8,128)(2,1)S(1)} %collective-permute-done.8.b_ref, bf16[224,128]{1,0:T(8,128)(2,1)S(1)} %collective-permute-done.9.c_ref), custom_call_target="tpu_custom_call" | custom-call | bytes 344064 | tf_op jit(solution)/shard_map/pallas_call | solution.py:382
Async XLA Ops:
  0.6 1.0 %copy-start.1 = (bf16[1,4,4,96,128]{4,3,2,1,0:T(8,128)(2,1)S(1)}, bf16[1,4,4,96,128]{4,3,2,1,0:T(8,128)(2,1)}, u32[]{:S(2)}) copy-start(bf16[1,4,4,96,128]{4,3,2,1,0:T(8,128)(2,1)} %param.6) | copy-start | bytes 1179652
  1.6 3.3 %copy-start = (bf16[1,4,4,96,256]{4,3,2,1,0:T(8,128)(2,1)S(1)}, bf16[1,4,4,96,256]{4,3,2,1,0:T(8,128)(2,1)}, u32[]{:S(2)}) copy-start(bf16[1,4,4,96,256]{4,3,2,1,0:T(8,128)(2,1)} %param.11) | copy-start | bytes 2359300
  1.6 3.3 %copy-start.3 = (bf16[3456,256]{1,0:T(8,128)(2,1)S(1)}, bf16[3456,256]{1,0:T(8,128)(2,1)}, u32[]{:S(2)}) copy-start(bf16[3456,256]{1,0:T(8,128)(2,1)} %weight_ref.3) | copy-start | bytes 5308420
  1.9 8.2 %collective-permute-start.1 = (bf16[784,128]{1,0:T(8,128)(2,1)S(1)}, bf16[784,128]{1,0:T(8,128)(2,1)S(1)}, u32[]{:S(2)}, u32[]{:S(2)}) collective-permute-start(bf16[784,128]{1,0:T(8,128)(2,1)S(1)} %get-tuple-element.40), channel_id=1, source_target_pairs={{0,1},{1,0},{2,3},{3,2},{4,5},{5,4},{6,7},{7,6},{8,9},{9,8},{10,11... | collective-permute-start | bytes 602120 | tf_op jit(solution)/shard_map/ppermute | solution.py:416
  4.9 5.2 %copy-start.4 = (f32[128]{0:T(128)S(1)}, f32[128]{0:T(128)}, u32[]{:S(2)}) copy-start(f32[128]{0:T(128)} %param.7) | copy-start | bytes 1540
  4.9 5.2 %copy-start.5 = (f32[128]{0:T(128)S(1)}, f32[128]{0:T(128)}, u32[]{:S(2)}) copy-start(f32[128]{0:T(128)} %param.8) | copy-start | bytes 1540
  8.8 8.3 %collective-permute-start = (bf16[2,384,128]{2,1,0:T(8,128)(2,1)S(1)}, bf16[2,384,128]{2,1,0:T(8,128)(2,1)S(1)}, u32[]{:S(2)}, u32[]{:S(2)}) collective-permute-start(bf16[2,384,128]{2,1,0:T(8,128)(2,1)S(1)} %get-tuple-element.39), channel_id=1, source_target_pairs={{1,0},{3,2},{5,4},{7,6},{9,8},{11,10},{13,12},{15,14},{17,16},{19,... | collective-permute-start | bytes 589832 | tf_op jit(solution)/shard_map/ppermute | solution.py:339
  17.0 2.5 %collective-permute-start.2 = (bf16[2,8,224,128]{3,2,1,0:T(8,128)(2,1)S(1)}, bf16[2,8,224,128]{3,2,1,0:T(8,128)(2,1)S(1)}, u32[]{:S(2)}, u32[]{:S(2)}) collective-permute-start(bf16[2,8,224,128]{3,2,1,0:T(8,128)(2,1)S(1)} %get-tuple-element.47), channel_id=1, source_target_pairs={{0,2},{1,3},{2,0},{3,1},{4,6},{5,7},{6,4},{7,5},{8,10},{9,11},{10,... | collective-permute-start | bytes 2752520 | tf_op jit(solution)/shard_map/ppermute | solution.py:357
  17.8 5.7 %copy-start.2 = (bf16[128,256]{1,0:T(8,128)(2,1)S(1)}, bf16[128,256]{1,0:T(8,128)(2,1)}, u32[]{:S(2)}) copy-start(bf16[128,256]{1,0:T(8,128)(2,1)} %short_ref.3) | copy-start | bytes 196612
  19.7 7.8 %collective-permute-start.6 = (f32[8,128]{1,0:T(8,128)S(1)}, f32[8,128]{1,0:T(8,128)S(1)}, u32[]{:S(2)}, u32[]{:S(2)}) collective-permute-start(f32[8,128]{1,0:T(8,128)S(1)} %get-tuple-element.59.sums_a), channel_id=1, source_target_pairs={{0,1},{1,0},{2,3},{3,2},{4,5},{5,4},{6,7},{7,6},{8,9},{9,8},{10,11... | collective-permute-start | bytes 12296 | tf_op jit(solution)/shard_map/ppermute | solution.py:346
  19.8 9.6 %collective-permute-start.3 = (bf16[4,224,128]{2,1,0:T(8,128)(2,1)S(1)}, bf16[4,224,128]{2,1,0:T(8,128)(2,1)S(1)}, u32[]{:S(2)}, u32[]{:S(2)}) collective-permute-start(bf16[4,224,128]{2,1,0:T(8,128)(2,1)S(1)} %get-tuple-element.53), channel_id=1, source_target_pairs={{0,5},{1,4},{2,7},{3,6},{4,1},{5,0},{6,3},{7,2},{8,13},{9,12},{10,... | collective-permute-start | bytes 688136 | tf_op jit(solution)/shard_map/ppermute | solution.py:357
  22.9 10.7 %collective-permute-start.4 = (bf16[4,224,128]{2,1,0:T(8,128)(2,1)S(1)}, bf16[4,224,128]{2,1,0:T(8,128)(2,1)S(1)}, u32[]{:S(2)}, u32[]{:S(2)}) collective-permute-start(bf16[4,224,128]{2,1,0:T(8,128)(2,1)S(1)} %get-tuple-element.54), channel_id=1, source_target_pairs={{0,4},{1,5},{2,6},{3,7},{4,0},{5,1},{6,2},{7,3},{8,12},{9,13},{10,... | collective-permute-start | bytes 688136 | tf_op jit(solution)/shard_map/ppermute | solution.py:357
  23.2 10.3 %collective-permute-start.5 = (bf16[4,224,128]{2,1,0:T(8,128)(2,1)S(1)}, bf16[4,224,128]{2,1,0:T(8,128)(2,1)S(1)}, u32[]{:S(2)}, u32[]{:S(2)}) collective-permute-start(bf16[4,224,128]{2,1,0:T(8,128)(2,1)S(1)} %get-tuple-element.55), channel_id=1, source_target_pairs={{0,1},{1,0},{2,3},{3,2},{4,5},{5,4},{6,7},{7,6},{8,9},{9,8},{10,11... | collective-permute-start | bytes 688136 | tf_op jit(solution)/shard_map/ppermute | solution.py:357
  33.7 6.4 %collective-permute-start.7 = (bf16[224,128]{1,0:T(8,128)(2,1)S(1)}, bf16[224,128]{1,0:T(8,128)(2,1)S(1)}, u32[]{:S(2)}, u32[]{:S(2)}) collective-permute-start(bf16[224,128]{1,0:T(8,128)(2,1)S(1)} %get-tuple-element.69), channel_id=1, source_target_pairs={{0,24},{1,25},{2,26},{3,27},{4,28},{5,29},{6,30},{7,31},{8,16},{9,... | collective-permute-start | bytes 172040 | tf_op jit(solution)/shard_map/ppermute | solution.py:357
  37.5 5.1 %collective-permute-start.8 = (bf16[224,128]{1,0:T(8,128)(2,1)S(1)}, bf16[224,128]{1,0:T(8,128)(2,1)S(1)}, u32[]{:S(2)}, u32[]{:S(2)}) collective-permute-start(bf16[224,128]{1,0:T(8,128)(2,1)S(1)} %get-tuple-element.70), channel_id=1, source_target_pairs={{0,16},{1,17},{2,18},{3,19},{4,20},{5,21},{6,22},{7,23},{8,24},{9,... | collective-permute-start | bytes 172040 | tf_op jit(solution)/shard_map/ppermute | solution.py:357
  37.5 5.1 %collective-permute-start.9 = (bf16[224,128]{1,0:T(8,128)(2,1)S(1)}, bf16[224,128]{1,0:T(8,128)(2,1)S(1)}, u32[]{:S(2)}, u32[]{:S(2)}) collective-permute-start(bf16[224,128]{1,0:T(8,128)(2,1)S(1)} %get-tuple-element.71), channel_id=1, source_target_pairs={{0,8},{1,9},{2,10},{3,11},{4,12},{5,13},{6,14},{7,15},{8,0},{9,1},... | collective-permute-start | bytes 172040 | tf_op jit(solution)/shard_map/ppermute | solution.py:357

commit v3 on v2

--- a/solution.py
+++ b/solution.py
@@ -81,9 +81,13 @@
     parcel_ref[lead * places :] = pieces_block(totals)
 
 
+def whole(parcel):
+    pieces = parcel[parcel.shape[0] - 16 :].astype(f32)
+    return pieces[0:2] + (pieces[2:4] + pieces[4:6])
+
+
 def moments(stats, parcel, members):
-    pieces = parcel[parcel.shape[0] - 16 :].astype(f32)
-    totals = stats[0:2] + (pieces[0:2] + (pieces[2:4] + pieces[4:6]))
+    totals = stats[0:2] + whole(parcel)
     mean = totals[0:1] / members
     variance = totals[1:2] / members - mean * mean
     return mean, lax.rsqrt(variance + epsilon)
@@ -139,17 +143,15 @@
 
 def weight_kernel(
     members, split,
-    clip_ref, parcel_ref, stats_ref, gain_ref, bias_ref, cot_ref,
-    padded, *rest,
+    clip_ref, parcel_ref, stats_ref, gain_ref, bias_ref, cot_t_ref,
+    padded, total, *rest,
 ):
     frames, rows, cols, width = clip_ref.shape
-    out_width = cot_ref.shape[-1]
     mean, inv = moments(stats_ref, parcel_ref, members)
     fill_hidden(padded, clip_ref, parcel_ref, mean, inv, gain_ref[...], bias_ref[...])
-    cot_t = cot_ref[...].reshape(-1, out_width).T
+    cot_t = cot_t_ref[...]
     pieces = [(t, i) for t in range(KT) for i in range(KS)]
     begin = 0
-    total = rest[-1]
     for at in range(0, len(pieces), 2):
         parts = []
         for t, i in pieces[at : at + 2]:
@@ -158,17 +160,16 @@
             parts.append(clip_ref[...].reshape(-1, width))
         part = jnp.dot(cot_t, jnp.concatenate(parts, axis=1), preferred_element_type=f32).T
         if split is None:
-            rest[0][begin : begin + part.shape[0], :] = part
+            total[begin : begin + part.shape[0], :] = part
         else:
             scatter_rows(total, part, begin, split)
         begin += part.shape[0]
     if split is not None:
-        own_ref, send_ref = rest[:-1]
+        (send_ref,) = rest
         core = lax.rem(lax.axis_index("dp"), 2)
-        halves, blocks = total.shape[0], total.shape[1] // 2
+        halves, blocks = send_ref.shape[:2]
         for half in range(halves):
             for k in range(blocks):
-                own_ref[half, k] = total[half, 2 * k + core]
                 send_ref[half, k] = total[half, 2 * k + 1 - core].astype(bf16)
 
 
@@ -239,10 +240,11 @@
     return lax.dot_general(block, weights, (((1,), (1,)), ((), ())), preferred_element_type=f32)
 
 
-def back_kernel(cot_ref, weight_ref, out_ref, before_ref, padded):
+def back_kernel(cot_ref, weight_ref, out_ref, before_ref, cot_t_ref, padded):
     frames, rows, cols, out_width = cot_ref.shape
     width = out_ref.shape[-1]
     at_start = lax.axis_index("ctx") == 0
+    cot_t_ref[...] = cot_ref[...].reshape(-1, out_width).T
     fill_cot(padded, cot_ref)
     late = back_weights(weight_ref, width, (2, 1))
     early = back_weights(weight_ref, width, (0,))
@@ -268,53 +270,80 @@
 
 def activation_kernel(
     members,
-    part_ref, after_ref, clip_ref, parcel_ref, stats_ref, gain_ref, bias_ref,
-    grad_ref, sums_ref,
+    part_ref, leading_ref, clip_ref, parcel_ref, stats_ref, gain_ref, bias_ref,
+    grad_ref, slope_ref, sums_ref, out_ref,
 ):
     frames, rows, cols, width = clip_ref.shape
+    places = rows * cols
+    gain = gain_ref[...]
     mean, inv = moments(stats_ref, parcel_ref, members)
+
+    def standard_and_slope(value):
+        standard = (value.astype(f32) - mean) * inv
+        affine = standard * gain + bias_ref[...]
+        logistic = jax.nn.sigmoid(affine)
+        return standard, logistic * (1.0 + affine * (1.0 - logistic)) * gain
+
     total = jnp.zeros((1, width), f32)
     cross = jnp.zeros((1, width), f32)
-    ahead = after_ref.shape[0]
-    for frame in range(frames):
-        grad = part_ref[frame]
-        if frame >= frames - ahead:
-            grad = grad + after_ref[frame - (frames - ahead)].astype(f32)
-        standard = (clip_ref[frame].reshape(-1, width).astype(f32) - mean) * inv
-        affine = standard * gain_ref[...] + bias_ref[...]
-        logistic = jax.nn.sigmoid(affine)
-        grad = grad * logistic * (1.0 + affine * (1.0 - logistic)) * gain_ref[...]
-        grad_ref[frame] = grad
+    lead = leading_ref.shape[0]
+    for frame in range(lead):
+        here = slice(frame * places, (frame + 1) * places)
+        standard, slope = standard_and_slope(parcel_ref[here])
+        grad = leading_ref[frame].astype(f32) * slope
         total = total + column_totals(grad)
         cross = cross + column_totals(grad * standard)
-    sums_ref[...] = group_totals(two_rows(total, cross))
+        out_ref[here] = leading_ref[frame]
+    at_start = lax.axis_index("ctx") == 0
+    total = jnp.where(at_start, 0.0, total)
+    cross = jnp.where(at_start, 0.0, cross)
+    for frame in range(frames):
+        standard, slope = standard_and_slope(clip_ref[frame].reshape(-1, width))
+        grad = part_ref[frame] * slope
+        grad_ref[frame] = grad
+        if frame >= frames - lead:
+            slope_ref[frame - (frames - lead)] = slope
+        total = total + column_totals(grad)
+        cross = cross + column_totals(grad * standard)
+    sums = group_totals(two_rows(total, cross))
+    sums_ref[...] = sums
+    out_ref[lead * places :] = pieces_block(sums)
 
 
 def finish_kernel(
     members,
-    grad_ref, sums_a, sums_b, clip_ref, parcel_ref, stats_ref, cot_ref, short_ref,
+    grad_ref, slope_ref, sums_ref, after_ref, clip_ref, parcel_ref, stats_ref, cot_ref, short_ref,
     out_ref,
 ):
     frames, rows, cols, width = clip_ref.shape
+    places = rows * cols
     out_width = cot_ref.shape[-1]
+    lead = slope_ref.shape[0]
+    is_last = lax.axis_index("ctx") == lax.axis_size("ctx") - 1
     mean, inv = moments(stats_ref, parcel_ref, members)
-    sums = sums_a[...] + sums_b[...]
+    sums = sums_ref[0:2] + whole(after_ref)
     mean_grad = sums[0:1] / members
     mean_cross = sums[1:2] / members
     for frame in range(frames):
         standard = (clip_ref[frame].reshape(-1, width).astype(f32) - mean) * inv
         shortcut = back_dot(cot_ref[frame].reshape(-1, out_width), short_ref[...])
-        grad = (grad_ref[frame] - mean_grad - standard * mean_cross) * inv + shortcut
+        grad = grad_ref[frame]
+        at = frame - (frames - lead)
+        if at >= 0:
+            following = after_ref[at * places : (at + 1) * places].astype(f32) * slope_ref[at]
+            grad = grad + jnp.where(is_last, 0.0, following)
+        grad = (grad - mean_grad - standard * mean_cross) * inv + shortcut
         out_ref[frame] = grad.astype(bf16).reshape(rows, cols, width)
 
 
 def plane_kernel(own_ref, got_ref, keep_ref, x_ref, y_ref, xy_ref):
-    halves, deep, wide = own_ref.shape[:3]
+    deep = got_ref.shape[1]
+    core = lax.rem(lax.axis_index("dp"), 2)
     x = lax.rem(lax.axis_index("dp") // 2, 2)
     y = lax.axis_index("ctx")
     for z in range(deep):
         for half, col, target in ((y, x, keep_ref), (y, 1 - x, x_ref), (1 - y, x, y_ref), (1 - y, 1 - x, xy_ref)):
-            value = own_ref[half, z, col] + got_ref[half, z, col].astype(f32)
+            value = own_ref[half, z, col, core] + got_ref[half, z, col].astype(f32)
             target[z] = value.astype(target.dtype)
 
 
@@ -357,15 +386,13 @@
     return lax.ppermute(value, ("dp", "ctx"), pairs)
 
 
-def sort_plane(own, got):
-    halves, blocks, rows, cols = own.shape
-    shape = (halves, blocks // 2, 2, rows, cols)
+def sort_plane(total, got):
+    halves, blocks, rows, cols = got.shape
     part = (blocks // 2, rows, cols)
     return call(
         plane_kernel,
         [jax.ShapeDtypeStruct(part, f32)] + [jax.ShapeDtypeStruct(part, bf16)] * 3,
-        moved=own.size * 8,
-    )(own.reshape(shape), got.reshape(shape))
+    )(total.reshape(halves, blocks // 2, 2, 2, rows, cols), got.reshape(halves, blocks // 2, 2, rows, cols))
 
 
 def sort_line(keep, *planes):
@@ -418,64 +445,68 @@
         before = from_behind(clip[frames - lead :], "ctx", 1).reshape(-1, in_width)
         before = jnp.concatenate([before, pieces_block(others_total(stats))], axis=0)
 
-    back_part, leading = call(
+    back_part, leading, cot_t = call(
         back_kernel,
         [
             jax.ShapeDtypeStruct((frames, height * breadth, in_width), f32),
             jax.ShapeDtypeStruct((lead, height * breadth, in_width), bf16),
+            jax.ShapeDtypeStruct((out_width, places), bf16),
         ],
         [pltpu.VMEM((KS, frames, height + 2, breadth, out_width), bf16)],
         flops=2 * work, moved=conv_weight.size * 2,
     )(cot, conv_weight)
     before, back_part = lax.optimization_barrier((before, back_part))
-    after = from_behind(leading, "ctx", -1)
 
     staged = dp_size == 16 and ctx_size == 2
     conv_rows, short_rows = conv_all // dp_size, in_width // dp_size
     if staged:
         cols = out_width // ctx_size
-        blocks = (ctx_size, dp_size // 2, conv_rows + short_rows, cols)
-        outs = [jax.ShapeDtypeStruct(blocks, f32), jax.ShapeDtypeStruct(blocks, bf16)]
-        scratch = [pltpu.VMEM((ctx_size, dp_size, conv_rows + short_rows, cols), f32)]
+        block = (conv_rows + short_rows, cols)
+        outs = [
+            jax.ShapeDtypeStruct((ctx_size, dp_size) + block, f32),
+            jax.ShapeDtypeStruct((ctx_size, dp_size // 2) + block, bf16),
+        ]
         split = (conv_rows, short_rows, conv_all)
     else:
         outs = [jax.ShapeDtypeStruct((conv_all + in_width, out_width), f32)]
-        scratch = []
         split = None
     hidden, *parts = call(
         functools.partial(weight_kernel, members, split),
-        [jax.ShapeDtypeStruct((KS, frames + KT - 1, height + 2, breadth, in_width), bf16)] + outs,
-        scratch,
+        [jax.ShapeDtypeStruct((KS, frames + lead, height + 2, breadth, in_width), bf16)] + outs,
         flops=work, moved=cot.size * 2,
-    )(clip, before, stats, gain, bias, cot)
-
-    after, *parts = lax.optimization_barrier((after, *parts))
-    grad, sums = call(
+    )(clip, before, stats, gain, bias, cot_t)
+
+    if staged:
+        keep, to_x, to_y, to_xy = sort_plane(parts[0], swap(parts[1], 1))
+        planes = (swap(to_xy, 2, 1), swap(to_x, 2), swap(to_y, 0, 1))
+        hidden, keep = lax.optimization_barrier((hidden, keep))
+    clip_out = call(
+        forward_kernel,
+        jax.ShapeDtypeStruct((frames, height, breadth, out_width), bf16),
+        flops=work // 4,
+    )(hidden, clip, conv_weight, short_weight)
+    leading, clip_out = lax.optimization_barrier((leading, clip_out))
+    parcel_shape = jax.ShapeDtypeStruct((lead * height * breadth + 16, in_width), bf16)
+    grad, slope, sums, parcel = call(
         functools.partial(activation_kernel, members),
         [
             jax.ShapeDtypeStruct((frames, height * breadth, in_width), f32),
+            jax.ShapeDtypeStruct((lead, height * breadth, in_width), f32),
             jax.ShapeDtypeStruct((8, in_width), f32),
+            parcel_shape,
         ],
-        flops=work, moved=conv_weight.size * 2,
-    )(back_part, after, clip, before, stats, gain, bias)
+    )(back_part, leading, clip, before, stats, gain, bias)
+    if ctx_size == 2:
+        after = lax.ppermute(parcel, "ctx", [(0, 1), (1, 0)])
+    else:
+        after = from_behind(leading, "ctx", -1).reshape(-1, in_width)
+        after = jnp.concatenate([after, pieces_block(others_total(sums))], axis=0)
     if staged:
-        own, got, sums = lax.optimization_barrier((parts[0], swap(parts[1], 1), sums))
-        keep, to_x, to_y, to_xy = sort_plane(own, got)
-        from_xy, from_x, from_y = swap(to_xy, 2, 1), swap(to_x, 2), swap(to_y, 0, 1)
-        planes = (from_xy, from_x, from_y)
-        hidden, keep = lax.optimization_barrier((hidden, keep))
-    other_sums = others_total(sums)
-    clip_out = call(
-        forward_kernel,
-        jax.ShapeDtypeStruct((frames, height, breadth, out_width), bf16),
-        flops=work, moved=conv_weight.size * 2,
-    )(hidden, clip, conv_weight, short_weight)
-    if staged:
-        *planes, clip_out, other_sums = lax.optimization_barrier((*planes, clip_out, other_sums))
+        *planes, sums = lax.optimization_barrier((*planes, sums))
         mine, *lines = sort_line(keep, *planes)
         lines = (swap(lines[2], 12), swap(lines[1], 8), swap(lines[0], 4))
         conv_grad, short_grad = add_line(mine, *lines, conv_rows, short_rows, scale)
-        grad, mine = lax.optimization_barrier((grad, mine))
+        after, mine = lax.optimization_barrier((after, mine))
     else:
         summed = []
         for part in (parts[0][:conv_all], parts[0][conv_all:]):
@@ -483,12 +514,11 @@
             part = lax.psum_scatter(part, "ctx", scatter_dimension=1, tiled=True)
             summed.append(part * scale)
         conv_grad, short_grad = summed
-
     clip_grad = call(
         functools.partial(finish_kernel, members),
         jax.ShapeDtypeStruct((frames, height, breadth, in_width), bf16),
         flops=work // 20, moved=cot.size * 4,
-    )(grad, sums, other_sums, clip, before, stats, cot, short_weight)
+    )(grad, slope, sums, after, clip, before, stats, cot, short_weight)
     return (clip_out[None], clip_grad[None], conv_grad, short_grad)
 
 

time: 43.4 us -> 39.8 us (0.917)
  waiting for transfers between devices: 13.8 us -> 10.2 us
    ppermute x2 -> x1, waiting for transfers between devices: 2.72 us -> 0.01 us  [body(): after = lax.ppermute(parcel, 'ctx', [(0, 1), (1, 0)])]
    ppermute x7, waiting for transfers between devices: 11.1 us -> 9.08 us  [swap(): return lax.ppermute(value, ('dp', 'ctx'), pairs)]
    ppermute x1, waiting for transfers between devices: 0.01 us -> 1.1 us  [body(): before = lax.ppermute(parcel, 'ctx', [(0, 1), (1, 0)])]
    pallas_call x1, Pallas kernels: 4.21 us -> 3.56 us  [body(): call(functools.partial(weight_kernel, members, split), [jax.ShapeDtypeStr...]
    ppermute x2 -> x1, starting transfers between devices: 1.37 us -> 1.76 us  [body(): after = lax.ppermute(parcel, 'ctx', [(0, 1), (1, 0)])]
    unnamed x12 -> x14, local copies, waits for them, and re-layouts: 1.01 us -> 1.02 us
  transfers between devices with their start and end apart: 10 -> 9, of which waited for: 6 -> 5; matrix products, arithmetic and copies ran while one was open for 0% -> 0% of each run, Pallas kernels for 32% -> 26%
where the time goes in v3:
time: 39.8 us; the launch traced here: 39.7 us
  Pallas kernels  15 us (38%)
  starting transfers between devices  12.8 us (32%)
  waiting for transfers between devices  10.2 us (26%)
  local copies, waits for them, and re-layouts  1.02 us (3%)
  between operations  0.7 us (2%)
    ppermute x7, waiting for transfers between devices, swap(): return lax.ppermute(value, ('dp', 'ctx'), pairs)  9.08 us
    ppermute x7, starting transfers between devices, swap(): return lax.ppermute(value, ('dp', 'ctx'), pairs)  8.08 us
    pallas_call x1, Pallas kernels, body(): call(forward_kernel, jax.ShapeDtypeStruct((frames, height, breadth, out_w...  4.06 us
    pallas_call x1, Pallas kernels, body(): call(back_kernel, [jax.ShapeDtypeStruct((frames, height * breadth, in_wid...  3.85 us
    pallas_call x1, Pallas kernels, body(): call(functools.partial(weight_kernel, members, split), [jax.ShapeDtypeStr...  3.56 us
    ppermute x1, starting transfers between devices, body(): before = lax.ppermute(parcel, 'ctx', [(0, 1), (1, 0)])  2.97 us
    ppermute x1, starting transfers between devices, body(): after = lax.ppermute(parcel, 'ctx', [(0, 1), (1, 0)])  1.76 us
    pallas_call x1, Pallas kernels, body(): call(functools.partial(finish_kernel, members), jax.ShapeDtypeStruct((fra...  1.18 us
  transfers between devices with their start and end apart: 9, of which 5 were waited for; matrix products, arithmetic and copies ran while one was open for 0% of the time, Pallas kernels for 26%

profile of v3, /device:TPU:0, one launch (start us, length us, event | category | flops | bytes accessed | tf_op | source)
XLA Modules:
  0.0 39.7 jit_solution(17057767522208028581)
XLA Ops:
  0.6 0.0 copy-start
  0.6 1.0 %copy-done = bf16[1,4,4,96,128]{4,3,2,1,0:T(8,128)(2,1)S(1)} copy-done((bf16[1,4,4,96,128]{4,3,2,1,0:T(8,128)(2,1)S(1)}, bf16[1,4,4,96,128]{4,3,2,1,0:T(8,128)(2,1)}, u32[]{:S(2)}) %copy-start) | copy-done | bytes 393240
  1.6 0.0 copy-start.2
  1.6 0.0 copy-start.3
  1.6 0.3 shard_map.94
  1.9 3.0 %collective-permute-start = (bf16[784,128]{1,0:T(8,128)(2,1)S(1)}, bf16[784,128]{1,0:T(8,128)(2,1)S(1)}, u32[]{:S(2)}, u32[]{:S(2)}) collective-permute-start(bf16[784,128]{1,0:T(8,128)(2,1)S(1)} %get-tuple-element.38), channel_id=1, source_target_pairs={{0,1},{1,0},{2,3},{3,2},{4,5},{5,4},{6,7},{7,6},{8,9},{9,8},{10,11... | collective-permute-start | bytes 602120 | tf_op jit(solution)/shard_map/ppermute | solution.py:443
  4.9 0.0 copy-done.2
  4.9 0.0 copy-done.3
  4.9 0.0 copy-start.1
  4.9 0.0 copy-start.5
  4.9 0.0 copy-start.6
  4.9 3.9 %shard_map.93 = (f32[4,384,128]{2,1,0:T(8,128)S(1)}, bf16[2,384,128]{2,1,0:T(8,128)(2,1)S(1)}, bf16[256,1536]{1,0:T(8,128)(2,1)S(1)}) custom-call(bf16[4,4,96,256]{3,2,1,0:T(8,128)(2,1)S(1)} %bitcast.15, bf16[3456,256]{1,0:T(8,128)(2,1)S(1)} %copy-done.2), custom_call_target="tpu_custom_call" | custom-call | flops 5435817984 | bytes 1769472 | tf_op jit(solution)/shard_map/pallas_call | solution.py:448
  8.8 1.1 %collective-permute-done.parcel_ref = bf16[784,128]{1,0:T(8,128)(2,1)S(1)} collective-permute-done((bf16[784,128]{1,0:T(8,128)(2,1)S(1)}, bf16[784,128]{1,0:T(8,128)(2,1)S(1)}, u32[]{:S(2)}, u32[]{:S(2)}) %collective-permute-start) | collective-permute-done | bytes 200736 | tf_op jit(solution)/shard_map/ppermute | solution.py:443
  9.9 0.0 copy-done.1
  9.9 0.0 copy-done.5
  9.9 0.0 copy-done.6
  9.9 3.6 %shard_map.95 = (bf16[3,6,6,96,128]{4,3,2,1,0:T(8,128)(2,1)S(1)}, f32[2,16,224,128]{3,2,1,0:T(8,128)S(1)}, bf16[2,8,224,128]{3,2,1,0:T(8,128)(2,1)S(1)}) custom-call(bf16[4,4,96,128]{3,2,1,0:T(8,128)(2,1)S(1)} %bitcast.10, bf16[784,128]{1,0:T(8,128)(2,1)S(1)} %collective-permute-done.parcel_ref, f32[8,128]{1,0:T(8,128)S(1)} %get-tuple-element.41.stats_ref, ...), custom_call_target="tpu_custom_call" | custom-call | flops 2717908992 | bytes 786432 | tf_op jit(solution)/shard_map/pallas_call | solution.py:473
  13.5 0.0 copy-start.4
  13.5 0.1 collective-permute-start.1
  13.6 2.5 %collective-permute-done.1 = bf16[2,8,224,128]{3,2,1,0:T(8,128)(2,1)S(1)} collective-permute-done((bf16[2,8,224,128]{3,2,1,0:T(8,128)(2,1)S(1)}, bf16[2,8,224,128]{3,2,1,0:T(8,128)(2,1)S(1)}, u32[]{:S(2)}, u32[]{:S(2)}) %collective-permute-start.1) | collective-permute-done | bytes 917536 | tf_op jit(solution)/shard_map/ppermute | solution.py:386
  16.0 0.2 shard_map.96
  16.2 2.7 %collective-permute-start.2 = (bf16[4,224,128]{2,1,0:T(8,128)(2,1)S(1)}, bf16[4,224,128]{2,1,0:T(8,128)(2,1)S(1)}, u32[]{:S(2)}, u32[]{:S(2)}) collective-permute-start(bf16[4,224,128]{2,1,0:T(8,128)(2,1)S(1)} %get-tuple-element.53), channel_id=1, source_target_pairs={{0,5},{1,4},{2,7},{3,6},{4,1},{5,0},{6,3},{7,2},{8,13},{9,12},{10,... | collective-permute-start | bytes 688136 | tf_op jit(solution)/shard_map/ppermute | solution.py:386
  18.9 0.5 %collective-permute-start.3 = (bf16[4,224,128]{2,1,0:T(8,128)(2,1)S(1)}, bf16[4,224,128]{2,1,0:T(8,128)(2,1)S(1)}, u32[]{:S(2)}, u32[]{:S(2)}) collective-permute-start(bf16[4,224,128]{2,1,0:T(8,128)(2,1)S(1)} %get-tuple-element.54), channel_id=1, source_target_pairs={{0,4},{1,5},{2,6},{3,7},{4,0},{5,1},{6,2},{7,3},{8,12},{9,13},{10,... | collective-permute-start | bytes 688136 | tf_op jit(solution)/shard_map/ppermute | solution.py:386
  19.5 0.3 collective-permute-start.4
  19.7 0.0 copy-done.4
  19.7 4.1 %shard_map.97 = bf16[4,4,96,256]{3,2,1,0:T(8,128)(2,1)} custom-call(bf16[3,6,6,96,128]{4,3,2,1,0:T(8,128)(2,1)S(1)} %get-tuple-element.47.padded, bf16[4,4,96,128]{3,2,1,0:T(8,128)(2,1)S(1)} %bitcast.11, bf16[3456,256]{1,0:T(8,128)(2,1)S(1)} %copy-done.2, bf16[128,256]{1,0:T(8,128)(2,1)S(1)} %copy-done.4), custom_call_target="tpu_custom_call" | custom-call | flops 679477248 | tf_op jit(solution)/shard_map/pallas_call | solution.py:483
  23.8 1.1 %shard_map.98 = (f32[4,384,128]{2,1,0:T(8,128)S(1)}, f32[2,384,128]{2,1,0:T(8,128)S(1)}, f32[8,128]{1,0:T(8,128)S(1)}, bf16[784,128]{1,0:T(8,128)(2,1)S(1)}) custom-call(f32[4,384,128]{2,1,0:T(8,128)S(1)} %get-tuple-element.49.part_ref, bf16[2,384,128]{2,1,0:T(8,128)(2,1)S(1)} %get-tuple-element.50.leading_ref, bf16[4,4,96,128]{3,2,1,0:T(8,128)(2,1)S(1)} %bitcast.12, ...), custom_call_target="tpu_custom_call" | custom-call | tf_op jit(solution)/shard_map/pallas_call | solution.py:490
  24.9 1.8 %collective-permute-start.5 = (bf16[784,128]{1,0:T(8,128)(2,1)S(1)}, bf16[784,128]{1,0:T(8,128)(2,1)S(1)}, u32[]{:S(2)}, u32[]{:S(2)}) collective-permute-start(bf16[784,128]{1,0:T(8,128)(2,1)S(1)} %get-tuple-element.58), channel_id=1, source_target_pairs={{0,1},{1,0},{2,3},{3,2},{4,5},{5,4},{6,7},{7,6},{8,9},{9,8},{10,11... | collective-permute-start | bytes 602120 | tf_op jit(solution)/shard_map/ppermute | solution.py:500
  26.6 0.0 collective-permute-done.2.xy_ref
  26.6 3.4 %collective-permute-done.3.x_ref = bf16[4,224,128]{2,1,0:T(8,128)(2,1)S(1)} collective-permute-done((bf16[4,224,128]{2,1,0:T(8,128)(2,1)S(1)}, bf16[4,224,128]{2,1,0:T(8,128)(2,1)S(1)}, u32[]{:S(2)}, u32[]{:S(2)}) %collective-permute-start.3) | collective-permute-done | bytes 229408 | tf_op jit(solution)/shard_map/ppermute | solution.py:386
  30.0 0.0 collective-permute-done.4.y_ref
  30.0 0.1 shard_map.99
  30.2 3.7 %collective-permute-start.6 = (bf16[224,128]{1,0:T(8,128)(2,1)S(1)}, bf16[224,128]{1,0:T(8,128)(2,1)S(1)}, u32[]{:S(2)}, u32[]{:S(2)}) collective-permute-start(bf16[224,128]{1,0:T(8,128)(2,1)S(1)} %get-tuple-element.65), channel_id=1, source_target_pairs={{0,24},{1,25},{2,26},{3,27},{4,28},{5,29},{6,30},{7,31},{8,16},{9,... | collective-permute-start | bytes 172040 | tf_op jit(solution)/shard_map/ppermute | solution.py:386
  33.8 0.0 collective-permute-start.7
  33.8 0.8 %collective-permute-start.8 = (bf16[224,128]{1,0:T(8,128)(2,1)S(1)}, bf16[224,128]{1,0:T(8,128)(2,1)S(1)}, u32[]{:S(2)}, u32[]{:S(2)}) collective-permute-start(bf16[224,128]{1,0:T(8,128)(2,1)S(1)} %get-tuple-element.67), channel_id=1, source_target_pairs={{0,8},{1,9},{2,10},{3,11},{4,12},{5,13},{6,14},{7,15},{8,0},{9,1},... | collective-permute-start | bytes 172040 | tf_op jit(solution)/shard_map/ppermute | solution.py:386
  34.6 0.0 collective-permute-done.5.after_ref
  34.6 1.2 %shard_map.100 = bf16[4,4,96,128]{3,2,1,0:T(8,128)(2,1)} custom-call(f32[4,384,128]{2,1,0:T(8,128)S(1)} %get-tuple-element.51.grad_ref, f32[2,384,128]{2,1,0:T(8,128)S(1)} %get-tuple-element.52.slope_ref, f32[8,128]{1,0:T(8,128)S(1)} %get-tuple-element.57.sums_ref, bf16[784,128]{1,0:T(8,128)(2,1)S(1)} %collective-permute-done.5.after_ref, ...), custom_call_target="tpu_custom_call" | custom-call | flops 135895456 | bytes 1572864 | tf_op jit(solution)/shard_map/pallas_call | solution.py:517
  35.8 0.8 %collective-permute-done.6.a_ref = bf16[224,128]{1,0:T(8,128)(2,1)S(1)} collective-permute-done((bf16[224,128]{1,0:T(8,128)(2,1)S(1)}, bf16[224,128]{1,0:T(8,128)(2,1)S(1)}, u32[]{:S(2)}, u32[]{:S(2)}) %collective-permute-start.6) | collective-permute-done | bytes 57376 | tf_op jit(solution)/shard_map/ppermute | solution.py:386
  36.6 2.4 %collective-permute-done.7.b_ref = bf16[224,128]{1,0:T(8,128)(2,1)S(1)} collective-permute-done((bf16[224,128]{1,0:T(8,128)(2,1)S(1)}, bf16[224,128]{1,0:T(8,128)(2,1)S(1)}, u32[]{:S(2)}, u32[]{:S(2)}) %collective-permute-start.7) | collective-permute-done | bytes 57376 | tf_op jit(solution)/shard_map/ppermute | solution.py:386
  39.0 0.0 collective-permute-done.8.c_ref
  39.0 0.7 %shard_map.101 = (f32[216,128]{1,0:T(8,128)}, f32[8,128]{1,0:T(8,128)}) custom-call(f32[224,128]{1,0:T(8,128)S(1)} %get-tuple-element.63.own_ref, bf16[224,128]{1,0:T(8,128)(2,1)S(1)} %collective-permute-done.6.a_ref, bf16[224,128]{1,0:T(8,128)(2,1)S(1)} %collective-permute-done.7.b_ref, bf16[224,128]{1,0:T(8,128)(2,1)S(1)} %collective-permute-done.8.c_ref), custom_call_target="tpu_custom_call" | custom-call | bytes 344064 | tf_op jit(solution)/shard_map/pallas_call | solution.py:409
Async XLA Ops:
  0.6 1.0 %copy-start = (bf16[1,4,4,96,128]{4,3,2,1,0:T(8,128)(2,1)S(1)}, bf16[1,4,4,96,128]{4,3,2,1,0:T(8,128)(2,1)}, u32[]{:S(2)}) copy-start(bf16[1,4,4,96,128]{4,3,2,1,0:T(8,128)(2,1)} %param.6) | copy-start | bytes 1179652
  1.6 3.3 %copy-start.2 = (bf16[3456,256]{1,0:T(8,128)(2,1)S(1)}, bf16[3456,256]{1,0:T(8,128)(2,1)}, u32[]{:S(2)}) copy-start(bf16[3456,256]{1,0:T(8,128)(2,1)} %weight_ref.3) | copy-start | bytes 5308420
  1.6 3.3 %copy-start.3 = (bf16[1,4,4,96,256]{4,3,2,1,0:T(8,128)(2,1)S(1)}, bf16[1,4,4,96,256]{4,3,2,1,0:T(8,128)(2,1)}, u32[]{:S(2)}) copy-start(bf16[1,4,4,96,256]{4,3,2,1,0:T(8,128)(2,1)} %param.11) | copy-start | bytes 2359300
  1.9 8.0 %collective-permute-start = (bf16[784,128]{1,0:T(8,128)(2,1)S(1)}, bf16[784,128]{1,0:T(8,128)(2,1)S(1)}, u32[]{:S(2)}, u32[]{:S(2)}) collective-permute-start(bf16[784,128]{1,0:T(8,128)(2,1)S(1)} %get-tuple-element.38), channel_id=1, source_target_pairs={{0,1},{1,0},{2,3},{3,2},{4,5},{5,4},{6,7},{7,6},{8,9},{9,8},{10,11... | collective-permute-start | bytes 602120 | tf_op jit(solution)/shard_map/ppermute | solution.py:443
  4.9 5.0 %copy-start.1 = (bf16[1,4,4,96,128]{4,3,2,1,0:T(8,128)(2,1)S(1)}, bf16[1,4,4,96,128]{4,3,2,1,0:T(8,128)(2,1)}, u32[]{:S(2)}) copy-start(bf16[1,4,4,96,128]{4,3,2,1,0:T(8,128)(2,1)} %param.6) | copy-start | bytes 1179652
  4.9 5.0 %copy-start.5 = (f32[128]{0:T(128)S(1)}, f32[128]{0:T(128)}, u32[]{:S(2)}) copy-start(f32[128]{0:T(128)} %param.7) | copy-start | bytes 1540
  4.9 5.0 %copy-start.6 = (f32[128]{0:T(128)S(1)}, f32[128]{0:T(128)}, u32[]{:S(2)}) copy-start(f32[128]{0:T(128)} %param.8) | copy-start | bytes 1540
  13.5 6.3 %copy-start.4 = (bf16[128,256]{1,0:T(8,128)(2,1)S(1)}, bf16[128,256]{1,0:T(8,128)(2,1)}, u32[]{:S(2)}) copy-start(bf16[128,256]{1,0:T(8,128)(2,1)} %short_ref.3) | copy-start | bytes 196612
  13.5 2.5 %collective-permute-start.1 = (bf16[2,8,224,128]{3,2,1,0:T(8,128)(2,1)S(1)}, bf16[2,8,224,128]{3,2,1,0:T(8,128)(2,1)S(1)}, u32[]{:S(2)}, u32[]{:S(2)}) collective-permute-start(bf16[2,8,224,128]{3,2,1,0:T(8,128)(2,1)S(1)} %get-tuple-element.45), channel_id=1, source_target_pairs={{0,2},{1,3},{2,0},{3,1},{4,6},{5,7},{6,4},{7,5},{8,10},{9,11},{10,... | collective-permute-start | bytes 2752520 | tf_op jit(solution)/shard_map/ppermute | solution.py:386
  16.2 10.5 %collective-permute-start.2 = (bf16[4,224,128]{2,1,0:T(8,128)(2,1)S(1)}, bf16[4,224,128]{2,1,0:T(8,128)(2,1)S(1)}, u32[]{:S(2)}, u32[]{:S(2)}) collective-permute-start(bf16[4,224,128]{2,1,0:T(8,128)(2,1)S(1)} %get-tuple-element.53), channel_id=1, source_target_pairs={{0,5},{1,4},{2,7},{3,6},{4,1},{5,0},{6,3},{7,2},{8,13},{9,12},{10,... | collective-permute-start | bytes 688136 | tf_op jit(solution)/shard_map/ppermute | solution.py:386
  18.9 11.1 %collective-permute-start.3 = (bf16[4,224,128]{2,1,0:T(8,128)(2,1)S(1)}, bf16[4,224,128]{2,1,0:T(8,128)(2,1)S(1)}, u32[]{:S(2)}, u32[]{:S(2)}) collective-permute-start(bf16[4,224,128]{2,1,0:T(8,128)(2,1)S(1)} %get-tuple-element.54), channel_id=1, source_target_pairs={{0,4},{1,5},{2,6},{3,7},{4,0},{5,1},{6,2},{7,3},{8,12},{9,13},{10,... | collective-permute-start | bytes 688136 | tf_op jit(solution)/shard_map/ppermute | solution.py:386
  19.5 10.6 %collective-permute-start.4 = (bf16[4,224,128]{2,1,0:T(8,128)(2,1)S(1)}, bf16[4,224,128]{2,1,0:T(8,128)(2,1)S(1)}, u32[]{:S(2)}, u32[]{:S(2)}) collective-permute-start(bf16[4,224,128]{2,1,0:T(8,128)(2,1)S(1)} %get-tuple-element.55), channel_id=1, source_target_pairs={{0,1},{1,0},{2,3},{3,2},{4,5},{5,4},{6,7},{7,6},{8,9},{9,8},{10,11... | collective-permute-start | bytes 688136 | tf_op jit(solution)/shard_map/ppermute | solution.py:386
  24.9 9.7 %collective-permute-start.5 = (bf16[784,128]{1,0:T(8,128)(2,1)S(1)}, bf16[784,128]{1,0:T(8,128)(2,1)S(1)}, u32[]{:S(2)}, u32[]{:S(2)}) collective-permute-start(bf16[784,128]{1,0:T(8,128)(2,1)S(1)} %get-tuple-element.58), channel_id=1, source_target_pairs={{0,1},{1,0},{2,3},{3,2},{4,5},{5,4},{6,7},{7,6},{8,9},{9,8},{10,11... | collective-permute-start | bytes 602120 | tf_op jit(solution)/shard_map/ppermute | solution.py:500
  30.2 6.5 %collective-permute-start.6 = (bf16[224,128]{1,0:T(8,128)(2,1)S(1)}, bf16[224,128]{1,0:T(8,128)(2,1)S(1)}, u32[]{:S(2)}, u32[]{:S(2)}) collective-permute-start(bf16[224,128]{1,0:T(8,128)(2,1)S(1)} %get-tuple-element.65), channel_id=1, source_target_pairs={{0,24},{1,25},{2,26},{3,27},{4,28},{5,29},{6,30},{7,31},{8,16},{9,... | collective-permute-start | bytes 172040 | tf_op jit(solution)/shard_map/ppermute | solution.py:386
  33.8 5.2 %collective-permute-start.7 = (bf16[224,128]{1,0:T(8,128)(2,1)S(1)}, bf16[224,128]{1,0:T(8,128)(2,1)S(1)}, u32[]{:S(2)}, u32[]{:S(2)}) collective-permute-start(bf16[224,128]{1,0:T(8,128)(2,1)S(1)} %get-tuple-element.66), channel_id=1, source_target_pairs={{0,16},{1,17},{2,18},{3,19},{4,20},{5,21},{6,22},{7,23},{8,24},{9,... | collective-permute-start | bytes 172040 | tf_op jit(solution)/shard_map/ppermute | solution.py:386
  33.8 5.2 %collective-permute-start.8 = (bf16[224,128]{1,0:T(8,128)(2,1)S(1)}, bf16[224,128]{1,0:T(8,128)(2,1)S(1)}, u32[]{:S(2)}, u32[]{:S(2)}) collective-permute-start(bf16[224,128]{1,0:T(8,128)(2,1)S(1)} %get-tuple-element.67), channel_id=1, source_target_pairs={{0,8},{1,9},{2,10},{3,11},{4,12},{5,13},{6,14},{7,15},{8,0},{9,1},... | collective-permute-start | bytes 172040 | tf_op jit(solution)/shard_map/ppermute | solution.py:386

commit v4 on v3

--- a/solution.py
+++ b/solution.py
@@ -121,13 +121,12 @@
     return affine * jax.nn.sigmoid(affine)
 
 
-def fill_hidden(padded, clip_ref, parcel_ref, mean, inv, gain, bias):
-    clear_edges(padded)
+def fill_hidden(padded, clip_ref, parcel_ref, mean, inv, gain, bias, begin, stop):
     frames, rows, cols, width = clip_ref.shape
     places = rows * cols
     lead = KT - 1
     at_start = lax.axis_index("ctx") == 0
-    for frame in range(frames + lead):
+    for frame in range(begin, stop):
         if frame < lead:
             before = parcel_ref[frame * places : (frame + 1) * places].reshape(rows, cols, width)
             value = jnp.where(at_start, clip_ref[0].astype(f32), before.astype(f32))
@@ -148,12 +147,16 @@
 ):
     frames, rows, cols, width = clip_ref.shape
     mean, inv = moments(stats_ref, parcel_ref, members)
-    fill_hidden(padded, clip_ref, parcel_ref, mean, inv, gain_ref[...], bias_ref[...])
+    clear_edges(padded)
+    filled = 0
     cot_t = cot_t_ref[...]
     pieces = [(t, i) for t in range(KT) for i in range(KS)]
     begin = 0
     for at in range(0, len(pieces), 2):
         parts = []
+        needed = pieces[at : at + 2][-1][0] + frames
+        fill_hidden(padded, clip_ref, parcel_ref, mean, inv, gain_ref[...], bias_ref[...], filled, needed)
+        filled = needed
         for t, i in pieces[at : at + 2]:
             parts += tap_block(padded, frames, rows, t, i)
         if at + 2 > len(pieces):
@@ -194,9 +197,11 @@
         row += count
 
 
-def forward_kernel(padded, clip_ref, weight_ref, short_ref, out_ref):
-    frames, rows, cols, width = clip_ref.shape
-    for frame in range(frames):
+def forward_kernel(begin, padded, clip_ref, weight_ref, short_ref, *rest):
+    out_ref = rest[-1]
+    rows, cols, width = clip_ref.shape[1:]
+    for at in range(out_ref.shape[0]):
+        frame = begin + at
         parts = []
         for t in range(KT):
             for i in range(KS):
@@ -206,7 +211,26 @@
         result = result + jnp.dot(
             clip_ref[frame].reshape(-1, width), short_ref[...], preferred_element_type=f32
         )
-        out_ref[frame] = result.astype(bf16).reshape(rows, cols, -1)
+        out_ref[at] = result.astype(bf16).reshape(rows, cols, -1)
+
+
+def forward_half(half, hidden, clip, conv_weight, short_weight, whole=None):
+    frames, height, breadth, _ = clip.shape
+    out_width = conv_weight.shape[1]
+    count = frames // 2
+    flops = 2 * conv_weight.size * count * height * breadth
+    vmem = pl.BlockSpec(memory_space=pltpu.VMEM)
+    operands = [hidden, clip, conv_weight, short_weight] + ([] if whole is None else [whole])
+    return pl.pallas_call(
+        functools.partial(forward_kernel, half * count),
+        out_shape=jax.ShapeDtypeStruct((frames, height, breadth, out_width), bf16),
+        grid=(1,),
+        in_specs=[vmem] * 4 + ([] if whole is None else [pl.BlockSpec(memory_space=pl.ANY)]),
+        out_specs=pl.BlockSpec((count, height, breadth, out_width), lambda step: (half, 0, 0, 0)),
+        input_output_aliases={} if whole is None else {4: 0},
+        compiler_params=pltpu.CompilerParams(vmem_limit_bytes=VMEM_BYTES),
+        cost_estimate=pl.CostEstimate(flops=flops // 4, bytes_accessed=0, transcendentals=0),
+    )(*operands)
 
 
 def back_weights(weight_ref, width, taps_t):
@@ -336,22 +360,27 @@
         out_ref[frame] = grad.astype(bf16).reshape(rows, cols, width)
 
 
-def plane_kernel(own_ref, got_ref, keep_ref, x_ref, y_ref, xy_ref):
-    deep = got_ref.shape[1]
-    core = lax.rem(lax.axis_index("dp"), 2)
-    x = lax.rem(lax.axis_index("dp") // 2, 2)
+def first_kernel(total_ref, got_ref, keep_ref, *send_refs):
+    at = lax.axis_index("dp")
+    z, x, core = at // 4, lax.rem(at // 2, 2), lax.rem(at, 2)
     y = lax.axis_index("ctx")
-    for z in range(deep):
-        for half, col, target in ((y, x, keep_ref), (y, 1 - x, x_ref), (1 - y, x, y_ref), (1 - y, 1 - x, xy_ref)):
-            value = own_ref[half, z, col, core] + got_ref[half, z, col].astype(f32)
-            target[z] = value.astype(target.dtype)
-
-
-def line_kernel(keep_ref, xy_ref, x_ref, y_ref, own_ref, a_ref, b_ref, c_ref):
-    z = lax.axis_index("dp") // 4
-    for step, target in enumerate((own_ref, a_ref, b_ref, c_ref)):
-        at = lax.bitwise_xor(z, step)
-        value = keep_ref[at] + x_ref[at].astype(f32) + (y_ref[at].astype(f32) + xy_ref[at].astype(f32))
+    plane = x + 2 * y
+    for step, target in enumerate((keep_ref, *send_refs)):
+        for inner in range(4):
+            to_plane = jnp.where(core == 0, lax.bitwise_xor(plane, step), inner)
+            to_z = jnp.where(core == 0, inner, lax.bitwise_xor(z, step))
+            to_x, to_y = lax.rem(to_plane, 2), to_plane // 2
+            value = total_ref[to_y, to_z, to_x, core] + got_ref[to_y, to_z, to_x].astype(f32)
+            target[inner] = value.astype(target.dtype)
+
+
+def second_kernel(keep_ref, a_ref, b_ref, c_ref, own_ref, *send_refs):
+    at = lax.axis_index("dp")
+    plane = lax.rem(at // 2, 2) + 2 * lax.axis_index("ctx")
+    here = jnp.where(lax.rem(at, 2) == 0, at // 4, plane)
+    for step, target in enumerate((own_ref, *send_refs)):
+        to = lax.bitwise_xor(here, step)
+        value = keep_ref[to] + a_ref[to].astype(f32) + (b_ref[to].astype(f32) + c_ref[to].astype(f32))
         target[...] = value.astype(target.dtype)
 
 
@@ -377,34 +406,45 @@
     return jnp.zeros_like(value) if total is None else total
 
 
-def swap(value, dp_mask, ctx_mask=0):
+def swap(value, core_0, core_1):
     dp, ctx = lax.axis_size("dp"), lax.axis_size("ctx")
+    masks = (core_0, core_1)
     pairs = []
     for source in range(dp * ctx):
         at, side = divmod(source, ctx)
+        dp_mask, ctx_mask = masks[at % 2]
         pairs.append((source, (at ^ dp_mask) * ctx + (side ^ ctx_mask)))
     return lax.ppermute(value, ("dp", "ctx"), pairs)
 
 
-def sort_plane(total, got):
+def exchange(sends, plane_core):
+    got = []
+    for step in (3, 2, 1):
+        masks = [None, None]
+        masks[plane_core] = (2 * (step % 2), step // 2)
+        masks[1 - plane_core] = (4 * step, 0)
+        got.append(swap(sends[step - 1], *masks))
+    return got
+
+
+def sort_first(total, got):
     halves, blocks, rows, cols = got.shape
-    part = (blocks // 2, rows, cols)
+    part = (4, rows, cols)
     return call(
-        plane_kernel,
+        first_kernel,
         [jax.ShapeDtypeStruct(part, f32)] + [jax.ShapeDtypeStruct(part, bf16)] * 3,
     )(total.reshape(halves, blocks // 2, 2, 2, rows, cols), got.reshape(halves, blocks // 2, 2, rows, cols))
 
 
-def sort_line(keep, *planes):
+def sort_second(keep, *got):
     part = keep.shape[1:]
     return call(
-        line_kernel,
+        second_kernel,
         [jax.ShapeDtypeStruct(part, f32)] + [jax.ShapeDtypeStruct(part, bf16)] * 3,
-        moved=keep.size * 12,
-    )(keep, *planes)
-
-
-def add_line(mine, from_a, from_b, from_c, conv_rows, short_rows, scale):
+    )(keep, *got)
+
+
+def add_last(mine, from_a, from_b, from_c, conv_rows, short_rows, scale):
     cols = mine.shape[1]
     return call(
         functools.partial(last_kernel, scale),
@@ -476,15 +516,13 @@
         flops=work, moved=cot.size * 2,
     )(clip, before, stats, gain, bias, cot_t)
 
+    clip_out = forward_half(0, hidden, clip, conv_weight, short_weight)
     if staged:
-        keep, to_x, to_y, to_xy = sort_plane(parts[0], swap(parts[1], 1))
-        planes = (swap(to_xy, 2, 1), swap(to_x, 2), swap(to_y, 0, 1))
+        got, clip_out = lax.optimization_barrier((swap(parts[1], (1, 0), (1, 0)), clip_out))
+        keep, *sends = sort_first(parts[0], got)
+        got = exchange(sends, 0)
         hidden, keep = lax.optimization_barrier((hidden, keep))
-    clip_out = call(
-        forward_kernel,
-        jax.ShapeDtypeStruct((frames, height, breadth, out_width), bf16),
-        flops=work // 4,
-    )(hidden, clip, conv_weight, short_weight)
+    clip_out = forward_half(1, hidden, clip, conv_weight, short_weight, clip_out)
     leading, clip_out = lax.optimization_barrier((leading, clip_out))
     parcel_shape = jax.ShapeDtypeStruct((lead * height * breadth + 16, in_width), bf16)
     grad, slope, sums, parcel = call(
@@ -502,10 +540,10 @@
         after = from_behind(leading, "ctx", -1).reshape(-1, in_width)
         after = jnp.concatenate([after, pieces_block(others_total(sums))], axis=0)
     if staged:
-        *planes, sums = lax.optimization_barrier((*planes, sums))
-        mine, *lines = sort_line(keep, *planes)
-        lines = (swap(lines[2], 12), swap(lines[1], 8), swap(lines[0], 4))
-        conv_grad, short_grad = add_line(mine, *lines, conv_rows, short_rows, scale)
+        *got, sums = lax.optimization_barrier((*got, sums))
+        mine, *sends = sort_second(keep, *got)
+        got = exchange(sends, 1)
+        conv_grad, short_grad = add_last(mine, *got, conv_rows, short_rows, scale)
         after, mine = lax.optimization_barrier((after, mine))
     else:
         summed = []

time: 39.8 us -> 36.3 us (0.912); the launches traced: 39.7 us -> 35.6 us
  waiting for transfers between devices: 10.2 us -> 5.23 us
  Pallas kernels: 15 us -> 15.9 us
    ppermute x7, waiting for transfers between devices: 9.08 us -> 3.64 us  [swap(): return lax.ppermute(value, ('dp', 'ctx'), pairs)]
    pallas_call x4 -> x5, Pallas kernels: 5.02 us -> 5.8 us  [the longest x2 4.83 us: forward_half(): pl.pallas_call(functools.partial(forward_kernel, half * count), out_shape...]
    ppermute x1, waiting for transfers between devices: 0.01 us -> 0.49 us  [body(): after = lax.ppermute(parcel, 'ctx', [(0, 1), (1, 0)])]
  transfers between devices with their start and end apart: 9 -> 9, of which waited for: 5 -> 5; matrix products, arithmetic and copies ran while one was open for 0% -> 0% of each run, Pallas kernels for 26% -> 31%
where the time goes in v4:
time: 36.3 us; the launch traced here: 35.6 us
  Pallas kernels  15.9 us (44%)
  starting transfers between devices  12.8 us (35%)
  waiting for transfers between devices  5.23 us (14%)
  local copies, waits for them, and re-layouts  1.02 us (3%)
  between operations  0.71 us (2%)
    ppermute x7, starting transfers between devices, swap(): return lax.ppermute(value, ('dp', 'ctx'), pairs)  8.08 us
    pallas_call x2, Pallas kernels, forward_half(): pl.pallas_call(functools.partial(forward_kernel, half * count), out_shape...  4.83 us
    pallas_call x1, Pallas kernels, body(): call(back_kernel, [jax.ShapeDtypeStruct((frames, height * breadth, in_wid...  3.85 us
    pallas_call x1, Pallas kernels, body(): call(functools.partial(weight_kernel, members, split), [jax.ShapeDtypeStr...  3.69 us
    ppermute x7, waiting for transfers between devices, swap(): return lax.ppermute(value, ('dp', 'ctx'), pairs)  3.64 us
    ppermute x1, starting transfers between devices, body(): before = lax.ppermute(parcel, 'ctx', [(0, 1), (1, 0)])  2.97 us
    ppermute x1, starting transfers between devices, body(): after = lax.ppermute(parcel, 'ctx', [(0, 1), (1, 0)])  1.76 us
    pallas_call x1, Pallas kernels, body(): call(functools.partial(finish_kernel, members), jax.ShapeDtypeStruct((fra...  1.17 us
  transfers between devices with their start and end apart: 9, of which 5 were waited for; matrix products, arithmetic and copies ran while one was open for 0% of the time, Pallas kernels for 31%

profile of v4, /device:TPU:0, one launch (start us, length us, event | category | flops | bytes accessed | tf_op | source)
XLA Modules:
  0.0 35.6 jit_solution(6004530688811154515)
XLA Ops:
  0.6 0.0 copy-start.1
  0.6 1.0 %copy-done.1 = bf16[1,4,4,96,128]{4,3,2,1,0:T(8,128)(2,1)S(1)} copy-done((bf16[1,4,4,96,128]{4,3,2,1,0:T(8,128)(2,1)S(1)}, bf16[1,4,4,96,128]{4,3,2,1,0:T(8,128)(2,1)}, u32[]{:S(2)}) %copy-start.1) | copy-done | bytes 393240
  1.6 0.0 copy-start
  1.6 0.0 copy-start.3
  1.6 0.3 shard_map.94
  1.9 3.0 %collective-permute-start = (bf16[784,128]{1,0:T(8,128)(2,1)S(1)}, bf16[784,128]{1,0:T(8,128)(2,1)S(1)}, u32[]{:S(2)}, u32[]{:S(2)}) collective-permute-start(bf16[784,128]{1,0:T(8,128)(2,1)S(1)} %get-tuple-element.40), channel_id=1, source_target_pairs={{0,1},{1,0},{2,3},{3,2},{4,5},{5,4},{6,7},{7,6},{8,9},{9,8},{10,11... | collective-permute-start | bytes 602120 | tf_op jit(solution)/shard_map/ppermute | solution.py:483
  4.9 0.0 copy-done
  4.9 0.0 copy-done.3
  4.9 0.0 copy-start.2
  4.9 0.0 copy-start.5
  4.9 0.0 copy-start.6
  4.9 3.9 %shard_map.93 = (f32[4,384,128]{2,1,0:T(8,128)S(1)}, bf16[2,384,128]{2,1,0:T(8,128)(2,1)S(1)}, bf16[256,1536]{1,0:T(8,128)(2,1)S(1)}) custom-call(bf16[4,4,96,256]{3,2,1,0:T(8,128)(2,1)S(1)} %bitcast.16, bf16[3456,256]{1,0:T(8,128)(2,1)S(1)} %copy-done), custom_call_target="tpu_custom_call" | custom-call | flops 5435817984 | bytes 1769472 | tf_op jit(solution)/shard_map/pallas_call | solution.py:488
  8.8 1.1 %collective-permute-done.parcel_ref = bf16[784,128]{1,0:T(8,128)(2,1)S(1)} collective-permute-done((bf16[784,128]{1,0:T(8,128)(2,1)S(1)}, bf16[784,128]{1,0:T(8,128)(2,1)S(1)}, u32[]{:S(2)}, u32[]{:S(2)}) %collective-permute-start) | collective-permute-done | bytes 200736 | tf_op jit(solution)/shard_map/ppermute | solution.py:483
  9.9 0.0 copy-done.2
  9.9 0.0 copy-done.5
  9.9 0.0 copy-done.6
  9.9 0.0 copy-start.4
  9.9 3.7 %shard_map.95 = (bf16[3,6,6,96,128]{4,3,2,1,0:T(8,128)(2,1)S(1)}, f32[2,16,224,128]{3,2,1,0:T(8,128)S(1)}, bf16[2,8,224,128]{3,2,1,0:T(8,128)(2,1)S(1)}) custom-call(bf16[4,4,96,128]{3,2,1,0:T(8,128)(2,1)S(1)} %bitcast.9, bf16[784,128]{1,0:T(8,128)(2,1)S(1)} %collective-permute-done.parcel_ref, f32[8,128]{1,0:T(8,128)S(1)} %get-tuple-element.43.stats_ref, ...), custom_call_target="tpu_custom_call" | custom-call | flops 2717908992 | bytes 786432 | tf_op jit(solution)/shard_map/pallas_call | solution.py:513
  13.6 0.1 collective-permute-start.1
  13.7 0.0 copy-done.4
  13.7 2.4 %shard_map.96.rest_0_ = bf16[4,4,96,256]{3,2,1,0:T(8,128)(2,1)} custom-call(bf16[3,6,6,96,128]{4,3,2,1,0:T(8,128)(2,1)S(1)} %get-tuple-element.50.padded, bf16[4,4,96,128]{3,2,1,0:T(8,128)(2,1)S(1)} %bitcast.10, bf16[3456,256]{1,0:T(8,128)(2,1)S(1)} %copy-done, bf16[128,256]{1,0:T(8,128)(2,1)S(1)} %copy-done.4), custom_call_target="tpu_custom_call" | custom-call | flops 339738624 | tf_op jit(solution)/shard_map/pallas_call | solution.py:224
  16.1 0.0 collective-permute-done.1
  16.1 0.2 shard_map.97
  16.3 2.7 %collective-permute-start.2 = (bf16[4,224,128]{2,1,0:T(8,128)(2,1)S(1)}, bf16[4,224,128]{2,1,0:T(8,128)(2,1)S(1)}, u32[]{:S(2)}, u32[]{:S(2)}) collective-permute-start(bf16[4,224,128]{2,1,0:T(8,128)(2,1)S(1)} %get-tuple-element.57), channel_id=1, source_target_pairs={{0,5},{1,4},{2,26},{3,27},{4,1},{5,0},{6,30},{7,31},{8,13},{9,12},... | collective-permute-start | bytes 688136 | tf_op jit(solution)/shard_map/ppermute | solution.py:417
  19.1 0.5 %collective-permute-start.3 = (bf16[4,224,128]{2,1,0:T(8,128)(2,1)S(1)}, bf16[4,224,128]{2,1,0:T(8,128)(2,1)S(1)}, u32[]{:S(2)}, u32[]{:S(2)}) collective-permute-start(bf16[4,224,128]{2,1,0:T(8,128)(2,1)S(1)} %get-tuple-element.58), channel_id=1, source_target_pairs={{0,1},{1,0},{2,18},{3,19},{4,5},{5,4},{6,22},{7,23},{8,9},{9,8},{1... | collective-permute-start | bytes 688136 | tf_op jit(solution)/shard_map/ppermute | solution.py:417
  19.6 0.3 collective-permute-start.4
  19.9 2.4 %shard_map.98 = bf16[4,4,96,256]{3,2,1,0:T(8,128)(2,1)} custom-call(bf16[3,6,6,96,128]{4,3,2,1,0:T(8,128)(2,1)S(1)} %get-tuple-element.50.padded, bf16[4,4,96,128]{3,2,1,0:T(8,128)(2,1)S(1)} %bitcast.11, bf16[3456,256]{1,0:T(8,128)(2,1)S(1)} %copy-done, bf16[128,256]{1,0:T(8,128)(2,1)S(1)} %copy-done.4, ...), custom_call_target="tpu_custom_call", output_to_operand_aliasing={{}: (4, {})} | custom-call | flops 339738624 | tf_op jit(solution)/shard_map/pallas_call | solution.py:224
  22.3 1.1 %shard_map.99 = (f32[4,384,128]{2,1,0:T(8,128)S(1)}, f32[2,384,128]{2,1,0:T(8,128)S(1)}, f32[8,128]{1,0:T(8,128)S(1)}, bf16[784,128]{1,0:T(8,128)(2,1)S(1)}) custom-call(f32[4,384,128]{2,1,0:T(8,128)S(1)} %get-tuple-element.53.part_ref, bf16[2,384,128]{2,1,0:T(8,128)(2,1)S(1)} %get-tuple-element.54.leading_ref, bf16[4,4,96,128]{3,2,1,0:T(8,128)(2,1)S(1)} %bitcast.12, ...), custom_call_target="tpu_custom_call" | custom-call | tf_op jit(solution)/shard_map/pallas_call | solution.py:528
  23.4 1.8 %collective-permute-start.5 = (bf16[784,128]{1,0:T(8,128)(2,1)S(1)}, bf16[784,128]{1,0:T(8,128)(2,1)S(1)}, u32[]{:S(2)}, u32[]{:S(2)}) collective-permute-start(bf16[784,128]{1,0:T(8,128)(2,1)S(1)} %get-tuple-element.62), channel_id=1, source_target_pairs={{0,1},{1,0},{2,3},{3,2},{4,5},{5,4},{6,7},{7,6},{8,9},{9,8},{10,11... | collective-permute-start | bytes 602120 | tf_op jit(solution)/shard_map/ppermute | solution.py:538
  25.1 0.0 collective-permute-done.2.a_ref
  25.1 0.6 %collective-permute-done.3.b_ref = bf16[4,224,128]{2,1,0:T(8,128)(2,1)S(1)} collective-permute-done((bf16[4,224,128]{2,1,0:T(8,128)(2,1)S(1)}, bf16[4,224,128]{2,1,0:T(8,128)(2,1)S(1)}, u32[]{:S(2)}, u32[]{:S(2)}) %collective-permute-start.3) | collective-permute-done | bytes 229408 | tf_op jit(solution)/shard_map/ppermute | solution.py:417
  25.8 0.3 collective-permute-done.4.c_ref
  26.1 0.1 shard_map.100
  26.2 3.7 %collective-permute-start.6 = (bf16[224,128]{1,0:T(8,128)(2,1)S(1)}, bf16[224,128]{1,0:T(8,128)(2,1)S(1)}, u32[]{:S(2)}, u32[]{:S(2)}) collective-permute-start(bf16[224,128]{1,0:T(8,128)(2,1)S(1)} %get-tuple-element.69), channel_id=1, source_target_pairs={{0,24},{1,25},{2,7},{3,6},{4,28},{5,29},{6,3},{7,2},{8,16},{9,17},... | collective-permute-start | bytes 172040 | tf_op jit(solution)/shard_map/ppermute | solution.py:417
  29.9 0.0 collective-permute-start.7
  29.9 0.8 %collective-permute-start.8 = (bf16[224,128]{1,0:T(8,128)(2,1)S(1)}, bf16[224,128]{1,0:T(8,128)(2,1)S(1)}, u32[]{:S(2)}, u32[]{:S(2)}) collective-permute-start(bf16[224,128]{1,0:T(8,128)(2,1)S(1)} %get-tuple-element.71), channel_id=1, source_target_pairs={{0,8},{1,9},{2,6},{3,7},{4,12},{5,13},{6,2},{7,3},{8,0},{9,1},{10,... | collective-permute-start | bytes 172040 | tf_op jit(solution)/shard_map/ppermute | solution.py:417
  30.7 0.5 %collective-permute-done.5.after_ref = bf16[784,128]{1,0:T(8,128)(2,1)S(1)} collective-permute-done((bf16[784,128]{1,0:T(8,128)(2,1)S(1)}, bf16[784,128]{1,0:T(8,128)(2,1)S(1)}, u32[]{:S(2)}, u32[]{:S(2)}) %collective-permute-start.5) | collective-permute-done | bytes 200736 | tf_op jit(solution)/shard_map/ppermute | solution.py:538
  31.2 1.2 %shard_map.101 = bf16[4,4,96,128]{3,2,1,0:T(8,128)(2,1)} custom-call(f32[4,384,128]{2,1,0:T(8,128)S(1)} %get-tuple-element.55.grad_ref, f32[2,384,128]{2,1,0:T(8,128)S(1)} %get-tuple-element.56.slope_ref, f32[8,128]{1,0:T(8,128)S(1)} %get-tuple-element.61.sums_ref, bf16[784,128]{1,0:T(8,128)(2,1)S(1)} %collective-permute-done.5.after_ref, ...), custom_call_target="tpu_custom_call" | custom-call | flops 135895456 | bytes 1572864 | tf_op jit(solution)/shard_map/pallas_call | solution.py:555
  32.3 0.0 collective-permute-done.6.a_ref
  32.3 2.6 %collective-permute-done.7.b_ref = bf16[224,128]{1,0:T(8,128)(2,1)S(1)} collective-permute-done((bf16[224,128]{1,0:T(8,128)(2,1)S(1)}, bf16[224,128]{1,0:T(8,128)(2,1)S(1)}, u32[]{:S(2)}, u32[]{:S(2)}) %collective-permute-start.7) | collective-permute-done | bytes 57376 | tf_op jit(solution)/shard_map/ppermute | solution.py:417
  35.0 0.0 collective-permute-done.8.c_ref
  35.0 0.7 %shard_map.102 = (f32[216,128]{1,0:T(8,128)}, f32[8,128]{1,0:T(8,128)}) custom-call(f32[224,128]{1,0:T(8,128)S(1)} %get-tuple-element.67.own_ref, bf16[224,128]{1,0:T(8,128)(2,1)S(1)} %collective-permute-done.6.a_ref, bf16[224,128]{1,0:T(8,128)(2,1)S(1)} %collective-permute-done.7.b_ref, bf16[224,128]{1,0:T(8,128)(2,1)S(1)} %collective-permute-done.8.c_ref), custom_call_target="tpu_custom_call" | custom-call | bytes 344064 | tf_op jit(solution)/shard_map/pallas_call | solution.py:449
Async XLA Ops:
  0.6 1.0 %copy-start.1 = (bf16[1,4,4,96,128]{4,3,2,1,0:T(8,128)(2,1)S(1)}, bf16[1,4,4,96,128]{4,3,2,1,0:T(8,128)(2,1)}, u32[]{:S(2)}) copy-start(bf16[1,4,4,96,128]{4,3,2,1,0:T(8,128)(2,1)} %param.6) | copy-start | bytes 1179652
  1.6 3.3 %copy-start = (bf16[3456,256]{1,0:T(8,128)(2,1)S(1)}, bf16[3456,256]{1,0:T(8,128)(2,1)}, u32[]{:S(2)}) copy-start(bf16[3456,256]{1,0:T(8,128)(2,1)} %weight_ref.5) | copy-start | bytes 5308420
  1.6 3.3 %copy-start.3 = (bf16[1,4,4,96,256]{4,3,2,1,0:T(8,128)(2,1)S(1)}, bf16[1,4,4,96,256]{4,3,2,1,0:T(8,128)(2,1)}, u32[]{:S(2)}) copy-start(bf16[1,4,4,96,256]{4,3,2,1,0:T(8,128)(2,1)} %param.11) | copy-start | bytes 2359300
  1.9 8.0 %collective-permute-start = (bf16[784,128]{1,0:T(8,128)(2,1)S(1)}, bf16[784,128]{1,0:T(8,128)(2,1)S(1)}, u32[]{:S(2)}, u32[]{:S(2)}) collective-permute-start(bf16[784,128]{1,0:T(8,128)(2,1)S(1)} %get-tuple-element.40), channel_id=1, source_target_pairs={{0,1},{1,0},{2,3},{3,2},{4,5},{5,4},{6,7},{7,6},{8,9},{9,8},{10,11... | collective-permute-start | bytes 602120 | tf_op jit(solution)/shard_map/ppermute | solution.py:483
  4.9 5.0 %copy-start.2 = (bf16[1,4,4,96,128]{4,3,2,1,0:T(8,128)(2,1)S(1)}, bf16[1,4,4,96,128]{4,3,2,1,0:T(8,128)(2,1)}, u32[]{:S(2)}) copy-start(bf16[1,4,4,96,128]{4,3,2,1,0:T(8,128)(2,1)} %param.6) | copy-start | bytes 1179652
  4.9 5.0 %copy-start.5 = (f32[128]{0:T(128)S(1)}, f32[128]{0:T(128)}, u32[]{:S(2)}) copy-start(f32[128]{0:T(128)} %param.7) | copy-start | bytes 1540
  4.9 5.0 %copy-start.6 = (f32[128]{0:T(128)S(1)}, f32[128]{0:T(128)}, u32[]{:S(2)}) copy-start(f32[128]{0:T(128)} %param.8) | copy-start | bytes 1540
  9.9 3.8 %copy-start.4 = (bf16[128,256]{1,0:T(8,128)(2,1)S(1)}, bf16[128,256]{1,0:T(8,128)(2,1)}, u32[]{:S(2)}) copy-start(bf16[128,256]{1,0:T(8,128)(2,1)} %short_ref.5) | copy-start | bytes 196612
  13.6 2.5 %collective-permute-start.1 = (bf16[2,8,224,128]{3,2,1,0:T(8,128)(2,1)S(1)}, bf16[2,8,224,128]{3,2,1,0:T(8,128)(2,1)S(1)}, u32[]{:S(2)}, u32[]{:S(2)}) collective-permute-start(bf16[2,8,224,128]{3,2,1,0:T(8,128)(2,1)S(1)} %get-tuple-element.47), channel_id=1, source_target_pairs={{0,2},{1,3},{2,0},{3,1},{4,6},{5,7},{6,4},{7,5},{8,10},{9,11},{10,... | collective-permute-start | bytes 2752520 | tf_op jit(solution)/shard_map/ppermute | solution.py:417
  16.3 8.8 %collective-permute-start.2 = (bf16[4,224,128]{2,1,0:T(8,128)(2,1)S(1)}, bf16[4,224,128]{2,1,0:T(8,128)(2,1)S(1)}, u32[]{:S(2)}, u32[]{:S(2)}) collective-permute-start(bf16[4,224,128]{2,1,0:T(8,128)(2,1)S(1)} %get-tuple-element.57), channel_id=1, source_target_pairs={{0,5},{1,4},{2,26},{3,27},{4,1},{5,0},{6,30},{7,31},{8,13},{9,12},... | collective-permute-start | bytes 688136 | tf_op jit(solution)/shard_map/ppermute | solution.py:417
  19.1 6.7 %collective-permute-start.3 = (bf16[4,224,128]{2,1,0:T(8,128)(2,1)S(1)}, bf16[4,224,128]{2,1,0:T(8,128)(2,1)S(1)}, u32[]{:S(2)}, u32[]{:S(2)}) collective-permute-start(bf16[4,224,128]{2,1,0:T(8,128)(2,1)S(1)} %get-tuple-element.58), channel_id=1, source_target_pairs={{0,1},{1,0},{2,18},{3,19},{4,5},{5,4},{6,22},{7,23},{8,9},{9,8},{1... | collective-permute-start | bytes 688136 | tf_op jit(solution)/shard_map/ppermute | solution.py:417
  19.6 6.5 %collective-permute-start.4 = (bf16[4,224,128]{2,1,0:T(8,128)(2,1)S(1)}, bf16[4,224,128]{2,1,0:T(8,128)(2,1)S(1)}, u32[]{:S(2)}, u32[]{:S(2)}) collective-permute-start(bf16[4,224,128]{2,1,0:T(8,128)(2,1)S(1)} %get-tuple-element.59), channel_id=1, source_target_pairs={{0,4},{1,5},{2,10},{3,11},{4,0},{5,1},{6,14},{7,15},{8,12},{9,13},... | collective-permute-start | bytes 688136 | tf_op jit(solution)/shard_map/ppermute | solution.py:417
  23.4 7.8 %collective-permute-start.5 = (bf16[784,128]{1,0:T(8,128)(2,1)S(1)}, bf16[784,128]{1,0:T(8,128)(2,1)S(1)}, u32[]{:S(2)}, u32[]{:S(2)}) collective-permute-start(bf16[784,128]{1,0:T(8,128)(2,1)S(1)} %get-tuple-element.62), channel_id=1, source_target_pairs={{0,1},{1,0},{2,3},{3,2},{4,5},{5,4},{6,7},{7,6},{8,9},{9,8},{10,11... | collective-permute-start | bytes 602120 | tf_op jit(solution)/shard_map/ppermute | solution.py:538
  26.2 6.1 %collective-permute-start.6 = (bf16[224,128]{1,0:T(8,128)(2,1)S(1)}, bf16[224,128]{1,0:T(8,128)(2,1)S(1)}, u32[]{:S(2)}, u32[]{:S(2)}) collective-permute-start(bf16[224,128]{1,0:T(8,128)(2,1)S(1)} %get-tuple-element.69), channel_id=1, source_target_pairs={{0,24},{1,25},{2,7},{3,6},{4,28},{5,29},{6,3},{7,2},{8,16},{9,17},... | collective-permute-start | bytes 172040 | tf_op jit(solution)/shard_map/ppermute | solution.py:417
  29.9 5.1 %collective-permute-start.7 = (bf16[224,128]{1,0:T(8,128)(2,1)S(1)}, bf16[224,128]{1,0:T(8,128)(2,1)S(1)}, u32[]{:S(2)}, u32[]{:S(2)}) collective-permute-start(bf16[224,128]{1,0:T(8,128)(2,1)S(1)} %get-tuple-element.70), channel_id=1, source_target_pairs={{0,16},{1,17},{2,3},{3,2},{4,20},{5,21},{6,7},{7,6},{8,24},{9,25},... | collective-permute-start | bytes 172040 | tf_op jit(solution)/shard_map/ppermute | solution.py:417
  29.9 5.1 %collective-permute-start.8 = (bf16[224,128]{1,0:T(8,128)(2,1)S(1)}, bf16[224,128]{1,0:T(8,128)(2,1)S(1)}, u32[]{:S(2)}, u32[]{:S(2)}) collective-permute-start(bf16[224,128]{1,0:T(8,128)(2,1)S(1)} %get-tuple-element.71), channel_id=1, source_target_pairs={{0,8},{1,9},{2,6},{3,7},{4,12},{5,13},{6,2},{7,3},{8,0},{9,1},{10,... | collective-permute-start | bytes 172040 | tf_op jit(solution)/shard_map/ppermute | solution.py:417

commit v5 on v4

--- a/solution.py
+++ b/solution.py
@@ -18,8 +18,10 @@
 bf16 = jnp.bfloat16
 
 
-def call(kernel, outs, scratch=(), flops=0, moved=0, in_specs=None):
+def call(kernel, outs, scratch=(), flops=0, moved=0, in_specs=None, out_specs=None, aliases=None):
     specs = {} if in_specs is None else {"in_specs": in_specs}
+    if out_specs is not None:
+        specs.update(out_specs=out_specs, input_output_aliases=aliases)
     return pl.pallas_call(
         kernel,
         out_shape=outs,
@@ -214,23 +216,23 @@
         out_ref[at] = result.astype(bf16).reshape(rows, cols, -1)
 
 
-def forward_half(half, hidden, clip, conv_weight, short_weight, whole=None):
+def forward_half(half, hidden, clip, conv_weight, short_weight, whole_shape=False):
     frames, height, breadth, _ = clip.shape
     out_width = conv_weight.shape[1]
     count = frames // 2
     flops = 2 * conv_weight.size * count * height * breadth
     vmem = pl.BlockSpec(memory_space=pltpu.VMEM)
-    operands = [hidden, clip, conv_weight, short_weight] + ([] if whole is None else [whole])
+    block = (count, height, breadth, out_width)
+    at = half if whole_shape else 0
     return pl.pallas_call(
         functools.partial(forward_kernel, half * count),
-        out_shape=jax.ShapeDtypeStruct((frames, height, breadth, out_width), bf16),
+        out_shape=jax.ShapeDtypeStruct((frames if whole_shape else count,) + block[1:], bf16),
         grid=(1,),
-        in_specs=[vmem] * 4 + ([] if whole is None else [pl.BlockSpec(memory_space=pl.ANY)]),
-        out_specs=pl.BlockSpec((count, height, breadth, out_width), lambda step: (half, 0, 0, 0)),
-        input_output_aliases={} if whole is None else {4: 0},
+        in_specs=[vmem] * 4,
+        out_specs=pl.BlockSpec(block, lambda step: (at, 0, 0, 0)),
         compiler_params=pltpu.CompilerParams(vmem_limit_bytes=VMEM_BYTES),
         cost_estimate=pl.CostEstimate(flops=flops // 4, bytes_accessed=0, transcendentals=0),
-    )(*operands)
+    )(hidden, clip, conv_weight, short_weight)
 
 
 def back_weights(weight_ref, width, taps_t):
@@ -294,9 +296,12 @@
 
 def activation_kernel(
     members,
-    part_ref, leading_ref, clip_ref, parcel_ref, stats_ref, gain_ref, bias_ref,
-    grad_ref, slope_ref, sums_ref, out_ref,
+    part_ref, leading_ref, clip_ref, parcel_ref, stats_ref, gain_ref, bias_ref, half_ref, _,
+    grad_ref, slope_ref, sums_ref, out_ref, whole_ref, sem,
 ):
+    count = half_ref.shape[0]
+    copy = pltpu.make_async_copy(half_ref, whole_ref.at[pl.ds(whole_ref.shape[0] - count, count)], sem)
+    copy.start()
     frames, rows, cols, width = clip_ref.shape
     places = rows * cols
     gain = gain_ref[...]
@@ -332,6 +337,7 @@
     sums = group_totals(two_rows(total, cross))
     sums_ref[...] = sums
     out_ref[lead * places :] = pieces_block(sums)
+    copy.wait()
 
 
 def finish_kernel(
@@ -516,24 +522,29 @@
         flops=work, moved=cot.size * 2,
     )(clip, before, stats, gain, bias, cot_t)
 
-    clip_out = forward_half(0, hidden, clip, conv_weight, short_weight)
+    clip_out = forward_half(0, hidden, clip, conv_weight, short_weight, True)
     if staged:
         got, clip_out = lax.optimization_barrier((swap(parts[1], (1, 0), (1, 0)), clip_out))
         keep, *sends = sort_first(parts[0], got)
         got = exchange(sends, 0)
         hidden, keep = lax.optimization_barrier((hidden, keep))
-    clip_out = forward_half(1, hidden, clip, conv_weight, short_weight, clip_out)
-    leading, clip_out = lax.optimization_barrier((leading, clip_out))
+    second_half = forward_half(1, hidden, clip, conv_weight, short_weight)
+    anywhere, vmem = pl.BlockSpec(memory_space=pl.ANY), pl.BlockSpec(memory_space=pltpu.VMEM)
     parcel_shape = jax.ShapeDtypeStruct((lead * height * breadth + 16, in_width), bf16)
-    grad, slope, sums, parcel = call(
+    grad, slope, sums, parcel, clip_out = call(
         functools.partial(activation_kernel, members),
         [
             jax.ShapeDtypeStruct((frames, height * breadth, in_width), f32),
             jax.ShapeDtypeStruct((lead, height * breadth, in_width), f32),
             jax.ShapeDtypeStruct((8, in_width), f32),
             parcel_shape,
+            jax.ShapeDtypeStruct(clip_out.shape, bf16),
         ],
-    )(back_part, leading, clip, before, stats, gain, bias)
+        [pltpu.SemaphoreType.DMA],
+        in_specs=[vmem] * 8 + [anywhere],
+        out_specs=[vmem] * 4 + [anywhere],
+        aliases={8: 4},
+    )(back_part, leading, clip, before, stats, gain, bias, second_half, clip_out)
     if ctx_size == 2:
         after = lax.ppermute(parcel, "ctx", [(0, 1), (1, 0)])
     else:

time: 36.3 us -> 36.2 us (level)
  Pallas kernels: 15.9 us -> 15 us
  waiting for transfers between devices: 5.23 us -> 5.88 us
    ppermute x7, waiting for transfers between devices: 3.64 us -> 4.77 us  [swap(): return lax.ppermute(value, ('dp', 'ctx'), pairs)]
    pallas_call x2, Pallas kernels: 4.83 us -> 4.07 us  [forward_half(): pl.pallas_call(functools.partial(forward_kernel, half * count), out_shape...]
    ppermute x1, waiting for transfers between devices: 0.49 us -> 0.01 us  [body(): after = lax.ppermute(parcel, 'ctx', [(0, 1), (1, 0)])]
  transfers between devices with their start and end apart: 9 -> 9, of which waited for: 5 -> 5; matrix products, arithmetic and copies ran while one was open for 0% -> 0% of each run, Pallas kernels for 31% -> 29%
where the time goes in v5:
time: 36.2 us; the launch traced here: 35.5 us
  Pallas kernels  15 us (41%)
  starting transfers between devices  12.9 us (36%)
  waiting for transfers between devices  5.88 us (16%)
  local copies, waits for them, and re-layouts  1.02 us (3%)
  between operations  0.72 us (2%)
    ppermute x7, starting transfers between devices, swap(): return lax.ppermute(value, ('dp', 'ctx'), pairs)  8.08 us
    ppermute x7, waiting for transfers between devices, swap(): return lax.ppermute(value, ('dp', 'ctx'), pairs)  4.77 us
    pallas_call x2, Pallas kernels, forward_half(): pl.pallas_call(functools.partial(forward_kernel, half * count), out_shape...  4.07 us
    pallas_call x1, Pallas kernels, body(): call(back_kernel, [jax.ShapeDtypeStruct((frames, height * breadth, in_wid...  3.85 us
    pallas_call x1, Pallas kernels, body(): call(functools.partial(weight_kernel, members, split), [jax.ShapeDtypeStr...  3.56 us
    ppermute x1, starting transfers between devices, body(): before = lax.ppermute(parcel, 'ctx', [(0, 1), (1, 0)])  2.97 us
    ppermute x1, starting transfers between devices, body(): after = lax.ppermute(parcel, 'ctx', [(0, 1), (1, 0)])  1.81 us
    pallas_call x1, Pallas kernels, body(): call(functools.partial(finish_kernel, members), jax.ShapeDtypeStruct((fra...  1.17 us
  transfers between devices with their start and end apart: 9, of which 5 were waited for; matrix products, arithmetic and copies ran while one was open for 0% of the time, Pallas kernels for 29%

profile of v5, /device:TPU:0, one launch (start us, length us, event | category | flops | bytes accessed | tf_op | source)
XLA Modules:
  0.0 35.5 jit_solution(5381509635511064138)
XLA Ops:
  0.6 0.0 copy-start.1
  0.6 1.0 %copy-done.1 = bf16[1,4,4,96,128]{4,3,2,1,0:T(8,128)(2,1)S(1)} copy-done((bf16[1,4,4,96,128]{4,3,2,1,0:T(8,128)(2,1)S(1)}, bf16[1,4,4,96,128]{4,3,2,1,0:T(8,128)(2,1)}, u32[]{:S(2)}) %copy-start.1) | copy-done | bytes 393240
  1.6 0.0 copy-start
  1.6 0.0 copy-start.3
  1.6 0.3 shard_map.93
  1.9 3.0 %collective-permute-start = (bf16[784,128]{1,0:T(8,128)(2,1)S(1)}, bf16[784,128]{1,0:T(8,128)(2,1)S(1)}, u32[]{:S(2)}, u32[]{:S(2)}) collective-permute-start(bf16[784,128]{1,0:T(8,128)(2,1)S(1)} %get-tuple-element.38), channel_id=1, source_target_pairs={{0,1},{1,0},{2,3},{3,2},{4,5},{5,4},{6,7},{7,6},{8,9},{9,8},{10,11... | collective-permute-start | bytes 602120 | tf_op jit(solution)/shard_map/ppermute | solution.py:489
  4.9 0.0 copy-done
  4.9 0.0 copy-done.3
  4.9 0.0 copy-start.2
  4.9 0.0 copy-start.5
  4.9 0.0 copy-start.6
  4.9 3.9 %shard_map.94 = (f32[4,384,128]{2,1,0:T(8,128)S(1)}, bf16[2,384,128]{2,1,0:T(8,128)(2,1)S(1)}, bf16[256,1536]{1,0:T(8,128)(2,1)S(1)}) custom-call(bf16[4,4,96,256]{3,2,1,0:T(8,128)(2,1)S(1)} %bitcast.16, bf16[3456,256]{1,0:T(8,128)(2,1)S(1)} %copy-done), custom_call_target="tpu_custom_call" | custom-call | flops 5435817984 | bytes 1769472 | tf_op jit(solution)/shard_map/pallas_call | solution.py:494
  8.8 1.1 %collective-permute-done.parcel_ref = bf16[784,128]{1,0:T(8,128)(2,1)S(1)} collective-permute-done((bf16[784,128]{1,0:T(8,128)(2,1)S(1)}, bf16[784,128]{1,0:T(8,128)(2,1)S(1)}, u32[]{:S(2)}, u32[]{:S(2)}) %collective-permute-start) | collective-permute-done | bytes 200736 | tf_op jit(solution)/shard_map/ppermute | solution.py:489
  9.9 0.0 copy-done.2
  9.9 0.0 copy-done.5
  9.9 0.0 copy-done.6
  9.9 0.0 copy-start.4
  9.9 3.6 %shard_map.95 = (bf16[3,6,6,96,128]{4,3,2,1,0:T(8,128)(2,1)S(1)}, f32[2,16,224,128]{3,2,1,0:T(8,128)S(1)}, bf16[2,8,224,128]{3,2,1,0:T(8,128)(2,1)S(1)}) custom-call(bf16[4,4,96,128]{3,2,1,0:T(8,128)(2,1)S(1)} %bitcast.9, bf16[784,128]{1,0:T(8,128)(2,1)S(1)} %collective-permute-done.parcel_ref, f32[8,128]{1,0:T(8,128)S(1)} %get-tuple-element.43.stats_ref, ...), custom_call_target="tpu_custom_call" | custom-call | flops 2717908992 | bytes 786432 | tf_op jit(solution)/shard_map/pallas_call | solution.py:519
  13.5 0.1 collective-permute-start.1
  13.6 0.0 copy-done.4
  13.6 2.4 %shard_map.96._ = bf16[4,4,96,256]{3,2,1,0:T(8,128)(2,1)} custom-call(bf16[3,6,6,96,128]{4,3,2,1,0:T(8,128)(2,1)S(1)} %get-tuple-element.50.padded, bf16[4,4,96,128]{3,2,1,0:T(8,128)(2,1)S(1)} %bitcast.10, bf16[3456,256]{1,0:T(8,128)(2,1)S(1)} %copy-done, bf16[128,256]{1,0:T(8,128)(2,1)S(1)} %copy-done.4), custom_call_target="tpu_custom_call" | custom-call | flops 339738624 | tf_op jit(solution)/shard_map/pallas_call | solution.py:227
  16.0 0.0 collective-permute-done.1
  16.0 0.2 shard_map.97
  16.2 2.7 %collective-permute-start.2 = (bf16[4,224,128]{2,1,0:T(8,128)(2,1)S(1)}, bf16[4,224,128]{2,1,0:T(8,128)(2,1)S(1)}, u32[]{:S(2)}, u32[]{:S(2)}) collective-permute-start(bf16[4,224,128]{2,1,0:T(8,128)(2,1)S(1)} %get-tuple-element.55), channel_id=1, source_target_pairs={{0,5},{1,4},{2,26},{3,27},{4,1},{5,0},{6,30},{7,31},{8,13},{9,12},... | collective-permute-start | bytes 688136 | tf_op jit(solution)/shard_map/ppermute | solution.py:423
  18.9 0.5 %collective-permute-start.3 = (bf16[4,224,128]{2,1,0:T(8,128)(2,1)S(1)}, bf16[4,224,128]{2,1,0:T(8,128)(2,1)S(1)}, u32[]{:S(2)}, u32[]{:S(2)}) collective-permute-start(bf16[4,224,128]{2,1,0:T(8,128)(2,1)S(1)} %get-tuple-element.56), channel_id=1, source_target_pairs={{0,1},{1,0},{2,18},{3,19},{4,5},{5,4},{6,22},{7,23},{8,9},{9,8},{1... | collective-permute-start | bytes 688136 | tf_op jit(solution)/shard_map/ppermute | solution.py:423
  19.4 0.3 collective-permute-start.4
  19.8 1.7 %shard_map.98.half_ref = bf16[2,4,96,256]{3,2,1,0:T(8,128)(2,1)S(1)} custom-call(bf16[3,6,6,96,128]{4,3,2,1,0:T(8,128)(2,1)S(1)} %get-tuple-element.50.padded, bf16[4,4,96,128]{3,2,1,0:T(8,128)(2,1)S(1)} %bitcast.11, bf16[3456,256]{1,0:T(8,128)(2,1)S(1)} %copy-done, bf16[128,256]{1,0:T(8,128)(2,1)S(1)} %copy-done.4), custom_call_target="tpu_custom_call" | custom-call | flops 339738624 | tf_op jit(solution)/shard_map/pallas_call | solution.py:227
  21.4 1.1 %shard_map.99 = (f32[4,384,128]{2,1,0:T(8,128)S(1)}, f32[2,384,128]{2,1,0:T(8,128)S(1)}, f32[8,128]{1,0:T(8,128)S(1)}, bf16[784,128]{1,0:T(8,128)(2,1)S(1)}, bf16[4,4,96,256]{3,2,1,0:T(8,128)(2,1)}) custom-call(f32[4,384,128]{2,1,0:T(8,128)S(1)} %get-tuple-element.40.part_ref, ...), custom_call_target="tpu_custom_call", output_to_operand_aliasing={{4}: (8, {})} | custom-call | tf_op jit(solution)/shard_map/pallas_call | solution.py:534
  22.5 1.8 %collective-permute-start.5 = (bf16[784,128]{1,0:T(8,128)(2,1)S(1)}, bf16[784,128]{1,0:T(8,128)(2,1)S(1)}, u32[]{:S(2)}, u32[]{:S(2)}) collective-permute-start(bf16[784,128]{1,0:T(8,128)(2,1)S(1)} %get-tuple-element.60), channel_id=1, source_target_pairs={{0,1},{1,0},{2,3},{3,2},{4,5},{5,4},{6,7},{7,6},{8,9},{9,8},{10,11... | collective-permute-start | bytes 602120 | tf_op jit(solution)/shard_map/ppermute | solution.py:549
  24.3 0.0 collective-permute-done.2.a_ref
  24.3 1.3 %collective-permute-done.3.b_ref = bf16[4,224,128]{2,1,0:T(8,128)(2,1)S(1)} collective-permute-done((bf16[4,224,128]{2,1,0:T(8,128)(2,1)S(1)}, bf16[4,224,128]{2,1,0:T(8,128)(2,1)S(1)}, u32[]{:S(2)}, u32[]{:S(2)}) %collective-permute-start.3) | collective-permute-done | bytes 229408 | tf_op jit(solution)/shard_map/ppermute | solution.py:423
  25.6 0.3 collective-permute-done.4.c_ref
  26.0 0.1 shard_map.100
  26.1 3.7 %collective-permute-start.6 = (bf16[224,128]{1,0:T(8,128)(2,1)S(1)}, bf16[224,128]{1,0:T(8,128)(2,1)S(1)}, u32[]{:S(2)}, u32[]{:S(2)}) collective-permute-start(bf16[224,128]{1,0:T(8,128)(2,1)S(1)} %get-tuple-element.67), channel_id=1, source_target_pairs={{0,24},{1,25},{2,7},{3,6},{4,28},{5,29},{6,3},{7,2},{8,16},{9,17},... | collective-permute-start | bytes 172040 | tf_op jit(solution)/shard_map/ppermute | solution.py:423
  29.7 0.0 collective-permute-start.7
  29.7 0.8 %collective-permute-start.8 = (bf16[224,128]{1,0:T(8,128)(2,1)S(1)}, bf16[224,128]{1,0:T(8,128)(2,1)S(1)}, u32[]{:S(2)}, u32[]{:S(2)}) collective-permute-start(bf16[224,128]{1,0:T(8,128)(2,1)S(1)} %get-tuple-element.69), channel_id=1, source_target_pairs={{0,8},{1,9},{2,6},{3,7},{4,12},{5,13},{6,2},{7,3},{8,0},{9,1},{10,... | collective-permute-start | bytes 172040 | tf_op jit(solution)/shard_map/ppermute | solution.py:423
  30.5 0.0 collective-permute-done.5.after_ref
  30.5 1.2 %shard_map.101 = bf16[4,4,96,128]{3,2,1,0:T(8,128)(2,1)} custom-call(f32[4,384,128]{2,1,0:T(8,128)S(1)} %get-tuple-element.53.grad_ref, f32[2,384,128]{2,1,0:T(8,128)S(1)} %get-tuple-element.54.slope_ref, f32[8,128]{1,0:T(8,128)S(1)} %get-tuple-element.59.sums_ref, bf16[784,128]{1,0:T(8,128)(2,1)S(1)} %collective-permute-done.5.after_ref, ...), custom_call_target="tpu_custom_call" | custom-call | flops 135895456 | bytes 1572864 | tf_op jit(solution)/shard_map/pallas_call | solution.py:566
  31.7 0.4 %collective-permute-done.6.a_ref = bf16[224,128]{1,0:T(8,128)(2,1)S(1)} collective-permute-done((bf16[224,128]{1,0:T(8,128)(2,1)S(1)}, bf16[224,128]{1,0:T(8,128)(2,1)S(1)}, u32[]{:S(2)}, u32[]{:S(2)}) %collective-permute-start.6) | collective-permute-done | bytes 57376 | tf_op jit(solution)/shard_map/ppermute | solution.py:423
  32.1 2.7 %collective-permute-done.7.b_ref = bf16[224,128]{1,0:T(8,128)(2,1)S(1)} collective-permute-done((bf16[224,128]{1,0:T(8,128)(2,1)S(1)}, bf16[224,128]{1,0:T(8,128)(2,1)S(1)}, u32[]{:S(2)}, u32[]{:S(2)}) %collective-permute-start.7) | collective-permute-done | bytes 57376 | tf_op jit(solution)/shard_map/ppermute | solution.py:423
  34.8 0.0 collective-permute-done.8.c_ref
  34.8 0.7 %shard_map.102 = (f32[216,128]{1,0:T(8,128)}, f32[8,128]{1,0:T(8,128)}) custom-call(f32[224,128]{1,0:T(8,128)S(1)} %get-tuple-element.65.own_ref, bf16[224,128]{1,0:T(8,128)(2,1)S(1)} %collective-permute-done.6.a_ref, bf16[224,128]{1,0:T(8,128)(2,1)S(1)} %collective-permute-done.7.b_ref, bf16[224,128]{1,0:T(8,128)(2,1)S(1)} %collective-permute-done.8.c_ref), custom_call_target="tpu_custom_call" | custom-call | bytes 344064 | tf_op jit(solution)/shard_map/pallas_call | solution.py:455
Async XLA Ops:
  0.6 1.0 %copy-start.1 = (bf16[1,4,4,96,128]{4,3,2,1,0:T(8,128)(2,1)S(1)}, bf16[1,4,4,96,128]{4,3,2,1,0:T(8,128)(2,1)}, u32[]{:S(2)}) copy-start(bf16[1,4,4,96,128]{4,3,2,1,0:T(8,128)(2,1)} %param.6) | copy-start | bytes 1179652
  1.6 3.3 %copy-start = (bf16[3456,256]{1,0:T(8,128)(2,1)S(1)}, bf16[3456,256]{1,0:T(8,128)(2,1)}, u32[]{:S(2)}) copy-start(bf16[3456,256]{1,0:T(8,128)(2,1)} %weight_ref.5) | copy-start | bytes 5308420
  1.6 3.3 %copy-start.3 = (bf16[1,4,4,96,256]{4,3,2,1,0:T(8,128)(2,1)S(1)}, bf16[1,4,4,96,256]{4,3,2,1,0:T(8,128)(2,1)}, u32[]{:S(2)}) copy-start(bf16[1,4,4,96,256]{4,3,2,1,0:T(8,128)(2,1)} %param.11) | copy-start | bytes 2359300
  1.9 8.0 %collective-permute-start = (bf16[784,128]{1,0:T(8,128)(2,1)S(1)}, bf16[784,128]{1,0:T(8,128)(2,1)S(1)}, u32[]{:S(2)}, u32[]{:S(2)}) collective-permute-start(bf16[784,128]{1,0:T(8,128)(2,1)S(1)} %get-tuple-element.38), channel_id=1, source_target_pairs={{0,1},{1,0},{2,3},{3,2},{4,5},{5,4},{6,7},{7,6},{8,9},{9,8},{10,11... | collective-permute-start | bytes 602120 | tf_op jit(solution)/shard_map/ppermute | solution.py:489
  4.9 5.0 %copy-start.2 = (bf16[1,4,4,96,128]{4,3,2,1,0:T(8,128)(2,1)S(1)}, bf16[1,4,4,96,128]{4,3,2,1,0:T(8,128)(2,1)}, u32[]{:S(2)}) copy-start(bf16[1,4,4,96,128]{4,3,2,1,0:T(8,128)(2,1)} %param.6) | copy-start | bytes 1179652
  4.9 5.0 %copy-start.5 = (f32[128]{0:T(128)S(1)}, f32[128]{0:T(128)}, u32[]{:S(2)}) copy-start(f32[128]{0:T(128)} %param.7) | copy-start | bytes 1540
  4.9 5.0 %copy-start.6 = (f32[128]{0:T(128)S(1)}, f32[128]{0:T(128)}, u32[]{:S(2)}) copy-start(f32[128]{0:T(128)} %param.8) | copy-start | bytes 1540
  9.9 3.7 %copy-start.4 = (bf16[128,256]{1,0:T(8,128)(2,1)S(1)}, bf16[128,256]{1,0:T(8,128)(2,1)}, u32[]{:S(2)}) copy-start(bf16[128,256]{1,0:T(8,128)(2,1)} %short_ref.5) | copy-start | bytes 196612
  13.5 2.5 %collective-permute-start.1 = (bf16[2,8,224,128]{3,2,1,0:T(8,128)(2,1)S(1)}, bf16[2,8,224,128]{3,2,1,0:T(8,128)(2,1)S(1)}, u32[]{:S(2)}, u32[]{:S(2)}) collective-permute-start(bf16[2,8,224,128]{3,2,1,0:T(8,128)(2,1)S(1)} %get-tuple-element.47), channel_id=1, source_target_pairs={{0,2},{1,3},{2,0},{3,1},{4,6},{5,7},{6,4},{7,5},{8,10},{9,11},{10,... | collective-permute-start | bytes 2752520 | tf_op jit(solution)/shard_map/ppermute | solution.py:423
  16.2 8.1 %collective-permute-start.2 = (bf16[4,224,128]{2,1,0:T(8,128)(2,1)S(1)}, bf16[4,224,128]{2,1,0:T(8,128)(2,1)S(1)}, u32[]{:S(2)}, u32[]{:S(2)}) collective-permute-start(bf16[4,224,128]{2,1,0:T(8,128)(2,1)S(1)} %get-tuple-element.55), channel_id=1, source_target_pairs={{0,5},{1,4},{2,26},{3,27},{4,1},{5,0},{6,30},{7,31},{8,13},{9,12},... | collective-permute-start | bytes 688136 | tf_op jit(solution)/shard_map/ppermute | solution.py:423
  18.9 6.7 %collective-permute-start.3 = (bf16[4,224,128]{2,1,0:T(8,128)(2,1)S(1)}, bf16[4,224,128]{2,1,0:T(8,128)(2,1)S(1)}, u32[]{:S(2)}, u32[]{:S(2)}) collective-permute-start(bf16[4,224,128]{2,1,0:T(8,128)(2,1)S(1)} %get-tuple-element.56), channel_id=1, source_target_pairs={{0,1},{1,0},{2,18},{3,19},{4,5},{5,4},{6,22},{7,23},{8,9},{9,8},{1... | collective-permute-start | bytes 688136 | tf_op jit(solution)/shard_map/ppermute | solution.py:423
  19.4 6.5 %collective-permute-start.4 = (bf16[4,224,128]{2,1,0:T(8,128)(2,1)S(1)}, bf16[4,224,128]{2,1,0:T(8,128)(2,1)S(1)}, u32[]{:S(2)}, u32[]{:S(2)}) collective-permute-start(bf16[4,224,128]{2,1,0:T(8,128)(2,1)S(1)} %get-tuple-element.57), channel_id=1, source_target_pairs={{0,4},{1,5},{2,10},{3,11},{4,0},{5,1},{6,14},{7,15},{8,12},{9,13},... | collective-permute-start | bytes 688136 | tf_op jit(solution)/shard_map/ppermute | solution.py:423
  22.5 8.0 %collective-permute-start.5 = (bf16[784,128]{1,0:T(8,128)(2,1)S(1)}, bf16[784,128]{1,0:T(8,128)(2,1)S(1)}, u32[]{:S(2)}, u32[]{:S(2)}) collective-permute-start(bf16[784,128]{1,0:T(8,128)(2,1)S(1)} %get-tuple-element.60), channel_id=1, source_target_pairs={{0,1},{1,0},{2,3},{3,2},{4,5},{5,4},{6,7},{7,6},{8,9},{9,8},{10,11... | collective-permute-start | bytes 602120 | tf_op jit(solution)/shard_map/ppermute | solution.py:549
  26.1 6.0 %collective-permute-start.6 = (bf16[224,128]{1,0:T(8,128)(2,1)S(1)}, bf16[224,128]{1,0:T(8,128)(2,1)S(1)}, u32[]{:S(2)}, u32[]{:S(2)}) collective-permute-start(bf16[224,128]{1,0:T(8,128)(2,1)S(1)} %get-tuple-element.67), channel_id=1, source_target_pairs={{0,24},{1,25},{2,7},{3,6},{4,28},{5,29},{6,3},{7,2},{8,16},{9,17},... | collective-permute-start | bytes 172040 | tf_op jit(solution)/shard_map/ppermute | solution.py:423
  29.7 5.1 %collective-permute-start.7 = (bf16[224,128]{1,0:T(8,128)(2,1)S(1)}, bf16[224,128]{1,0:T(8,128)(2,1)S(1)}, u32[]{:S(2)}, u32[]{:S(2)}) collective-permute-start(bf16[224,128]{1,0:T(8,128)(2,1)S(1)} %get-tuple-element.68), channel_id=1, source_target_pairs={{0,16},{1,17},{2,3},{3,2},{4,20},{5,21},{6,7},{7,6},{8,24},{9,25},... | collective-permute-start | bytes 172040 | tf_op jit(solution)/shard_map/ppermute | solution.py:423
  29.7 5.1 %collective-permute-start.8 = (bf16[224,128]{1,0:T(8,128)(2,1)S(1)}, bf16[224,128]{1,0:T(8,128)(2,1)S(1)}, u32[]{:S(2)}, u32[]{:S(2)}) collective-permute-start(bf16[224,128]{1,0:T(8,128)(2,1)S(1)} %get-tuple-element.69), channel_id=1, source_target_pairs={{0,8},{1,9},{2,6},{3,7},{4,12},{5,13},{6,2},{7,3},{8,0},{9,1},{10,... | collective-permute-start | bytes 172040 | tf_op jit(solution)/shard_map/ppermute | solution.py:423

commit v6 on v5

--- a/solution.py
+++ b/solution.py
@@ -18,10 +18,10 @@
 bf16 = jnp.bfloat16
 
 
-def call(kernel, outs, scratch=(), flops=0, moved=0, in_specs=None, out_specs=None, aliases=None):
+def call(kernel, outs, scratch=(), flops=0, moved=0, in_specs=None, out_specs=None):
     specs = {} if in_specs is None else {"in_specs": in_specs}
     if out_specs is not None:
-        specs.update(out_specs=out_specs, input_output_aliases=aliases)
+        specs["out_specs"] = out_specs
     return pl.pallas_call(
         kernel,
         out_shape=outs,
@@ -66,21 +66,17 @@
     return jnp.concatenate(pieces + [zero], axis=0).astype(bf16)
 
 
-def start_kernel(clip_ref, stats_ref, parcel_ref):
-    frames, rows, cols, width = clip_ref.shape
-    places = rows * cols
+def start_kernel(clip_ref, stats_ref, last_ref):
+    frames = clip_ref.shape[0]
+    width = clip_ref.shape[-1]
     total = jnp.zeros((1, width), f32)
     square = jnp.zeros((1, width), f32)
     for frame in range(frames):
         value = clip_ref[frame].reshape(-1, width).astype(f32)
         total = total + column_totals(value)
         square = square + column_totals(value * value)
-    totals = group_totals(two_rows(total, square))
-    stats_ref[...] = totals
-    lead = KT - 1
-    for frame in range(lead):
-        parcel_ref[frame * places : (frame + 1) * places] = clip_ref[frames - lead + frame].reshape(places, width)
-    parcel_ref[lead * places :] = pieces_block(totals)
+    stats_ref[...] = group_totals(two_rows(total, square))
+    last_ref[...] = clip_ref[frames - last_ref.shape[0] :]
 
 
 def whole(parcel):
@@ -88,8 +84,8 @@
     return pieces[0:2] + (pieces[2:4] + pieces[4:6])
 
 
-def moments(stats, parcel, members):
-    totals = stats[0:2] + whole(parcel)
+def moments(stats, other, members):
+    totals = stats[0:2] + other[0:2]
     mean = totals[0:1] / members
     variance = totals[1:2] / members - mean * mean
     return mean, lax.rsqrt(variance + epsilon)
@@ -123,52 +119,79 @@
     return affine * jax.nn.sigmoid(affine)
 
 
-def fill_hidden(padded, clip_ref, parcel_ref, mean, inv, gain, bias, begin, stop):
-    frames, rows, cols, width = clip_ref.shape
-    places = rows * cols
-    lead = KT - 1
-    at_start = lax.axis_index("ctx") == 0
-    for frame in range(begin, stop):
-        if frame < lead:
-            before = parcel_ref[frame * places : (frame + 1) * places].reshape(rows, cols, width)
-            value = jnp.where(at_start, clip_ref[0].astype(f32), before.astype(f32))
-        else:
-            value = clip_ref[frame - lead].astype(f32)
-        place(padded, frame, hidden_of(value, mean, inv, gain, bias))
-
-
 def tap_block(padded, frames, rows, t, i):
     width = padded.shape[-1]
     return [padded[j, t : t + frames, i : i + rows].reshape(-1, width) for j in range(KS)]
 
 
-def weight_kernel(
+def groups_of_taps():
+    return ((0, 1), (2,))
+
+
+def weight_own_kernel(
+    members,
+    clip_ref, stats_ref, other_ref, gain_ref, bias_ref, cot_t_ref,
+    padded, early_ref, late_ref,
+):
+    frames, rows, cols, width = clip_ref.shape
+    mean, inv = moments(stats_ref, other_ref, members)
+    clear_edges(padded)
+    for frame in range(frames):
+        place(padded, frame, hidden_of(clip_ref[frame], mean, inv, gain_ref[...], bias_ref[...]))
+    per_frame = rows * cols
+    for t in range(KT - 1, -1, -1):
+        skipped = KT - 1 - t
+        cot_t = cot_t_ref[:, skipped * per_frame :]
+        base = row = t * KS * KS * width
+        for group in groups_of_taps():
+            parts = []
+            for i in group:
+                parts += tap_block(padded, frames - skipped, rows, 0, i)
+            if t == KT - 1 and group[-1] == KS - 1:
+                parts.append(clip_ref[...].reshape(-1, width))
+            part = jnp.dot(cot_t, jnp.concatenate(parts, axis=1), preferred_element_type=f32)
+            stop = row + part.shape[1]
+            if t == KT - 1:
+                late_ref[row - base : stop - base, :] = part.T
+            else:
+                early_ref[:, row:stop] = part
+            row = stop
+
+
+def weight_halo_kernel(
     members, split,
-    clip_ref, parcel_ref, stats_ref, gain_ref, bias_ref, cot_t_ref,
+    halo_ref, clip_ref, stats_ref, other_ref, gain_ref, bias_ref, cot_t_ref, early_ref, late_ref,
     padded, total, *rest,
 ):
-    frames, rows, cols, width = clip_ref.shape
-    mean, inv = moments(stats_ref, parcel_ref, members)
+    at_start = lax.axis_index("ctx") == 0
+    lead, rows, cols, width = halo_ref.shape
+    mean, inv = moments(stats_ref, other_ref, members)
     clear_edges(padded)
-    filled = 0
-    cot_t = cot_t_ref[...]
-    pieces = [(t, i) for t in range(KT) for i in range(KS)]
-    begin = 0
-    for at in range(0, len(pieces), 2):
-        parts = []
-        needed = pieces[at : at + 2][-1][0] + frames
-        fill_hidden(padded, clip_ref, parcel_ref, mean, inv, gain_ref[...], bias_ref[...], filled, needed)
-        filled = needed
-        for t, i in pieces[at : at + 2]:
-            parts += tap_block(padded, frames, rows, t, i)
-        if at + 2 > len(pieces):
-            parts.append(clip_ref[...].reshape(-1, width))
-        part = jnp.dot(cot_t, jnp.concatenate(parts, axis=1), preferred_element_type=f32).T
+    for frame in range(lead):
+        value = jnp.where(at_start, clip_ref[0].astype(f32), halo_ref[frame].astype(f32))
+        place(padded, frame, hidden_of(value, mean, inv, gain_ref[...], bias_ref[...]))
+    per_frame = rows * cols
+
+    def give(part, begin):
         if split is None:
             total[begin : begin + part.shape[0], :] = part
         else:
             scatter_rows(total, part, begin, split)
-        begin += part.shape[0]
+
+    give(late_ref[...], early_ref.shape[1])
+    row = 0
+    for t in range(KT - 1):
+        count = lead - t
+        for group in groups_of_taps():
+            parts = []
+            for i in group:
+                parts += tap_block(padded, count, rows, t, i)
+            part = jnp.dot(
+                cot_t_ref[:, : count * per_frame], jnp.concatenate(parts, axis=1), preferred_element_type=f32
+            )
+            stop = row + part.shape[1]
+            give((part + early_ref[:, row:stop]).T, row)
+            row = stop
     if split is not None:
         (send_ref,) = rest
         core = lax.rem(lax.axis_index("dp"), 2)
@@ -199,40 +222,20 @@
         row += count
 
 
-def forward_kernel(begin, padded, clip_ref, weight_ref, short_ref, *rest):
-    out_ref = rest[-1]
-    rows, cols, width = clip_ref.shape[1:]
-    for at in range(out_ref.shape[0]):
-        frame = begin + at
+def forward_kernel(padded_lead, padded, clip_ref, weight_ref, short_ref, out_ref):
+    frames, rows, cols, width = clip_ref.shape
+    lead = padded_lead.shape[1]
+    for frame in range(frames):
         parts = []
         for t in range(KT):
+            source, at = (padded_lead, frame + t) if frame + t < lead else (padded, frame + t - lead)
             for i in range(KS):
-                for j in range(KS):
-                    parts.append(padded[j, frame + t, i : i + rows].reshape(-1, width))
+                parts += tap_block(source, 1, rows, at, i)
         result = jnp.dot(jnp.concatenate(parts, axis=1), weight_ref[...], preferred_element_type=f32)
         result = result + jnp.dot(
             clip_ref[frame].reshape(-1, width), short_ref[...], preferred_element_type=f32
         )
-        out_ref[at] = result.astype(bf16).reshape(rows, cols, -1)
-
-
-def forward_half(half, hidden, clip, conv_weight, short_weight, whole_shape=False):
-    frames, height, breadth, _ = clip.shape
-    out_width = conv_weight.shape[1]
-    count = frames // 2
-    flops = 2 * conv_weight.size * count * height * breadth
-    vmem = pl.BlockSpec(memory_space=pltpu.VMEM)
-    block = (count, height, breadth, out_width)
-    at = half if whole_shape else 0
-    return pl.pallas_call(
-        functools.partial(forward_kernel, half * count),
-        out_shape=jax.ShapeDtypeStruct((frames if whole_shape else count,) + block[1:], bf16),
-        grid=(1,),
-        in_specs=[vmem] * 4,
-        out_specs=pl.BlockSpec(block, lambda step: (at, 0, 0, 0)),
-        compiler_params=pltpu.CompilerParams(vmem_limit_bytes=VMEM_BYTES),
-        cost_estimate=pl.CostEstimate(flops=flops // 4, bytes_accessed=0, transcendentals=0),
-    )(hidden, clip, conv_weight, short_weight)
+        out_ref[frame] = result.astype(bf16).reshape(rows, cols, -1)
 
 
 def back_weights(weight_ref, width, taps_t):
@@ -247,12 +250,6 @@
     return jnp.concatenate(bands, axis=0) if len(bands) > 1 else bands[0]
 
 
-def fill_cot(padded, cot_ref):
-    clear_edges(padded)
-    for frame in range(cot_ref.shape[0]):
-        place(padded, frame, cot_ref[frame].astype(f32))
-
-
 def spatial_block(padded, frame, rows):
     out_width = padded.shape[-1]
     parts = []
@@ -266,46 +263,54 @@
     return lax.dot_general(block, weights, (((1,), (1,)), ((), ())), preferred_element_type=f32)
 
 
-def back_kernel(cot_ref, weight_ref, out_ref, before_ref, cot_t_ref, padded):
-    frames, rows, cols, out_width = cot_ref.shape
-    width = out_ref.shape[-1]
+def back_products(begin, count, cot_ref, weight_ref, width, padded):
+    rows, cols, out_width = cot_ref.shape[1:]
+    clear_edges(padded)
+    late = back_weights(weight_ref, width, (2, 1))
+    early = back_weights(weight_ref, width, (0,))
+    products = []
+    for at in range(count):
+        place(padded, at, cot_ref[begin + at].astype(f32))
+        block = spatial_block(padded, at, rows)
+        both = back_dot(block, late)
+        products.append((both[:, :width], both[:, width:], back_dot(block, early)))
+    return products
+
+
+def back_first_kernel(cot_ref, weight_ref, out_ref, before_ref, cot_t_ref, padded):
+    out_width = cot_ref.shape[-1]
     at_start = lax.axis_index("ctx") == 0
     cot_t_ref[...] = cot_ref[...].reshape(-1, out_width).T
-    fill_cot(padded, cot_ref)
-    late = back_weights(weight_ref, width, (2, 1))
-    early = back_weights(weight_ref, width, (0,))
-    for frame in range(frames):
-        block = spatial_block(padded, frame, rows)
-        both = back_dot(block, late)
-        y2, y1 = both[:, :width], both[:, width:]
-        y0 = back_dot(block, early)
-        if frame == 0:
-            lead, next_lead = y0, y1
-            out_ref[0] = y2
-        else:
-            out_ref[frame] = y2
-            out_ref[frame - 1] += y1
-            if frame == 1:
-                next_lead = next_lead + y0
-                before_ref[0] = lead.astype(bf16)
-                before_ref[1] = next_lead.astype(bf16)
-                out_ref[0] += jnp.where(at_start, lead + next_lead, 0.0)
-            else:
-                out_ref[frame - 2] += y0
+    width = out_ref.shape[-1]
+    (a2, a1, a0), (b2, b1, b0) = back_products(0, 2, cot_ref, weight_ref, width, padded)
+    last = a1 + b0
+    before_ref[0] = a0.astype(bf16)
+    before_ref[1] = last.astype(bf16)
+    out_ref[0] = a2 + b1 + jnp.where(at_start, a0 + last, 0.0)
+    out_ref[1] = b2
+
+
+def back_second_kernel(cot_ref, weight_ref, first_ref, out_ref, padded):
+    width = out_ref.shape[-1]
+    frames = cot_ref.shape[0]
+    out_ref[0:2] = first_ref[...]
+    for frame, (same, one, two) in enumerate(back_products(2, frames - 2, cot_ref, weight_ref, width, padded), 2):
+        out_ref[frame] = same
+        out_ref[frame - 1] += one
+        out_ref[frame - 2] += two
 
 
 def activation_kernel(
     members,
-    part_ref, leading_ref, clip_ref, parcel_ref, stats_ref, gain_ref, bias_ref, half_ref, _,
+    part_ref, leading_ref, clip_ref, halo_ref, stats_ref, other_ref, gain_ref, bias_ref, forward_ref,
     grad_ref, slope_ref, sums_ref, out_ref, whole_ref, sem,
 ):
-    count = half_ref.shape[0]
-    copy = pltpu.make_async_copy(half_ref, whole_ref.at[pl.ds(whole_ref.shape[0] - count, count)], sem)
+    copy = pltpu.make_async_copy(forward_ref, whole_ref, sem)
     copy.start()
     frames, rows, cols, width = clip_ref.shape
     places = rows * cols
     gain = gain_ref[...]
-    mean, inv = moments(stats_ref, parcel_ref, members)
+    mean, inv = moments(stats_ref, other_ref, members)
 
     def standard_and_slope(value):
         standard = (value.astype(f32) - mean) * inv
@@ -318,7 +323,7 @@
     lead = leading_ref.shape[0]
     for frame in range(lead):
         here = slice(frame * places, (frame + 1) * places)
-        standard, slope = standard_and_slope(parcel_ref[here])
+        standard, slope = standard_and_slope(halo_ref[frame].reshape(-1, width))
         grad = leading_ref[frame].astype(f32) * slope
         total = total + column_totals(grad)
         cross = cross + column_totals(grad * standard)
@@ -342,7 +347,7 @@
 
 def finish_kernel(
     members,
-    grad_ref, slope_ref, sums_ref, after_ref, clip_ref, parcel_ref, stats_ref, cot_ref, short_ref,
+    grad_ref, slope_ref, sums_ref, after_ref, clip_ref, stats_ref, other_ref, cot_ref, short_ref,
     out_ref,
 ):
     frames, rows, cols, width = clip_ref.shape
@@ -350,7 +355,7 @@
     out_width = cot_ref.shape[-1]
     lead = slope_ref.shape[0]
     is_last = lax.axis_index("ctx") == lax.axis_size("ctx") - 1
-    mean, inv = moments(stats_ref, parcel_ref, members)
+    mean, inv = moments(stats_ref, other_ref, members)
     sums = sums_ref[0:2] + whole(after_ref)
     mean_grad = sums[0:1] / members
     mean_cross = sums[1:2] / members
@@ -477,31 +482,36 @@
     work = places * conv_all * out_width * 2
 
     lead = KT - 1
-    stats, parcel = call(
+    stats, last_clip = call(
         start_kernel,
-        [
-            jax.ShapeDtypeStruct((8, in_width), f32),
-            jax.ShapeDtypeStruct((lead * height * breadth + 16, in_width), bf16),
-        ],
+        [jax.ShapeDtypeStruct((8, in_width), f32), jax.ShapeDtypeStruct((lead,) + clip.shape[1:], bf16)],
         flops=work, moved=clip.size * 2,
     )(clip)
-    if ctx_size == 2:
-        before = lax.ppermute(parcel, "ctx", [(0, 1), (1, 0)])
-    else:
-        before = from_behind(clip[frames - lead :], "ctx", 1).reshape(-1, in_width)
-        before = jnp.concatenate([before, pieces_block(others_total(stats))], axis=0)
-
-    back_part, leading, cot_t = call(
-        back_kernel,
+    other = others_total(stats)
+    halo = from_behind(last_clip, "ctx", 1)
+
+    half_cot = pltpu.VMEM((KS, 2, height + 2, breadth, out_width), bf16)
+    first_part, leading, cot_t = call(
+        back_first_kernel,
         [
-            jax.ShapeDtypeStruct((frames, height * breadth, in_width), f32),
+            jax.ShapeDtypeStruct((2, height * breadth, in_width), f32),
             jax.ShapeDtypeStruct((lead, height * breadth, in_width), bf16),
             jax.ShapeDtypeStruct((out_width, places), bf16),
         ],
-        [pltpu.VMEM((KS, frames, height + 2, breadth, out_width), bf16)],
-        flops=2 * work, moved=conv_weight.size * 2,
+        [half_cot],
+        flops=work, moved=conv_weight.size * 2,
     )(cot, conv_weight)
-    before, back_part = lax.optimization_barrier((before, back_part))
+    padded = (KS, frames, height + 2, breadth, in_width)
+    late_at = (KT - 1) * KS * KS * in_width
+    hidden, early, late = call(
+        functools.partial(weight_own_kernel, members),
+        [
+            jax.ShapeDtypeStruct(padded, bf16),
+            jax.ShapeDtypeStruct((out_width, late_at), f32),
+            jax.ShapeDtypeStruct((conv_all + in_width - late_at, out_width), f32),
+        ],
+        flops=work, moved=cot.size * 2,
+    )(clip, stats, other, gain, bias, cot_t)
 
     staged = dp_size == 16 and ctx_size == 2
     conv_rows, short_rows = conv_all // dp_size, in_width // dp_size
@@ -516,35 +526,43 @@
     else:
         outs = [jax.ShapeDtypeStruct((conv_all + in_width, out_width), f32)]
         split = None
-    hidden, *parts = call(
-        functools.partial(weight_kernel, members, split),
-        [jax.ShapeDtypeStruct((KS, frames + lead, height + 2, breadth, in_width), bf16)] + outs,
-        flops=work, moved=cot.size * 2,
-    )(clip, before, stats, gain, bias, cot_t)
-
-    clip_out = forward_half(0, hidden, clip, conv_weight, short_weight, True)
+    hidden_lead, *parts = call(
+        functools.partial(weight_halo_kernel, members, split),
+        [jax.ShapeDtypeStruct((KS, lead) + padded[2:], bf16)] + outs,
+        flops=work // 3, moved=cot.size * 2,
+    )(halo, clip, stats, other, gain, bias, cot_t, early, late)
+
+    first_part, hidden_lead = lax.optimization_barrier((first_part, hidden_lead))
+    back_part = call(
+        back_second_kernel,
+        jax.ShapeDtypeStruct((frames, height * breadth, in_width), f32),
+        [half_cot],
+        flops=work // 4,
+    )(cot, conv_weight, first_part)
     if staged:
-        got, clip_out = lax.optimization_barrier((swap(parts[1], (1, 0), (1, 0)), clip_out))
+        got, back_part = lax.optimization_barrier((swap(parts[1], (1, 0), (1, 0)), back_part))
         keep, *sends = sort_first(parts[0], got)
         got = exchange(sends, 0)
         hidden, keep = lax.optimization_barrier((hidden, keep))
-    second_half = forward_half(1, hidden, clip, conv_weight, short_weight)
+    forward = call(
+        forward_kernel,
+        jax.ShapeDtypeStruct((frames, height, breadth, out_width), bf16),
+        flops=work // 4,
+    )(hidden_lead, hidden, clip, conv_weight, short_weight)
     anywhere, vmem = pl.BlockSpec(memory_space=pl.ANY), pl.BlockSpec(memory_space=pltpu.VMEM)
-    parcel_shape = jax.ShapeDtypeStruct((lead * height * breadth + 16, in_width), bf16)
     grad, slope, sums, parcel, clip_out = call(
         functools.partial(activation_kernel, members),
         [
             jax.ShapeDtypeStruct((frames, height * breadth, in_width), f32),
             jax.ShapeDtypeStruct((lead, height * breadth, in_width), f32),
             jax.ShapeDtypeStruct((8, in_width), f32),
-            parcel_shape,
-            jax.ShapeDtypeStruct(clip_out.shape, bf16),
+            jax.ShapeDtypeStruct((lead * height * breadth + 16, in_width), bf16),
+            jax.ShapeDtypeStruct(forward.shape, bf16),
         ],
         [pltpu.SemaphoreType.DMA],
-        in_specs=[vmem] * 8 + [anywhere],
+        in_specs=[vmem] * 9,
         out_specs=[vmem] * 4 + [anywhere],
-        aliases={8: 4},
-    )(back_part, leading, clip, before, stats, gain, bias, second_half, clip_out)
+    )(back_part, leading, clip, halo, stats, other, gain, bias, forward)
     if ctx_size == 2:
         after = lax.ppermute(parcel, "ctx", [(0, 1), (1, 0)])
     else:
@@ -567,7 +585,7 @@
         functools.partial(finish_kernel, members),
         jax.ShapeDtypeStruct((frames, height, breadth, in_width), bf16),
         flops=work // 20, moved=cot.size * 4,
-    )(grad, slope, sums, after, clip, before, stats, cot, short_weight)
+    )(grad, slope, sums, after, clip, stats, other, cot, short_weight)
     return (clip_out[None], clip_grad[None], conv_grad, short_grad)
 
 

time: 36.2 us -> 35.9 us (level); the launches traced: 35.5 us -> 35.6 us
  starting transfers between devices: 12.9 us -> 15.1 us
  waiting for transfers between devices: 5.88 us -> 3.85 us
    ppermute x1 -> x2, starting transfers between devices: 2.97 us -> 5.01 us  [the longest x1 2.97 us: others_total(): lax.ppermute(value, 'ctx', [(source, (source + step) % count) for source...]
    ppermute x7, waiting for transfers between devices: 4.77 us -> 2.81 us  [swap(): return lax.ppermute(value, ('dp', 'ctx'), pairs)]
    ppermute x1 -> x2, waiting for transfers between devices: 1.1 us -> 0.01 us  [the longest x1 0.01 us: others_total(): lax.ppermute(value, 'ctx', [(source, (source + step) % count) for source...]
    ppermute x1, waiting for transfers between devices: 0.01 us -> 1.03 us  [body(): after = lax.ppermute(parcel, 'ctx', [(0, 1), (1, 0)])]
    pallas_call x4 -> x5, Pallas kernels: 11.5 us -> 11.4 us  [the longest x1 3.18 us: body(): call(forward_kernel, jax.ShapeDtypeStruct((frames, height, breadth, out_w...]
  transfers between devices with their start and end apart: 9 -> 10, of which waited for: 5 -> 4; matrix products, arithmetic and copies ran while one was open for 0% -> 0% of each run, Pallas kernels for 29% -> 34%
where the time goes in v6:
time: 35.9 us; the launch traced here: 35.6 us
  starting transfers between devices  15.1 us (42%)
  Pallas kernels  14.9 us (42%)
  waiting for transfers between devices  3.85 us (11%)
  local copies, waits for them, and re-layouts  1.02 us (3%)
  between operations  0.79 us (2%)
    ppermute x7, starting transfers between devices, swap(): return lax.ppermute(value, ('dp', 'ctx'), pairs)  8.29 us
    pallas_call x1, Pallas kernels, body(): call(forward_kernel, jax.ShapeDtypeStruct((frames, height, breadth, out_w...  3.18 us
    ppermute x1, starting transfers between devices, others_total(): lax.ppermute(value, 'ctx', [(source, (source + step) % count) for source...  2.97 us
    ppermute x7, waiting for transfers between devices, swap(): return lax.ppermute(value, ('dp', 'ctx'), pairs)  2.81 us
    pallas_call x1, Pallas kernels, body(): call(functools.partial(weight_own_kernel, members), [jax.ShapeDtypeStruct...  2.67 us
    ppermute x1, starting transfers between devices, from_behind(): lax.ppermute(value, axis, [(source, source + steps) for source in range(i...  2.04 us
    pallas_call x1, Pallas kernels, body(): call(back_second_kernel, jax.ShapeDtypeStruct((frames, height * breadth,...  2.01 us
    pallas_call x1, Pallas kernels, body(): call(back_first_kernel, [jax.ShapeDtypeStruct((2, height * breadth, in_wi...  2 us
  transfers between devices with their start and end apart: 10, of which 4 were waited for; matrix products, arithmetic and copies ran while one was open for 0% of the time, Pallas kernels for 34%

profile of v6, /device:TPU:0, one launch (start us, length us, event | category | flops | bytes accessed | tf_op | source)
XLA Modules:
  0.0 35.6 jit_solution(8805481442321695644)
XLA Ops:
  0.6 0.0 copy-start.1
  0.6 1.0 %copy-done.1 = bf16[1,4,4,96,128]{4,3,2,1,0:T(8,128)(2,1)S(1)} copy-done((bf16[1,4,4,96,128]{4,3,2,1,0:T(8,128)(2,1)S(1)}, bf16[1,4,4,96,128]{4,3,2,1,0:T(8,128)(2,1)}, u32[]{:S(2)}) %copy-start.1) | copy-done | bytes 393240
  1.6 0.0 copy-start
  1.6 0.0 copy-start.3
  1.6 0.3 shard_map.93
  1.9 3.0 %collective-permute-start.1 = (f32[8,128]{1,0:T(8,128)S(1)}, f32[8,128]{1,0:T(8,128)S(1)}, u32[]{:S(2)}, u32[]{:S(2)}) collective-permute-start(f32[8,128]{1,0:T(8,128)S(1)} %get-tuple-element.42.stats_ref), channel_id=1, source_target_pairs={{0,1},{1,0},{2,3},{3,2},{4,5},{5,4},{6,7},{7,6},{8,9},{9,8},{10,11... | collective-permute-start | bytes 12296 | tf_op jit(solution)/shard_map/ppermute | solution.py:415
  4.9 2.0 %collective-permute-start = (bf16[2,4,96,128]{3,2,1,0:T(8,128)(2,1)S(1)}, bf16[2,4,96,128]{3,2,1,0:T(8,128)(2,1)S(1)}, u32[]{:S(2)}, u32[]{:S(2)}) collective-permute-start(bf16[2,4,96,128]{3,2,1,0:T(8,128)(2,1)S(1)} %get-tuple-element.41), channel_id=1, source_target_pairs={{0,1},{2,3},{4,5},{6,7},{8,9},{10,11},{12,13},{14,15},{16,17},{18,... | collective-permute-start | bytes 589832 | tf_op jit(solution)/shard_map/ppermute | solution.py:408
  6.9 0.0 copy-done
  7.0 0.0 copy-done.3
  7.0 0.0 copy-start.2
  7.0 0.0 copy-start.5
  7.0 0.0 copy-start.6
  7.0 2.0 %shard_map.94 = (f32[2,384,128]{2,1,0:T(8,128)S(1)}, bf16[2,384,128]{2,1,0:T(8,128)(2,1)S(1)}, bf16[256,1536]{1,0:T(8,128)(2,1)S(1)}) custom-call(bf16[4,4,96,256]{3,2,1,0:T(8,128)(2,1)S(1)} %bitcast.15, bf16[3456,256]{1,0:T(8,128)(2,1)S(1)} %copy-done), custom_call_target="tpu_custom_call" | custom-call | flops 2717908992 | bytes 1769472 | tf_op jit(solution)/shard_map/pallas_call | solution.py:494
  9.0 0.0 collective-permute-done.1.other_ref
  9.0 0.0 copy-done.2
  9.0 0.0 copy-done.5
  9.0 0.0 copy-done.6
  9.0 2.7 %shard_map.95 = (bf16[3,4,6,96,128]{4,3,2,1,0:T(8,128)(2,1)S(1)}, f32[256,2304]{1,0:T(8,128)S(1)}, f32[1280,256]{1,0:T(8,128)S(1)}) custom-call(bf16[4,4,96,128]{3,2,1,0:T(8,128)(2,1)S(1)} %bitcast.9, f32[8,128]{1,0:T(8,128)S(1)} %get-tuple-element.42.stats_ref, f32[8,128]{1,0:T(8,128)S(1)} %collective-permute-done.1.other_ref, f32[1,128]{1,0:T(1,128)S(1)} %bitcast.19, ...), custom_call_target="tpu_custom_call" | custom-call | flops 2717908992 | bytes 786432 | tf_op jit(solution)/shard_map/pallas_call | solution.py:506
  11.7 0.0 collective-permute-done.halo_ref
  11.7 1.5 %shard_map.96 = (bf16[3,2,6,96,128]{4,3,2,1,0:T(8,128)(2,1)S(1)}, f32[2,16,224,128]{3,2,1,0:T(8,128)S(1)}, bf16[2,8,224,128]{3,2,1,0:T(8,128)(2,1)S(1)}) custom-call(bf16[2,4,96,128]{3,2,1,0:T(8,128)(2,1)S(1)} %collective-permute-done.halo_ref, bf16[4,4,96,128]{3,2,1,0:T(8,128)(2,1)S(1)} %bitcast.10, f32[8,128]{1,0:T(8,128)S(1)} %get-tuple-element.42.stats_ref, ...), custom_call_target="tpu_custom_call" | custom-call | flops 905969664 | bytes 786432 | tf_op jit(solution)/shard_map/pallas_call | solution.py:529
  13.3 0.1 collective-permute-start.2
  13.4 2.0 %shard_map.97.part_ref = f32[4,384,128]{2,1,0:T(8,128)S(1)} custom-call(bf16[4,4,96,256]{3,2,1,0:T(8,128)(2,1)S(1)} %bitcast.16, bf16[3456,256]{1,0:T(8,128)(2,1)S(1)} %copy-done, f32[2,384,128]{2,1,0:T(8,128)S(1)} %get-tuple-element.49.first_ref), custom_call_target="tpu_custom_call" | custom-call | flops 679477248 | tf_op jit(solution)/shard_map/pallas_call | solution.py:536
  15.4 0.4 %collective-permute-done.2 = bf16[2,8,224,128]{3,2,1,0:T(8,128)(2,1)S(1)} collective-permute-done((bf16[2,8,224,128]{3,2,1,0:T(8,128)(2,1)S(1)}, bf16[2,8,224,128]{3,2,1,0:T(8,128)(2,1)S(1)}, u32[]{:S(2)}, u32[]{:S(2)}) %collective-permute-start.2) | collective-permute-done | bytes 917536 | tf_op jit(solution)/shard_map/ppermute | solution.py:428
  15.8 0.0 copy-start.4
  15.8 0.2 shard_map.98
  16.0 3.0 %collective-permute-start.3 = (bf16[4,224,128]{2,1,0:T(8,128)(2,1)S(1)}, bf16[4,224,128]{2,1,0:T(8,128)(2,1)S(1)}, u32[]{:S(2)}, u32[]{:S(2)}) collective-permute-start(bf16[4,224,128]{2,1,0:T(8,128)(2,1)S(1)} %get-tuple-element.61), channel_id=1, source_target_pairs={{0,5},{1,4},{2,26},{3,27},{4,1},{5,0},{6,30},{7,31},{8,13},{9,12},... | collective-permute-start | bytes 688136 | tf_op jit(solution)/shard_map/ppermute | solution.py:428
  19.1 0.4 %collective-permute-start.4 = (bf16[4,224,128]{2,1,0:T(8,128)(2,1)S(1)}, bf16[4,224,128]{2,1,0:T(8,128)(2,1)S(1)}, u32[]{:S(2)}, u32[]{:S(2)}) collective-permute-start(bf16[4,224,128]{2,1,0:T(8,128)(2,1)S(1)} %get-tuple-element.62), channel_id=1, source_target_pairs={{0,1},{1,0},{2,18},{3,19},{4,5},{5,4},{6,22},{7,23},{8,9},{9,8},{1... | collective-permute-start | bytes 688136 | tf_op jit(solution)/shard_map/ppermute | solution.py:428
  19.4 0.3 collective-permute-start.5
  19.7 0.0 copy-done.4
  19.7 3.2 %shard_map.99.forward_ref = bf16[4,4,96,256]{3,2,1,0:T(8,128)(2,1)S(1)} custom-call(bf16[3,2,6,96,128]{4,3,2,1,0:T(8,128)(2,1)S(1)} %get-tuple-element.52.padded_lead, bf16[3,4,6,96,128]{4,3,2,1,0:T(8,128)(2,1)S(1)} %get-tuple-element.57.padded, bf16[4,4,96,128]{3,2,1,0:T(8,128)(2,1)S(1)} %bitcast.11, bf16[3456,256]{1,0:T(8,128)(2,1)S(1)} %copy-done, ...), custom_call_target="tpu_custom_call" | custom-call | flops 679477248 | tf_op jit(solution)/shard_map/pallas_call | solution.py:547
  22.9 1.1 %shard_map.100 = (f32[4,384,128]{2,1,0:T(8,128)S(1)}, f32[2,384,128]{2,1,0:T(8,128)S(1)}, f32[8,128]{1,0:T(8,128)S(1)}, bf16[784,128]{1,0:T(8,128)(2,1)S(1)}, bf16[4,4,96,256]{3,2,1,0:T(8,128)(2,1)}) custom-call(f32[4,384,128]{2,1,0:T(8,128)S(1)} %shard_map.97.part_ref, bf16[2,384,128]{2,1,0:T(8,128)(2,1)S(1)} %get-tuple-element.51.leading_ref, ...), custom_call_target="tpu_custom_call" | custom-call | tf_op jit(solution)/shard_map/pallas_call | solution.py:553
  24.0 1.8 %collective-permute-start.6 = (bf16[784,128]{1,0:T(8,128)(2,1)S(1)}, bf16[784,128]{1,0:T(8,128)(2,1)S(1)}, u32[]{:S(2)}, u32[]{:S(2)}) collective-permute-start(bf16[784,128]{1,0:T(8,128)(2,1)S(1)} %get-tuple-element.66), channel_id=1, source_target_pairs={{0,1},{1,0},{2,3},{3,2},{4,5},{5,4},{6,7},{7,6},{8,9},{9,8},{10,11... | collective-permute-start | bytes 602120 | tf_op jit(solution)/shard_map/ppermute | solution.py:567
  25.7 0.0 collective-permute-done.3.a_ref
  25.7 0.0 collective-permute-done.4.b_ref
  25.8 0.1 collective-permute-done.5.c_ref
  25.9 0.1 shard_map.101
  26.0 3.9 %collective-permute-start.7 = (bf16[224,128]{1,0:T(8,128)(2,1)S(1)}, bf16[224,128]{1,0:T(8,128)(2,1)S(1)}, u32[]{:S(2)}, u32[]{:S(2)}) collective-permute-start(bf16[224,128]{1,0:T(8,128)(2,1)S(1)} %get-tuple-element.73), channel_id=1, source_target_pairs={{0,24},{1,25},{2,7},{3,6},{4,28},{5,29},{6,3},{7,2},{8,16},{9,17},... | collective-permute-start | bytes 172040 | tf_op jit(solution)/shard_map/ppermute | solution.py:428
  29.9 0.0 collective-permute-start.8
  29.9 0.6 %collective-permute-start.9 = (bf16[224,128]{1,0:T(8,128)(2,1)S(1)}, bf16[224,128]{1,0:T(8,128)(2,1)S(1)}, u32[]{:S(2)}, u32[]{:S(2)}) collective-permute-start(bf16[224,128]{1,0:T(8,128)(2,1)S(1)} %get-tuple-element.75), channel_id=1, source_target_pairs={{0,8},{1,9},{2,6},{3,7},{4,12},{5,13},{6,2},{7,3},{8,0},{9,1},{10,... | collective-permute-start | bytes 172040 | tf_op jit(solution)/shard_map/ppermute | solution.py:428
  30.5 1.0 %collective-permute-done.6.after_ref = bf16[784,128]{1,0:T(8,128)(2,1)S(1)} collective-permute-done((bf16[784,128]{1,0:T(8,128)(2,1)S(1)}, bf16[784,128]{1,0:T(8,128)(2,1)S(1)}, u32[]{:S(2)}, u32[]{:S(2)}) %collective-permute-start.6) | collective-permute-done | bytes 200736 | tf_op jit(solution)/shard_map/ppermute | solution.py:567
  31.5 1.1 %shard_map.102 = bf16[4,4,96,128]{3,2,1,0:T(8,128)(2,1)} custom-call(f32[4,384,128]{2,1,0:T(8,128)S(1)} %get-tuple-element.59.grad_ref, f32[2,384,128]{2,1,0:T(8,128)S(1)} %get-tuple-element.60.slope_ref, f32[8,128]{1,0:T(8,128)S(1)} %get-tuple-element.65.sums_ref, bf16[784,128]{1,0:T(8,128)(2,1)S(1)} %collective-permute-done.6.after_ref, ...), custom_call_target="tpu_custom_call" | custom-call | flops 135895456 | bytes 1572864 | tf_op jit(solution)/shard_map/pallas_call | solution.py:584
  32.7 0.0 collective-permute-done.7.a_ref
  32.7 2.3 %collective-permute-done.8.b_ref = bf16[224,128]{1,0:T(8,128)(2,1)S(1)} collective-permute-done((bf16[224,128]{1,0:T(8,128)(2,1)S(1)}, bf16[224,128]{1,0:T(8,128)(2,1)S(1)}, u32[]{:S(2)}, u32[]{:S(2)}) %collective-permute-start.8) | collective-permute-done | bytes 57376 | tf_op jit(solution)/shard_map/ppermute | solution.py:428
  34.9 0.0 collective-permute-done.9.c_ref
  34.9 0.7 %shard_map.103 = (f32[216,128]{1,0:T(8,128)}, f32[8,128]{1,0:T(8,128)}) custom-call(f32[224,128]{1,0:T(8,128)S(1)} %get-tuple-element.71.own_ref, bf16[224,128]{1,0:T(8,128)(2,1)S(1)} %collective-permute-done.7.a_ref, bf16[224,128]{1,0:T(8,128)(2,1)S(1)} %collective-permute-done.8.b_ref, bf16[224,128]{1,0:T(8,128)(2,1)S(1)} %collective-permute-done.9.c_ref), custom_call_target="tpu_custom_call" | custom-call | bytes 344064 | tf_op jit(solution)/shard_map/pallas_call | solution.py:460
Async XLA Ops:
  0.6 1.0 %copy-start.1 = (bf16[1,4,4,96,128]{4,3,2,1,0:T(8,128)(2,1)S(1)}, bf16[1,4,4,96,128]{4,3,2,1,0:T(8,128)(2,1)}, u32[]{:S(2)}) copy-start(bf16[1,4,4,96,128]{4,3,2,1,0:T(8,128)(2,1)} %param.6) | copy-start | bytes 1179652
  1.6 5.3 %copy-start = (bf16[3456,256]{1,0:T(8,128)(2,1)S(1)}, bf16[3456,256]{1,0:T(8,128)(2,1)}, u32[]{:S(2)}) copy-start(bf16[3456,256]{1,0:T(8,128)(2,1)} %weight_ref.5) | copy-start | bytes 5308420
  1.6 5.3 %copy-start.3 = (bf16[1,4,4,96,256]{4,3,2,1,0:T(8,128)(2,1)S(1)}, bf16[1,4,4,96,256]{4,3,2,1,0:T(8,128)(2,1)}, u32[]{:S(2)}) copy-start(bf16[1,4,4,96,256]{4,3,2,1,0:T(8,128)(2,1)} %param.11) | copy-start | bytes 2359300
  1.9 7.1 %collective-permute-start.1 = (f32[8,128]{1,0:T(8,128)S(1)}, f32[8,128]{1,0:T(8,128)S(1)}, u32[]{:S(2)}, u32[]{:S(2)}) collective-permute-start(f32[8,128]{1,0:T(8,128)S(1)} %get-tuple-element.42.stats_ref), channel_id=1, source_target_pairs={{0,1},{1,0},{2,3},{3,2},{4,5},{5,4},{6,7},{7,6},{8,9},{9,8},{10,11... | collective-permute-start | bytes 12296 | tf_op jit(solution)/shard_map/ppermute | solution.py:415
  4.9 6.8 %collective-permute-start = (bf16[2,4,96,128]{3,2,1,0:T(8,128)(2,1)S(1)}, bf16[2,4,96,128]{3,2,1,0:T(8,128)(2,1)S(1)}, u32[]{:S(2)}, u32[]{:S(2)}) collective-permute-start(bf16[2,4,96,128]{3,2,1,0:T(8,128)(2,1)S(1)} %get-tuple-element.41), channel_id=1, source_target_pairs={{0,1},{2,3},{4,5},{6,7},{8,9},{10,11},{12,13},{14,15},{16,17},{18,... | collective-permute-start | bytes 589832 | tf_op jit(solution)/shard_map/ppermute | solution.py:408
  7.0 2.1 %copy-start.2 = (bf16[1,4,4,96,128]{4,3,2,1,0:T(8,128)(2,1)S(1)}, bf16[1,4,4,96,128]{4,3,2,1,0:T(8,128)(2,1)}, u32[]{:S(2)}) copy-start(bf16[1,4,4,96,128]{4,3,2,1,0:T(8,128)(2,1)} %param.6) | copy-start | bytes 1179652
  7.0 2.1 %copy-start.5 = (f32[128]{0:T(128)S(1)}, f32[128]{0:T(128)}, u32[]{:S(2)}) copy-start(f32[128]{0:T(128)} %param.7) | copy-start | bytes 1540
  7.0 2.1 %copy-start.6 = (f32[128]{0:T(128)S(1)}, f32[128]{0:T(128)}, u32[]{:S(2)}) copy-start(f32[128]{0:T(128)} %param.8) | copy-start | bytes 1540
  13.3 2.5 %collective-permute-start.2 = (bf16[2,8,224,128]{3,2,1,0:T(8,128)(2,1)S(1)}, bf16[2,8,224,128]{3,2,1,0:T(8,128)(2,1)S(1)}, u32[]{:S(2)}, u32[]{:S(2)}) collective-permute-start(bf16[2,8,224,128]{3,2,1,0:T(8,128)(2,1)S(1)} %get-tuple-element.46), channel_id=1, source_target_pairs={{0,2},{1,3},{2,0},{3,1},{4,6},{5,7},{6,4},{7,5},{8,10},{9,11},{10,... | collective-permute-start | bytes 2752520 | tf_op jit(solution)/shard_map/ppermute | solution.py:428
  15.8 3.9 %copy-start.4 = (bf16[128,256]{1,0:T(8,128)(2,1)S(1)}, bf16[128,256]{1,0:T(8,128)(2,1)}, u32[]{:S(2)}) copy-start(bf16[128,256]{1,0:T(8,128)(2,1)} %short_ref.3) | copy-start | bytes 196612
  16.0 9.7 %collective-permute-start.3 = (bf16[4,224,128]{2,1,0:T(8,128)(2,1)S(1)}, bf16[4,224,128]{2,1,0:T(8,128)(2,1)S(1)}, u32[]{:S(2)}, u32[]{:S(2)}) collective-permute-start(bf16[4,224,128]{2,1,0:T(8,128)(2,1)S(1)} %get-tuple-element.61), channel_id=1, source_target_pairs={{0,5},{1,4},{2,26},{3,27},{4,1},{5,0},{6,30},{7,31},{8,13},{9,12},... | collective-permute-start | bytes 688136 | tf_op jit(solution)/shard_map/ppermute | solution.py:428
  19.1 6.7 %collective-permute-start.4 = (bf16[4,224,128]{2,1,0:T(8,128)(2,1)S(1)}, bf16[4,224,128]{2,1,0:T(8,128)(2,1)S(1)}, u32[]{:S(2)}, u32[]{:S(2)}) collective-permute-start(bf16[4,224,128]{2,1,0:T(8,128)(2,1)S(1)} %get-tuple-element.62), channel_id=1, source_target_pairs={{0,1},{1,0},{2,18},{3,19},{4,5},{5,4},{6,22},{7,23},{8,9},{9,8},{1... | collective-permute-start | bytes 688136 | tf_op jit(solution)/shard_map/ppermute | solution.py:428
  19.4 6.4 %collective-permute-start.5 = (bf16[4,224,128]{2,1,0:T(8,128)(2,1)S(1)}, bf16[4,224,128]{2,1,0:T(8,128)(2,1)S(1)}, u32[]{:S(2)}, u32[]{:S(2)}) collective-permute-start(bf16[4,224,128]{2,1,0:T(8,128)(2,1)S(1)} %get-tuple-element.63), channel_id=1, source_target_pairs={{0,4},{1,5},{2,10},{3,11},{4,0},{5,1},{6,14},{7,15},{8,12},{9,13},... | collective-permute-start | bytes 688136 | tf_op jit(solution)/shard_map/ppermute | solution.py:428
  24.0 7.5 %collective-permute-start.6 = (bf16[784,128]{1,0:T(8,128)(2,1)S(1)}, bf16[784,128]{1,0:T(8,128)(2,1)S(1)}, u32[]{:S(2)}, u32[]{:S(2)}) collective-permute-start(bf16[784,128]{1,0:T(8,128)(2,1)S(1)} %get-tuple-element.66), channel_id=1, source_target_pairs={{0,1},{1,0},{2,3},{3,2},{4,5},{5,4},{6,7},{7,6},{8,9},{9,8},{10,11... | collective-permute-start | bytes 602120 | tf_op jit(solution)/shard_map/ppermute | solution.py:567
  26.0 6.7 %collective-permute-start.7 = (bf16[224,128]{1,0:T(8,128)(2,1)S(1)}, bf16[224,128]{1,0:T(8,128)(2,1)S(1)}, u32[]{:S(2)}, u32[]{:S(2)}) collective-permute-start(bf16[224,128]{1,0:T(8,128)(2,1)S(1)} %get-tuple-element.73), channel_id=1, source_target_pairs={{0,24},{1,25},{2,7},{3,6},{4,28},{5,29},{6,3},{7,2},{8,16},{9,17},... | collective-permute-start | bytes 172040 | tf_op jit(solution)/shard_map/ppermute | solution.py:428
  29.9 5.1 %collective-permute-start.8 = (bf16[224,128]{1,0:T(8,128)(2,1)S(1)}, bf16[224,128]{1,0:T(8,128)(2,1)S(1)}, u32[]{:S(2)}, u32[]{:S(2)}) collective-permute-start(bf16[224,128]{1,0:T(8,128)(2,1)S(1)} %get-tuple-element.74), channel_id=1, source_target_pairs={{0,16},{1,17},{2,3},{3,2},{4,20},{5,21},{6,7},{7,6},{8,24},{9,25},... | collective-permute-start | bytes 172040 | tf_op jit(solution)/shard_map/ppermute | solution.py:428
  29.9 5.1 %collective-permute-start.9 = (bf16[224,128]{1,0:T(8,128)(2,1)S(1)}, bf16[224,128]{1,0:T(8,128)(2,1)S(1)}, u32[]{:S(2)}, u32[]{:S(2)}) collective-permute-start(bf16[224,128]{1,0:T(8,128)(2,1)S(1)} %get-tuple-element.75), channel_id=1, source_target_pairs={{0,8},{1,9},{2,6},{3,7},{4,12},{5,13},{6,2},{7,3},{8,0},{9,1},{10,... | collective-permute-start | bytes 172040 | tf_op jit(solution)/shard_map/ppermute | solution.py:428

commit v7 on v6

--- a/solution.py
+++ b/solution.py
@@ -290,7 +290,29 @@
     out_ref[1] = b2
 
 
-def back_second_kernel(cot_ref, weight_ref, first_ref, out_ref, padded):
+def slope_of(value, mean, inv, gain, bias):
+    standard = (value.astype(f32) - mean) * inv
+    affine = standard * gain + bias
+    logistic = jax.nn.sigmoid(affine)
+    return standard, logistic * (1.0 + affine * (1.0 - logistic)) * gain
+
+
+def back_second_kernel(
+    members,
+    cot_ref, weight_ref, first_ref, leading_ref, halo_ref, stats_ref, other_ref, gain_ref, bias_ref,
+    out_ref, share_ref, padded,
+):
+    mean, inv = moments(stats_ref, other_ref, members)
+    total = jnp.zeros((1, out_ref.shape[-1]), f32)
+    cross = total
+    for frame in range(leading_ref.shape[0]):
+        value = halo_ref[frame].reshape(-1, out_ref.shape[-1])
+        standard, slope = slope_of(value, mean, inv, gain_ref[...], bias_ref[...])
+        grad = leading_ref[frame].astype(f32) * slope
+        total = total + column_totals(grad)
+        cross = cross + column_totals(grad * standard)
+    at_start = lax.axis_index("ctx") == 0
+    share_ref[...] = jnp.where(at_start, 0.0, two_rows(total, cross))
     width = out_ref.shape[-1]
     frames = cot_ref.shape[0]
     out_ref[0:2] = first_ref[...]
@@ -302,7 +324,7 @@
 
 def activation_kernel(
     members,
-    part_ref, leading_ref, clip_ref, halo_ref, stats_ref, other_ref, gain_ref, bias_ref, forward_ref,
+    part_ref, share_ref, leading_ref, clip_ref, stats_ref, other_ref, gain_ref, bias_ref, forward_ref,
     grad_ref, slope_ref, sums_ref, out_ref, whole_ref, sem,
 ):
     copy = pltpu.make_async_copy(forward_ref, whole_ref, sem)
@@ -312,27 +334,13 @@
     gain = gain_ref[...]
     mean, inv = moments(stats_ref, other_ref, members)
 
-    def standard_and_slope(value):
-        standard = (value.astype(f32) - mean) * inv
-        affine = standard * gain + bias_ref[...]
-        logistic = jax.nn.sigmoid(affine)
-        return standard, logistic * (1.0 + affine * (1.0 - logistic)) * gain
-
-    total = jnp.zeros((1, width), f32)
-    cross = jnp.zeros((1, width), f32)
+    total = share_ref[0:1]
+    cross = share_ref[1:2]
     lead = leading_ref.shape[0]
     for frame in range(lead):
-        here = slice(frame * places, (frame + 1) * places)
-        standard, slope = standard_and_slope(halo_ref[frame].reshape(-1, width))
-        grad = leading_ref[frame].astype(f32) * slope
-        total = total + column_totals(grad)
-        cross = cross + column_totals(grad * standard)
-        out_ref[here] = leading_ref[frame]
-    at_start = lax.axis_index("ctx") == 0
-    total = jnp.where(at_start, 0.0, total)
-    cross = jnp.where(at_start, 0.0, cross)
+        out_ref[frame * places : (frame + 1) * places] = leading_ref[frame]
     for frame in range(frames):
-        standard, slope = standard_and_slope(clip_ref[frame].reshape(-1, width))
+        standard, slope = slope_of(clip_ref[frame].reshape(-1, width), mean, inv, gain, bias_ref[...])
         grad = part_ref[frame] * slope
         grad_ref[frame] = grad
         if frame >= frames - lead:
@@ -533,12 +541,15 @@
     )(halo, clip, stats, other, gain, bias, cot_t, early, late)
 
     first_part, hidden_lead = lax.optimization_barrier((first_part, hidden_lead))
-    back_part = call(
-        back_second_kernel,
-        jax.ShapeDtypeStruct((frames, height * breadth, in_width), f32),
+    back_part, share = call(
+        functools.partial(back_second_kernel, members),
+        [
+            jax.ShapeDtypeStruct((frames, height * breadth, in_width), f32),
+            jax.ShapeDtypeStruct((8, in_width), f32),
+        ],
         [half_cot],
         flops=work // 4,
-    )(cot, conv_weight, first_part)
+    )(cot, conv_weight, first_part, leading, halo, stats, other, gain, bias)
     if staged:
         got, back_part = lax.optimization_barrier((swap(parts[1], (1, 0), (1, 0)), back_part))
         keep, *sends = sort_first(parts[0], got)
@@ -562,7 +573,7 @@
         [pltpu.SemaphoreType.DMA],
         in_specs=[vmem] * 9,
         out_specs=[vmem] * 4 + [anywhere],
-    )(back_part, leading, clip, halo, stats, other, gain, bias, forward)
+    )(back_part, share, leading, clip, stats, other, gain, bias, forward)
     if ctx_size == 2:
         after = lax.ppermute(parcel, "ctx", [(0, 1), (1, 0)])
     else:

time: 35.9 us -> 36.1 us (level)
  no operation moved by 1% of the time
where the time goes in v7:
time: 36.1 us; the launch traced here: 35.6 us
  Pallas kernels  15 us (42%)
  starting transfers between devices  15 us (42%)
  waiting for transfers between devices  3.79 us (10%)
  local copies, waits for them, and re-layouts  1.02 us (3%)
  between operations  0.79 us (2%)
    ppermute x7, starting transfers between devices, swap(): return lax.ppermute(value, ('dp', 'ctx'), pairs)  8.28 us
    pallas_call x1, Pallas kernels, body(): call(forward_kernel, jax.ShapeDtypeStruct((frames, height, breadth, out_w...  3.18 us
    ppermute x1, starting transfers between devices, others_total(): lax.ppermute(value, 'ctx', [(source, (source + step) % count) for source...  2.97 us
    ppermute x7, waiting for transfers between devices, swap(): return lax.ppermute(value, ('dp', 'ctx'), pairs)  2.77 us
    pallas_call x1, Pallas kernels, body(): call(functools.partial(weight_own_kernel, members), [jax.ShapeDtypeStruct...  2.67 us
    pallas_call x1, Pallas kernels, body(): call(functools.partial(back_second_kernel, members), [jax.ShapeDtypeStruc...  2.23 us
    ppermute x1, starting transfers between devices, from_behind(): lax.ppermute(value, axis, [(source, source + steps) for source in range(i...  2.04 us
    pallas_call x1, Pallas kernels, body(): call(back_first_kernel, [jax.ShapeDtypeStruct((2, height * breadth, in_wi...  2 us
  transfers between devices with their start and end apart: 10, of which 4 were waited for; matrix products, arithmetic and copies ran while one was open for 0% of the time, Pallas kernels for 34%

profile of v7, /device:TPU:0, one launch (start us, length us, event | category | flops | bytes accessed | tf_op | source)
XLA Modules:
  0.0 35.6 jit_solution(3384832345754566812)
XLA Ops:
  0.6 0.0 copy-start.1
  0.6 1.0 %copy-done.1 = bf16[1,4,4,96,128]{4,3,2,1,0:T(8,128)(2,1)S(1)} copy-done((bf16[1,4,4,96,128]{4,3,2,1,0:T(8,128)(2,1)S(1)}, bf16[1,4,4,96,128]{4,3,2,1,0:T(8,128)(2,1)}, u32[]{:S(2)}) %copy-start.1) | copy-done | bytes 393240
  1.6 0.0 copy-start
  1.6 0.0 copy-start.3
  1.6 0.3 shard_map.93
  1.9 3.0 %collective-permute-start.1 = (f32[8,128]{1,0:T(8,128)S(1)}, f32[8,128]{1,0:T(8,128)S(1)}, u32[]{:S(2)}, u32[]{:S(2)}) collective-permute-start(f32[8,128]{1,0:T(8,128)S(1)} %get-tuple-element.44.stats_ref), channel_id=1, source_target_pairs={{0,1},{1,0},{2,3},{3,2},{4,5},{5,4},{6,7},{7,6},{8,9},{9,8},{10,11... | collective-permute-start | bytes 12296 | tf_op jit(solution)/shard_map/ppermute | solution.py:423
  4.9 2.0 %collective-permute-start = (bf16[2,4,96,128]{3,2,1,0:T(8,128)(2,1)S(1)}, bf16[2,4,96,128]{3,2,1,0:T(8,128)(2,1)S(1)}, u32[]{:S(2)}, u32[]{:S(2)}) collective-permute-start(bf16[2,4,96,128]{3,2,1,0:T(8,128)(2,1)S(1)} %get-tuple-element.43), channel_id=1, source_target_pairs={{0,1},{2,3},{4,5},{6,7},{8,9},{10,11},{12,13},{14,15},{16,17},{18,... | collective-permute-start | bytes 589832 | tf_op jit(solution)/shard_map/ppermute | solution.py:416
  6.9 0.0 copy-done
  7.0 0.0 copy-done.3
  7.0 0.0 copy-start.2
  7.0 0.0 copy-start.5
  7.0 0.0 copy-start.6
  7.0 2.0 %shard_map.94 = (f32[2,384,128]{2,1,0:T(8,128)S(1)}, bf16[2,384,128]{2,1,0:T(8,128)(2,1)S(1)}, bf16[256,1536]{1,0:T(8,128)(2,1)S(1)}) custom-call(bf16[4,4,96,256]{3,2,1,0:T(8,128)(2,1)S(1)} %bitcast.15, bf16[3456,256]{1,0:T(8,128)(2,1)S(1)} %copy-done), custom_call_target="tpu_custom_call" | custom-call | flops 2717908992 | bytes 1769472 | tf_op jit(solution)/shard_map/pallas_call | solution.py:502
  9.0 0.0 collective-permute-done.1.other_ref
  9.0 0.0 copy-done.2
  9.0 0.0 copy-done.5
  9.0 0.0 copy-done.6
  9.0 2.7 %shard_map.95 = (bf16[3,4,6,96,128]{4,3,2,1,0:T(8,128)(2,1)S(1)}, f32[256,2304]{1,0:T(8,128)S(1)}, f32[1280,256]{1,0:T(8,128)S(1)}) custom-call(bf16[4,4,96,128]{3,2,1,0:T(8,128)(2,1)S(1)} %bitcast.9, f32[8,128]{1,0:T(8,128)S(1)} %get-tuple-element.44.stats_ref, f32[8,128]{1,0:T(8,128)S(1)} %collective-permute-done.1.other_ref, f32[1,128]{1,0:T(1,128)S(1)} %bitcast.19, ...), custom_call_target="tpu_custom_call" | custom-call | flops 2717908992 | bytes 786432 | tf_op jit(solution)/shard_map/pallas_call | solution.py:514
  11.7 0.0 collective-permute-done.halo_ref
  11.7 1.5 %shard_map.96 = (bf16[3,2,6,96,128]{4,3,2,1,0:T(8,128)(2,1)S(1)}, f32[2,16,224,128]{3,2,1,0:T(8,128)S(1)}, bf16[2,8,224,128]{3,2,1,0:T(8,128)(2,1)S(1)}) custom-call(bf16[2,4,96,128]{3,2,1,0:T(8,128)(2,1)S(1)} %collective-permute-done.halo_ref, bf16[4,4,96,128]{3,2,1,0:T(8,128)(2,1)S(1)} %bitcast.10, f32[8,128]{1,0:T(8,128)S(1)} %get-tuple-element.44.stats_ref, ...), custom_call_target="tpu_custom_call" | custom-call | flops 905969664 | bytes 786432 | tf_op jit(solution)/shard_map/pallas_call | solution.py:537
  13.3 0.1 collective-permute-start.2
  13.4 2.2 %shard_map.97 = (f32[4,384,128]{2,1,0:T(8,128)S(1)}, f32[8,128]{1,0:T(8,128)S(1)}) custom-call(bf16[4,4,96,256]{3,2,1,0:T(8,128)(2,1)S(1)} %bitcast.16, bf16[3456,256]{1,0:T(8,128)(2,1)S(1)} %copy-done, f32[2,384,128]{2,1,0:T(8,128)S(1)} %get-tuple-element.51.first_ref, bf16[2,384,128]{2,1,0:T(8,128)(2,1)S(1)} %get-tuple-element.52.leading_ref, ...), custom_call_target="tpu_custom_call" | custom-call | flops 679477248 | tf_op jit(solution)/shard_map/pallas_call | solution.py:544
  15.6 0.2 collective-permute-done.2
  15.8 0.0 copy-start.4
  15.8 0.2 shard_map.98
  16.0 3.0 %collective-permute-start.3 = (bf16[4,224,128]{2,1,0:T(8,128)(2,1)S(1)}, bf16[4,224,128]{2,1,0:T(8,128)(2,1)S(1)}, u32[]{:S(2)}, u32[]{:S(2)}) collective-permute-start(bf16[4,224,128]{2,1,0:T(8,128)(2,1)S(1)} %get-tuple-element.65), channel_id=1, source_target_pairs={{0,5},{1,4},{2,26},{3,27},{4,1},{5,0},{6,30},{7,31},{8,13},{9,12},... | collective-permute-start | bytes 688136 | tf_op jit(solution)/shard_map/ppermute | solution.py:436
  19.1 0.4 %collective-permute-start.4 = (bf16[4,224,128]{2,1,0:T(8,128)(2,1)S(1)}, bf16[4,224,128]{2,1,0:T(8,128)(2,1)S(1)}, u32[]{:S(2)}, u32[]{:S(2)}) collective-permute-start(bf16[4,224,128]{2,1,0:T(8,128)(2,1)S(1)} %get-tuple-element.66), channel_id=1, source_target_pairs={{0,1},{1,0},{2,18},{3,19},{4,5},{5,4},{6,22},{7,23},{8,9},{9,8},{1... | collective-permute-start | bytes 688136 | tf_op jit(solution)/shard_map/ppermute | solution.py:436
  19.4 0.3 collective-permute-start.5
  19.7 0.0 copy-done.4
  19.7 3.2 %shard_map.99.forward_ref = bf16[4,4,96,256]{3,2,1,0:T(8,128)(2,1)S(1)} custom-call(bf16[3,2,6,96,128]{4,3,2,1,0:T(8,128)(2,1)S(1)} %get-tuple-element.56.padded_lead, bf16[3,4,6,96,128]{4,3,2,1,0:T(8,128)(2,1)S(1)} %get-tuple-element.61.padded, bf16[4,4,96,128]{3,2,1,0:T(8,128)(2,1)S(1)} %bitcast.11, bf16[3456,256]{1,0:T(8,128)(2,1)S(1)} %copy-done, ...), custom_call_target="tpu_custom_call" | custom-call | flops 679477248 | tf_op jit(solution)/shard_map/pallas_call | solution.py:558
  22.9 0.9 %shard_map.100 = (f32[4,384,128]{2,1,0:T(8,128)S(1)}, f32[2,384,128]{2,1,0:T(8,128)S(1)}, f32[8,128]{1,0:T(8,128)S(1)}, bf16[784,128]{1,0:T(8,128)(2,1)S(1)}, bf16[4,4,96,256]{3,2,1,0:T(8,128)(2,1)}) custom-call(f32[4,384,128]{2,1,0:T(8,128)S(1)} %get-tuple-element.54.part_ref, f32[8,128]{1,0:T(8,128)S(1)} %get-tuple-element.55.share_ref, ...), custom_call_target="tpu_custom_call" | custom-call | tf_op jit(solution)/shard_map/pallas_call | solution.py:564
  23.8 1.8 %collective-permute-start.6 = (bf16[784,128]{1,0:T(8,128)(2,1)S(1)}, bf16[784,128]{1,0:T(8,128)(2,1)S(1)}, u32[]{:S(2)}, u32[]{:S(2)}) collective-permute-start(bf16[784,128]{1,0:T(8,128)(2,1)S(1)} %get-tuple-element.70), channel_id=1, source_target_pairs={{0,1},{1,0},{2,3},{3,2},{4,5},{5,4},{6,7},{7,6},{8,9},{9,8},{10,11... | collective-permute-start | bytes 602120 | tf_op jit(solution)/shard_map/ppermute | solution.py:578
  25.5 0.0 collective-permute-done.3.a_ref
  25.5 0.0 collective-permute-done.4.b_ref
  25.5 0.3 collective-permute-done.5.c_ref
  25.9 0.1 shard_map.101
  26.0 3.9 %collective-permute-start.7 = (bf16[224,128]{1,0:T(8,128)(2,1)S(1)}, bf16[224,128]{1,0:T(8,128)(2,1)S(1)}, u32[]{:S(2)}, u32[]{:S(2)}) collective-permute-start(bf16[224,128]{1,0:T(8,128)(2,1)S(1)} %get-tuple-element.77), channel_id=1, source_target_pairs={{0,24},{1,25},{2,7},{3,6},{4,28},{5,29},{6,3},{7,2},{8,16},{9,17},... | collective-permute-start | bytes 172040 | tf_op jit(solution)/shard_map/ppermute | solution.py:436
  29.9 0.0 collective-permute-start.8
  29.9 0.6 %collective-permute-start.9 = (bf16[224,128]{1,0:T(8,128)(2,1)S(1)}, bf16[224,128]{1,0:T(8,128)(2,1)S(1)}, u32[]{:S(2)}, u32[]{:S(2)}) collective-permute-start(bf16[224,128]{1,0:T(8,128)(2,1)S(1)} %get-tuple-element.79), channel_id=1, source_target_pairs={{0,8},{1,9},{2,6},{3,7},{4,12},{5,13},{6,2},{7,3},{8,0},{9,1},{10,... | collective-permute-start | bytes 172040 | tf_op jit(solution)/shard_map/ppermute | solution.py:436
  30.5 1.0 %collective-permute-done.6.after_ref = bf16[784,128]{1,0:T(8,128)(2,1)S(1)} collective-permute-done((bf16[784,128]{1,0:T(8,128)(2,1)S(1)}, bf16[784,128]{1,0:T(8,128)(2,1)S(1)}, u32[]{:S(2)}, u32[]{:S(2)}) %collective-permute-start.6) | collective-permute-done | bytes 200736 | tf_op jit(solution)/shard_map/ppermute | solution.py:578
  31.5 1.2 %shard_map.102 = bf16[4,4,96,128]{3,2,1,0:T(8,128)(2,1)} custom-call(f32[4,384,128]{2,1,0:T(8,128)S(1)} %get-tuple-element.63.grad_ref, f32[2,384,128]{2,1,0:T(8,128)S(1)} %get-tuple-element.64.slope_ref, f32[8,128]{1,0:T(8,128)S(1)} %get-tuple-element.69.sums_ref, bf16[784,128]{1,0:T(8,128)(2,1)S(1)} %collective-permute-done.6.after_ref, ...), custom_call_target="tpu_custom_call" | custom-call | flops 135895456 | bytes 1572864 | tf_op jit(solution)/shard_map/pallas_call | solution.py:595
  32.7 0.0 collective-permute-done.7.a_ref
  32.7 2.2 %collective-permute-done.8.b_ref = bf16[224,128]{1,0:T(8,128)(2,1)S(1)} collective-permute-done((bf16[224,128]{1,0:T(8,128)(2,1)S(1)}, bf16[224,128]{1,0:T(8,128)(2,1)S(1)}, u32[]{:S(2)}, u32[]{:S(2)}) %collective-permute-start.8) | collective-permute-done | bytes 57376 | tf_op jit(solution)/shard_map/ppermute | solution.py:436
  34.9 0.0 collective-permute-done.9.c_ref
  34.9 0.7 %shard_map.103 = (f32[216,128]{1,0:T(8,128)}, f32[8,128]{1,0:T(8,128)}) custom-call(f32[224,128]{1,0:T(8,128)S(1)} %get-tuple-element.75.own_ref, bf16[224,128]{1,0:T(8,128)(2,1)S(1)} %collective-permute-done.7.a_ref, bf16[224,128]{1,0:T(8,128)(2,1)S(1)} %collective-permute-done.8.b_ref, bf16[224,128]{1,0:T(8,128)(2,1)S(1)} %collective-permute-done.9.c_ref), custom_call_target="tpu_custom_call" | custom-call | bytes 344064 | tf_op jit(solution)/shard_map/pallas_call | solution.py:468
Async XLA Ops:
  0.6 1.0 %copy-start.1 = (bf16[1,4,4,96,128]{4,3,2,1,0:T(8,128)(2,1)S(1)}, bf16[1,4,4,96,128]{4,3,2,1,0:T(8,128)(2,1)}, u32[]{:S(2)}) copy-start(bf16[1,4,4,96,128]{4,3,2,1,0:T(8,128)(2,1)} %param.6) | copy-start | bytes 1179652
  1.6 5.3 %copy-start = (bf16[3456,256]{1,0:T(8,128)(2,1)S(1)}, bf16[3456,256]{1,0:T(8,128)(2,1)}, u32[]{:S(2)}) copy-start(bf16[3456,256]{1,0:T(8,128)(2,1)} %weight_ref.5) | copy-start | bytes 5308420
  1.6 5.3 %copy-start.3 = (bf16[1,4,4,96,256]{4,3,2,1,0:T(8,128)(2,1)S(1)}, bf16[1,4,4,96,256]{4,3,2,1,0:T(8,128)(2,1)}, u32[]{:S(2)}) copy-start(bf16[1,4,4,96,256]{4,3,2,1,0:T(8,128)(2,1)} %param.11) | copy-start | bytes 2359300
  1.9 7.1 %collective-permute-start.1 = (f32[8,128]{1,0:T(8,128)S(1)}, f32[8,128]{1,0:T(8,128)S(1)}, u32[]{:S(2)}, u32[]{:S(2)}) collective-permute-start(f32[8,128]{1,0:T(8,128)S(1)} %get-tuple-element.44.stats_ref), channel_id=1, source_target_pairs={{0,1},{1,0},{2,3},{3,2},{4,5},{5,4},{6,7},{7,6},{8,9},{9,8},{10,11... | collective-permute-start | bytes 12296 | tf_op jit(solution)/shard_map/ppermute | solution.py:423
  4.9 6.8 %collective-permute-start = (bf16[2,4,96,128]{3,2,1,0:T(8,128)(2,1)S(1)}, bf16[2,4,96,128]{3,2,1,0:T(8,128)(2,1)S(1)}, u32[]{:S(2)}, u32[]{:S(2)}) collective-permute-start(bf16[2,4,96,128]{3,2,1,0:T(8,128)(2,1)S(1)} %get-tuple-element.43), channel_id=1, source_target_pairs={{0,1},{2,3},{4,5},{6,7},{8,9},{10,11},{12,13},{14,15},{16,17},{18,... | collective-permute-start | bytes 589832 | tf_op jit(solution)/shard_map/ppermute | solution.py:416
  7.0 2.1 %copy-start.2 = (bf16[1,4,4,96,128]{4,3,2,1,0:T(8,128)(2,1)S(1)}, bf16[1,4,4,96,128]{4,3,2,1,0:T(8,128)(2,1)}, u32[]{:S(2)}) copy-start(bf16[1,4,4,96,128]{4,3,2,1,0:T(8,128)(2,1)} %param.6) | copy-start | bytes 1179652
  7.0 2.1 %copy-start.5 = (f32[128]{0:T(128)S(1)}, f32[128]{0:T(128)}, u32[]{:S(2)}) copy-start(f32[128]{0:T(128)} %param.7) | copy-start | bytes 1540
  7.0 2.1 %copy-start.6 = (f32[128]{0:T(128)S(1)}, f32[128]{0:T(128)}, u32[]{:S(2)}) copy-start(f32[128]{0:T(128)} %param.8) | copy-start | bytes 1540
  13.3 2.5 %collective-permute-start.2 = (bf16[2,8,224,128]{3,2,1,0:T(8,128)(2,1)S(1)}, bf16[2,8,224,128]{3,2,1,0:T(8,128)(2,1)S(1)}, u32[]{:S(2)}, u32[]{:S(2)}) collective-permute-start(bf16[2,8,224,128]{3,2,1,0:T(8,128)(2,1)S(1)} %get-tuple-element.48), channel_id=1, source_target_pairs={{0,2},{1,3},{2,0},{3,1},{4,6},{5,7},{6,4},{7,5},{8,10},{9,11},{10,... | collective-permute-start | bytes 2752520 | tf_op jit(solution)/shard_map/ppermute | solution.py:436
  15.8 3.9 %copy-start.4 = (bf16[128,256]{1,0:T(8,128)(2,1)S(1)}, bf16[128,256]{1,0:T(8,128)(2,1)}, u32[]{:S(2)}) copy-start(bf16[128,256]{1,0:T(8,128)(2,1)} %short_ref.3) | copy-start | bytes 196612
  16.0 9.5 %collective-permute-start.3 = (bf16[4,224,128]{2,1,0:T(8,128)(2,1)S(1)}, bf16[4,224,128]{2,1,0:T(8,128)(2,1)S(1)}, u32[]{:S(2)}, u32[]{:S(2)}) collective-permute-start(bf16[4,224,128]{2,1,0:T(8,128)(2,1)S(1)} %get-tuple-element.65), channel_id=1, source_target_pairs={{0,5},{1,4},{2,26},{3,27},{4,1},{5,0},{6,30},{7,31},{8,13},{9,12},... | collective-permute-start | bytes 688136 | tf_op jit(solution)/shard_map/ppermute | solution.py:436
  19.1 6.5 %collective-permute-start.4 = (bf16[4,224,128]{2,1,0:T(8,128)(2,1)S(1)}, bf16[4,224,128]{2,1,0:T(8,128)(2,1)S(1)}, u32[]{:S(2)}, u32[]{:S(2)}) collective-permute-start(bf16[4,224,128]{2,1,0:T(8,128)(2,1)S(1)} %get-tuple-element.66), channel_id=1, source_target_pairs={{0,1},{1,0},{2,18},{3,19},{4,5},{5,4},{6,22},{7,23},{8,9},{9,8},{1... | collective-permute-start | bytes 688136 | tf_op jit(solution)/shard_map/ppermute | solution.py:436
  19.4 6.4 %collective-permute-start.5 = (bf16[4,224,128]{2,1,0:T(8,128)(2,1)S(1)}, bf16[4,224,128]{2,1,0:T(8,128)(2,1)S(1)}, u32[]{:S(2)}, u32[]{:S(2)}) collective-permute-start(bf16[4,224,128]{2,1,0:T(8,128)(2,1)S(1)} %get-tuple-element.67), channel_id=1, source_target_pairs={{0,4},{1,5},{2,10},{3,11},{4,0},{5,1},{6,14},{7,15},{8,12},{9,13},... | collective-permute-start | bytes 688136 | tf_op jit(solution)/shard_map/ppermute | solution.py:436
  23.8 7.7 %collective-permute-start.6 = (bf16[784,128]{1,0:T(8,128)(2,1)S(1)}, bf16[784,128]{1,0:T(8,128)(2,1)S(1)}, u32[]{:S(2)}, u32[]{:S(2)}) collective-permute-start(bf16[784,128]{1,0:T(8,128)(2,1)S(1)} %get-tuple-element.70), channel_id=1, source_target_pairs={{0,1},{1,0},{2,3},{3,2},{4,5},{5,4},{6,7},{7,6},{8,9},{9,8},{10,11... | collective-permute-start | bytes 602120 | tf_op jit(solution)/shard_map/ppermute | solution.py:578
  26.0 6.7 %collective-permute-start.7 = (bf16[224,128]{1,0:T(8,128)(2,1)S(1)}, bf16[224,128]{1,0:T(8,128)(2,1)S(1)}, u32[]{:S(2)}, u32[]{:S(2)}) collective-permute-start(bf16[224,128]{1,0:T(8,128)(2,1)S(1)} %get-tuple-element.77), channel_id=1, source_target_pairs={{0,24},{1,25},{2,7},{3,6},{4,28},{5,29},{6,3},{7,2},{8,16},{9,17},... | collective-permute-start | bytes 172040 | tf_op jit(solution)/shard_map/ppermute | solution.py:436
  29.9 5.1 %collective-permute-start.8 = (bf16[224,128]{1,0:T(8,128)(2,1)S(1)}, bf16[224,128]{1,0:T(8,128)(2,1)S(1)}, u32[]{:S(2)}, u32[]{:S(2)}) collective-permute-start(bf16[224,128]{1,0:T(8,128)(2,1)S(1)} %get-tuple-element.78), channel_id=1, source_target_pairs={{0,16},{1,17},{2,3},{3,2},{4,20},{5,21},{6,7},{7,6},{8,24},{9,25},... | collective-permute-start | bytes 172040 | tf_op jit(solution)/shard_map/ppermute | solution.py:436
  29.9 5.1 %collective-permute-start.9 = (bf16[224,128]{1,0:T(8,128)(2,1)S(1)}, bf16[224,128]{1,0:T(8,128)(2,1)S(1)}, u32[]{:S(2)}, u32[]{:S(2)}) collective-permute-start(bf16[224,128]{1,0:T(8,128)(2,1)S(1)} %get-tuple-element.79), channel_id=1, source_target_pairs={{0,8},{1,9},{2,6},{3,7},{4,12},{5,13},{6,2},{7,3},{8,0},{9,1},{10,... | collective-permute-start | bytes 172040 | tf_op jit(solution)/shard_map/ppermute | solution.py:436

commit v8 on v6

--- a/solution.py
+++ b/solution.py
@@ -37,10 +37,10 @@
     per_group = width // GROUPS
     row = lax.broadcasted_iota(jnp.int32, (width, width), 0) // per_group
     col = lax.broadcasted_iota(jnp.int32, (width, width), 1) // per_group
-    same = (row == col).astype(f32)
-    return lax.dot_general(
-        rows, same, (((1,), (0,)), ((), ())), precision=lax.Precision.HIGHEST, preferred_element_type=f32
-    )
+    same = (row == col).astype(bf16)
+    stacked = jnp.concatenate([piece.astype(f32) for piece in in_pieces(rows)], axis=0).astype(bf16)
+    totals = jnp.dot(stacked, same, preferred_element_type=f32)
+    return totals[0:8] + (totals[8:16] + totals[16:24])
 
 
 def two_rows(first, second):

time: 35.9 us -> 35.9 us (level)
  transfers between devices with their start and end apart: 10 -> 10, of which waited for: 4 -> 3; matrix products, arithmetic and copies ran while one was open for 0% -> 0% of each run, Pallas kernels for 34% -> 34%
where the time goes in v8:
time: 35.9 us; the launch traced here: 35.6 us
  starting transfers between devices  15.1 us (42%)
  Pallas kernels  14.9 us (42%)
  waiting for transfers between devices  3.79 us (11%)
  local copies, waits for them, and re-layouts  1.02 us (3%)
  between operations  0.79 us (2%)
    ppermute x7, starting transfers between devices, swap(): return lax.ppermute(value, ('dp', 'ctx'), pairs)  8.3 us
    pallas_call x1, Pallas kernels, body(): call(forward_kernel, jax.ShapeDtypeStruct((frames, height, breadth, out_w...  3.18 us
    ppermute x1, starting transfers between devices, others_total(): lax.ppermute(value, 'ctx', [(source, (source + step) % count) for source...  2.97 us
    pallas_call x1, Pallas kernels, body(): call(functools.partial(weight_own_kernel, members), [jax.ShapeDtypeStruct...  2.67 us
    ppermute x7, waiting for transfers between devices, swap(): return lax.ppermute(value, ('dp', 'ctx'), pairs)  2.58 us
    ppermute x1, starting transfers between devices, from_behind(): lax.ppermute(value, axis, [(source, source + steps) for source in range(i...  2.04 us
    pallas_call x1, Pallas kernels, body(): call(back_second_kernel, jax.ShapeDtypeStruct((frames, height * breadth,...  2.01 us
    pallas_call x1, Pallas kernels, body(): call(back_first_kernel, [jax.ShapeDtypeStruct((2, height * breadth, in_wi...  2 us
  transfers between devices with their start and end apart: 10, of which 3 were waited for; matrix products, arithmetic and copies ran while one was open for 0% of the time, Pallas kernels for 34%

profile of v8, /device:TPU:0, one launch (start us, length us, event | category | flops | bytes accessed | tf_op | source)
XLA Modules:
  0.0 35.6 jit_solution(2030863941371433832)
XLA Ops:
  0.6 0.0 copy-start.1
  0.6 1.0 %copy-done.1 = bf16[1,4,4,96,128]{4,3,2,1,0:T(8,128)(2,1)S(1)} copy-done((bf16[1,4,4,96,128]{4,3,2,1,0:T(8,128)(2,1)S(1)}, bf16[1,4,4,96,128]{4,3,2,1,0:T(8,128)(2,1)}, u32[]{:S(2)}) %copy-start.1) | copy-done | bytes 393240
  1.6 0.0 copy-start
  1.6 0.0 copy-start.3
  1.6 0.3 shard_map.93
  1.9 3.0 %collective-permute-start.1 = (f32[8,128]{1,0:T(8,128)S(1)}, f32[8,128]{1,0:T(8,128)S(1)}, u32[]{:S(2)}, u32[]{:S(2)}) collective-permute-start(f32[8,128]{1,0:T(8,128)S(1)} %get-tuple-element.42.stats_ref), channel_id=1, source_target_pairs={{0,1},{1,0},{2,3},{3,2},{4,5},{5,4},{6,7},{7,6},{8,9},{9,8},{10,11... | collective-permute-start | bytes 12296 | tf_op jit(solution)/shard_map/ppermute | solution.py:415
  4.9 2.0 %collective-permute-start = (bf16[2,4,96,128]{3,2,1,0:T(8,128)(2,1)S(1)}, bf16[2,4,96,128]{3,2,1,0:T(8,128)(2,1)S(1)}, u32[]{:S(2)}, u32[]{:S(2)}) collective-permute-start(bf16[2,4,96,128]{3,2,1,0:T(8,128)(2,1)S(1)} %get-tuple-element.41), channel_id=1, source_target_pairs={{0,1},{2,3},{4,5},{6,7},{8,9},{10,11},{12,13},{14,15},{16,17},{18,... | collective-permute-start | bytes 589832 | tf_op jit(solution)/shard_map/ppermute | solution.py:408
  6.9 0.0 copy-done
  6.9 0.0 copy-done.3
  6.9 0.0 copy-start.2
  6.9 0.0 copy-start.5
  6.9 0.0 copy-start.6
  7.0 2.0 %shard_map.94 = (f32[2,384,128]{2,1,0:T(8,128)S(1)}, bf16[2,384,128]{2,1,0:T(8,128)(2,1)S(1)}, bf16[256,1536]{1,0:T(8,128)(2,1)S(1)}) custom-call(bf16[4,4,96,256]{3,2,1,0:T(8,128)(2,1)S(1)} %bitcast.15, bf16[3456,256]{1,0:T(8,128)(2,1)S(1)} %copy-done), custom_call_target="tpu_custom_call" | custom-call | flops 2717908992 | bytes 1769472 | tf_op jit(solution)/shard_map/pallas_call | solution.py:494
  9.0 0.0 collective-permute-done.1.other_ref
  9.0 0.0 copy-done.2
  9.0 0.0 copy-done.5
  9.0 0.0 copy-done.6
  9.0 2.7 %shard_map.95 = (bf16[3,4,6,96,128]{4,3,2,1,0:T(8,128)(2,1)S(1)}, f32[256,2304]{1,0:T(8,128)S(1)}, f32[1280,256]{1,0:T(8,128)S(1)}) custom-call(bf16[4,4,96,128]{3,2,1,0:T(8,128)(2,1)S(1)} %bitcast.9, f32[8,128]{1,0:T(8,128)S(1)} %get-tuple-element.42.stats_ref, f32[8,128]{1,0:T(8,128)S(1)} %collective-permute-done.1.other_ref, f32[1,128]{1,0:T(1,128)S(1)} %bitcast.19, ...), custom_call_target="tpu_custom_call" | custom-call | flops 2717908992 | bytes 786432 | tf_op jit(solution)/shard_map/pallas_call | solution.py:506
  11.7 0.0 collective-permute-done.halo_ref
  11.7 1.5 %shard_map.96 = (bf16[3,2,6,96,128]{4,3,2,1,0:T(8,128)(2,1)S(1)}, f32[2,16,224,128]{3,2,1,0:T(8,128)S(1)}, bf16[2,8,224,128]{3,2,1,0:T(8,128)(2,1)S(1)}) custom-call(bf16[2,4,96,128]{3,2,1,0:T(8,128)(2,1)S(1)} %collective-permute-done.halo_ref, bf16[4,4,96,128]{3,2,1,0:T(8,128)(2,1)S(1)} %bitcast.10, f32[8,128]{1,0:T(8,128)S(1)} %get-tuple-element.42.stats_ref, ...), custom_call_target="tpu_custom_call" | custom-call | flops 905969664 | bytes 786432 | tf_op jit(solution)/shard_map/pallas_call | solution.py:529
  13.2 0.1 collective-permute-start.2
  13.3 2.0 %shard_map.97.part_ref = f32[4,384,128]{2,1,0:T(8,128)S(1)} custom-call(bf16[4,4,96,256]{3,2,1,0:T(8,128)(2,1)S(1)} %bitcast.16, bf16[3456,256]{1,0:T(8,128)(2,1)S(1)} %copy-done, f32[2,384,128]{2,1,0:T(8,128)S(1)} %get-tuple-element.49.first_ref), custom_call_target="tpu_custom_call" | custom-call | flops 679477248 | tf_op jit(solution)/shard_map/pallas_call | solution.py:536
  15.3 0.4 %collective-permute-done.2 = bf16[2,8,224,128]{3,2,1,0:T(8,128)(2,1)S(1)} collective-permute-done((bf16[2,8,224,128]{3,2,1,0:T(8,128)(2,1)S(1)}, bf16[2,8,224,128]{3,2,1,0:T(8,128)(2,1)S(1)}, u32[]{:S(2)}, u32[]{:S(2)}) %collective-permute-start.2) | collective-permute-done | bytes 917536 | tf_op jit(solution)/shard_map/ppermute | solution.py:428
  15.8 0.0 copy-start.4
  15.8 0.2 shard_map.98
  16.0 3.0 %collective-permute-start.3 = (bf16[4,224,128]{2,1,0:T(8,128)(2,1)S(1)}, bf16[4,224,128]{2,1,0:T(8,128)(2,1)S(1)}, u32[]{:S(2)}, u32[]{:S(2)}) collective-permute-start(bf16[4,224,128]{2,1,0:T(8,128)(2,1)S(1)} %get-tuple-element.61), channel_id=1, source_target_pairs={{0,5},{1,4},{2,26},{3,27},{4,1},{5,0},{6,30},{7,31},{8,13},{9,12},... | collective-permute-start | bytes 688136 | tf_op jit(solution)/shard_map/ppermute | solution.py:428
  19.0 0.5 %collective-permute-start.4 = (bf16[4,224,128]{2,1,0:T(8,128)(2,1)S(1)}, bf16[4,224,128]{2,1,0:T(8,128)(2,1)S(1)}, u32[]{:S(2)}, u32[]{:S(2)}) collective-permute-start(bf16[4,224,128]{2,1,0:T(8,128)(2,1)S(1)} %get-tuple-element.62), channel_id=1, source_target_pairs={{0,1},{1,0},{2,18},{3,19},{4,5},{5,4},{6,22},{7,23},{8,9},{9,8},{1... | collective-permute-start | bytes 688136 | tf_op jit(solution)/shard_map/ppermute | solution.py:428
  19.5 0.2 collective-permute-start.5
  19.7 0.0 copy-done.4
  19.7 3.2 %shard_map.99.forward_ref = bf16[4,4,96,256]{3,2,1,0:T(8,128)(2,1)S(1)} custom-call(bf16[3,2,6,96,128]{4,3,2,1,0:T(8,128)(2,1)S(1)} %get-tuple-element.52.padded_lead, bf16[3,4,6,96,128]{4,3,2,1,0:T(8,128)(2,1)S(1)} %get-tuple-element.57.padded, bf16[4,4,96,128]{3,2,1,0:T(8,128)(2,1)S(1)} %bitcast.11, bf16[3456,256]{1,0:T(8,128)(2,1)S(1)} %copy-done, ...), custom_call_target="tpu_custom_call" | custom-call | flops 679477248 | tf_op jit(solution)/shard_map/pallas_call | solution.py:547
  22.8 1.1 %shard_map.100 = (f32[4,384,128]{2,1,0:T(8,128)S(1)}, f32[2,384,128]{2,1,0:T(8,128)S(1)}, f32[8,128]{1,0:T(8,128)S(1)}, bf16[784,128]{1,0:T(8,128)(2,1)S(1)}, bf16[4,4,96,256]{3,2,1,0:T(8,128)(2,1)}) custom-call(f32[4,384,128]{2,1,0:T(8,128)S(1)} %shard_map.97.part_ref, bf16[2,384,128]{2,1,0:T(8,128)(2,1)S(1)} %get-tuple-element.51.leading_ref, ...), custom_call_target="tpu_custom_call" | custom-call | tf_op jit(solution)/shard_map/pallas_call | solution.py:553
  24.0 1.8 %collective-permute-start.6 = (bf16[784,128]{1,0:T(8,128)(2,1)S(1)}, bf16[784,128]{1,0:T(8,128)(2,1)S(1)}, u32[]{:S(2)}, u32[]{:S(2)}) collective-permute-start(bf16[784,128]{1,0:T(8,128)(2,1)S(1)} %get-tuple-element.66), channel_id=1, source_target_pairs={{0,1},{1,0},{2,3},{3,2},{4,5},{5,4},{6,7},{7,6},{8,9},{9,8},{10,11... | collective-permute-start | bytes 602120 | tf_op jit(solution)/shard_map/ppermute | solution.py:567
  25.7 0.0 collective-permute-done.3.a_ref
  25.8 0.0 collective-permute-done.4.b_ref
  25.8 0.0 collective-permute-done.5.c_ref
  25.8 0.1 shard_map.101
  25.9 3.9 %collective-permute-start.7 = (bf16[224,128]{1,0:T(8,128)(2,1)S(1)}, bf16[224,128]{1,0:T(8,128)(2,1)S(1)}, u32[]{:S(2)}, u32[]{:S(2)}) collective-permute-start(bf16[224,128]{1,0:T(8,128)(2,1)S(1)} %get-tuple-element.73), channel_id=1, source_target_pairs={{0,24},{1,25},{2,7},{3,6},{4,28},{5,29},{6,3},{7,2},{8,16},{9,17},... | collective-permute-start | bytes 172040 | tf_op jit(solution)/shard_map/ppermute | solution.py:428
  29.8 0.0 collective-permute-start.8
  29.8 0.6 %collective-permute-start.9 = (bf16[224,128]{1,0:T(8,128)(2,1)S(1)}, bf16[224,128]{1,0:T(8,128)(2,1)S(1)}, u32[]{:S(2)}, u32[]{:S(2)}) collective-permute-start(bf16[224,128]{1,0:T(8,128)(2,1)S(1)} %get-tuple-element.75), channel_id=1, source_target_pairs={{0,8},{1,9},{2,6},{3,7},{4,12},{5,13},{6,2},{7,3},{8,0},{9,1},{10,... | collective-permute-start | bytes 172040 | tf_op jit(solution)/shard_map/ppermute | solution.py:428
  30.5 1.2 %collective-permute-done.6.after_ref = bf16[784,128]{1,0:T(8,128)(2,1)S(1)} collective-permute-done((bf16[784,128]{1,0:T(8,128)(2,1)S(1)}, bf16[784,128]{1,0:T(8,128)(2,1)S(1)}, u32[]{:S(2)}, u32[]{:S(2)}) %collective-permute-start.6) | collective-permute-done | bytes 200736 | tf_op jit(solution)/shard_map/ppermute | solution.py:567
  31.7 1.1 %shard_map.102 = bf16[4,4,96,128]{3,2,1,0:T(8,128)(2,1)} custom-call(f32[4,384,128]{2,1,0:T(8,128)S(1)} %get-tuple-element.59.grad_ref, f32[2,384,128]{2,1,0:T(8,128)S(1)} %get-tuple-element.60.slope_ref, f32[8,128]{1,0:T(8,128)S(1)} %get-tuple-element.65.sums_ref, bf16[784,128]{1,0:T(8,128)(2,1)S(1)} %collective-permute-done.6.after_ref, ...), custom_call_target="tpu_custom_call" | custom-call | flops 135895456 | bytes 1572864 | tf_op jit(solution)/shard_map/pallas_call | solution.py:584
  32.8 0.0 collective-permute-done.7.a_ref
  32.8 2.1 %collective-permute-done.8.b_ref = bf16[224,128]{1,0:T(8,128)(2,1)S(1)} collective-permute-done((bf16[224,128]{1,0:T(8,128)(2,1)S(1)}, bf16[224,128]{1,0:T(8,128)(2,1)S(1)}, u32[]{:S(2)}, u32[]{:S(2)}) %collective-permute-start.8) | collective-permute-done | bytes 57376 | tf_op jit(solution)/shard_map/ppermute | solution.py:428
  34.9 0.0 collective-permute-done.9.c_ref
  34.9 0.7 %shard_map.103 = (f32[216,128]{1,0:T(8,128)}, f32[8,128]{1,0:T(8,128)}) custom-call(f32[224,128]{1,0:T(8,128)S(1)} %get-tuple-element.71.own_ref, bf16[224,128]{1,0:T(8,128)(2,1)S(1)} %collective-permute-done.7.a_ref, bf16[224,128]{1,0:T(8,128)(2,1)S(1)} %collective-permute-done.8.b_ref, bf16[224,128]{1,0:T(8,128)(2,1)S(1)} %collective-permute-done.9.c_ref), custom_call_target="tpu_custom_call" | custom-call | bytes 344064 | tf_op jit(solution)/shard_map/pallas_call | solution.py:460
Async XLA Ops:
  0.6 1.0 %copy-start.1 = (bf16[1,4,4,96,128]{4,3,2,1,0:T(8,128)(2,1)S(1)}, bf16[1,4,4,96,128]{4,3,2,1,0:T(8,128)(2,1)}, u32[]{:S(2)}) copy-start(bf16[1,4,4,96,128]{4,3,2,1,0:T(8,128)(2,1)} %param.6) | copy-start | bytes 1179652
  1.6 5.3 %copy-start = (bf16[3456,256]{1,0:T(8,128)(2,1)S(1)}, bf16[3456,256]{1,0:T(8,128)(2,1)}, u32[]{:S(2)}) copy-start(bf16[3456,256]{1,0:T(8,128)(2,1)} %weight_ref.5) | copy-start | bytes 5308420
  1.6 5.3 %copy-start.3 = (bf16[1,4,4,96,256]{4,3,2,1,0:T(8,128)(2,1)S(1)}, bf16[1,4,4,96,256]{4,3,2,1,0:T(8,128)(2,1)}, u32[]{:S(2)}) copy-start(bf16[1,4,4,96,256]{4,3,2,1,0:T(8,128)(2,1)} %param.11) | copy-start | bytes 2359300
  1.9 7.1 %collective-permute-start.1 = (f32[8,128]{1,0:T(8,128)S(1)}, f32[8,128]{1,0:T(8,128)S(1)}, u32[]{:S(2)}, u32[]{:S(2)}) collective-permute-start(f32[8,128]{1,0:T(8,128)S(1)} %get-tuple-element.42.stats_ref), channel_id=1, source_target_pairs={{0,1},{1,0},{2,3},{3,2},{4,5},{5,4},{6,7},{7,6},{8,9},{9,8},{10,11... | collective-permute-start | bytes 12296 | tf_op jit(solution)/shard_map/ppermute | solution.py:415
  4.9 6.8 %collective-permute-start = (bf16[2,4,96,128]{3,2,1,0:T(8,128)(2,1)S(1)}, bf16[2,4,96,128]{3,2,1,0:T(8,128)(2,1)S(1)}, u32[]{:S(2)}, u32[]{:S(2)}) collective-permute-start(bf16[2,4,96,128]{3,2,1,0:T(8,128)(2,1)S(1)} %get-tuple-element.41), channel_id=1, source_target_pairs={{0,1},{2,3},{4,5},{6,7},{8,9},{10,11},{12,13},{14,15},{16,17},{18,... | collective-permute-start | bytes 589832 | tf_op jit(solution)/shard_map/ppermute | solution.py:408
  6.9 2.1 %copy-start.2 = (bf16[1,4,4,96,128]{4,3,2,1,0:T(8,128)(2,1)S(1)}, bf16[1,4,4,96,128]{4,3,2,1,0:T(8,128)(2,1)}, u32[]{:S(2)}) copy-start(bf16[1,4,4,96,128]{4,3,2,1,0:T(8,128)(2,1)} %param.6) | copy-start | bytes 1179652
  6.9 2.1 %copy-start.5 = (f32[128]{0:T(128)S(1)}, f32[128]{0:T(128)}, u32[]{:S(2)}) copy-start(f32[128]{0:T(128)} %param.7) | copy-start | bytes 1540
  6.9 2.1 %copy-start.6 = (f32[128]{0:T(128)S(1)}, f32[128]{0:T(128)}, u32[]{:S(2)}) copy-start(f32[128]{0:T(128)} %param.8) | copy-start | bytes 1540
  13.2 2.5 %collective-permute-start.2 = (bf16[2,8,224,128]{3,2,1,0:T(8,128)(2,1)S(1)}, bf16[2,8,224,128]{3,2,1,0:T(8,128)(2,1)S(1)}, u32[]{:S(2)}, u32[]{:S(2)}) collective-permute-start(bf16[2,8,224,128]{3,2,1,0:T(8,128)(2,1)S(1)} %get-tuple-element.46), channel_id=1, source_target_pairs={{0,2},{1,3},{2,0},{3,1},{4,6},{5,7},{6,4},{7,5},{8,10},{9,11},{10,... | collective-permute-start | bytes 2752520 | tf_op jit(solution)/shard_map/ppermute | solution.py:428
  15.8 3.9 %copy-start.4 = (bf16[128,256]{1,0:T(8,128)(2,1)S(1)}, bf16[128,256]{1,0:T(8,128)(2,1)}, u32[]{:S(2)}) copy-start(bf16[128,256]{1,0:T(8,128)(2,1)} %short_ref.3) | copy-start | bytes 196612
  16.0 9.8 %collective-permute-start.3 = (bf16[4,224,128]{2,1,0:T(8,128)(2,1)S(1)}, bf16[4,224,128]{2,1,0:T(8,128)(2,1)S(1)}, u32[]{:S(2)}, u32[]{:S(2)}) collective-permute-start(bf16[4,224,128]{2,1,0:T(8,128)(2,1)S(1)} %get-tuple-element.61), channel_id=1, source_target_pairs={{0,5},{1,4},{2,26},{3,27},{4,1},{5,0},{6,30},{7,31},{8,13},{9,12},... | collective-permute-start | bytes 688136 | tf_op jit(solution)/shard_map/ppermute | solution.py:428
  19.0 6.7 %collective-permute-start.4 = (bf16[4,224,128]{2,1,0:T(8,128)(2,1)S(1)}, bf16[4,224,128]{2,1,0:T(8,128)(2,1)S(1)}, u32[]{:S(2)}, u32[]{:S(2)}) collective-permute-start(bf16[4,224,128]{2,1,0:T(8,128)(2,1)S(1)} %get-tuple-element.62), channel_id=1, source_target_pairs={{0,1},{1,0},{2,18},{3,19},{4,5},{5,4},{6,22},{7,23},{8,9},{9,8},{1... | collective-permute-start | bytes 688136 | tf_op jit(solution)/shard_map/ppermute | solution.py:428
  19.5 6.3 %collective-permute-start.5 = (bf16[4,224,128]{2,1,0:T(8,128)(2,1)S(1)}, bf16[4,224,128]{2,1,0:T(8,128)(2,1)S(1)}, u32[]{:S(2)}, u32[]{:S(2)}) collective-permute-start(bf16[4,224,128]{2,1,0:T(8,128)(2,1)S(1)} %get-tuple-element.63), channel_id=1, source_target_pairs={{0,4},{1,5},{2,10},{3,11},{4,0},{5,1},{6,14},{7,15},{8,12},{9,13},... | collective-permute-start | bytes 688136 | tf_op jit(solution)/shard_map/ppermute | solution.py:428
  24.0 7.7 %collective-permute-start.6 = (bf16[784,128]{1,0:T(8,128)(2,1)S(1)}, bf16[784,128]{1,0:T(8,128)(2,1)S(1)}, u32[]{:S(2)}, u32[]{:S(2)}) collective-permute-start(bf16[784,128]{1,0:T(8,128)(2,1)S(1)} %get-tuple-element.66), channel_id=1, source_target_pairs={{0,1},{1,0},{2,3},{3,2},{4,5},{5,4},{6,7},{7,6},{8,9},{9,8},{10,11... | collective-permute-start | bytes 602120 | tf_op jit(solution)/shard_map/ppermute | solution.py:567
  25.9 6.9 %collective-permute-start.7 = (bf16[224,128]{1,0:T(8,128)(2,1)S(1)}, bf16[224,128]{1,0:T(8,128)(2,1)S(1)}, u32[]{:S(2)}, u32[]{:S(2)}) collective-permute-start(bf16[224,128]{1,0:T(8,128)(2,1)S(1)} %get-tuple-element.73), channel_id=1, source_target_pairs={{0,24},{1,25},{2,7},{3,6},{4,28},{5,29},{6,3},{7,2},{8,16},{9,17},... | collective-permute-start | bytes 172040 | tf_op jit(solution)/shard_map/ppermute | solution.py:428
  29.8 5.1 %collective-permute-start.8 = (bf16[224,128]{1,0:T(8,128)(2,1)S(1)}, bf16[224,128]{1,0:T(8,128)(2,1)S(1)}, u32[]{:S(2)}, u32[]{:S(2)}) collective-permute-start(bf16[224,128]{1,0:T(8,128)(2,1)S(1)} %get-tuple-element.74), channel_id=1, source_target_pairs={{0,16},{1,17},{2,3},{3,2},{4,20},{5,21},{6,7},{7,6},{8,24},{9,25},... | collective-permute-start | bytes 172040 | tf_op jit(solution)/shard_map/ppermute | solution.py:428
  29.8 5.1 %collective-permute-start.9 = (bf16[224,128]{1,0:T(8,128)(2,1)S(1)}, bf16[224,128]{1,0:T(8,128)(2,1)S(1)}, u32[]{:S(2)}, u32[]{:S(2)}) collective-permute-start(bf16[224,128]{1,0:T(8,128)(2,1)S(1)} %get-tuple-element.75), channel_id=1, source_target_pairs={{0,8},{1,9},{2,6},{3,7},{4,12},{5,13},{6,2},{7,3},{8,0},{9,1},{10,... | collective-permute-start | bytes 172040 | tf_op jit(solution)/shard_map/ppermute | solution.py:428
